TPU v7x, 32 devices: a whole 2x2x4 slice. The times are simulated.
32 devices in a mesh: fsdp: 8 (over y, x, core), seq: 4 (over z).
Axes of the slice: x: 2, y: 2, z: 4, core: 2. Of those that a mesh axis runs over, the one named last changes fastest.
Arguments:
- hidden_in: bfloat16 [8, 1024, 2048], P('fsdp', 'seq'), may hold values from -6 to 6
- norm_attn: bfloat16 [2048], P('fsdp'), may hold values from 0.5 to 1.5
- qkv_weight: bfloat16 [2048, 2560], P('fsdp'), may hold values from -0.1875 to 0.1875
- out_weight: bfloat16 [2048, 2048], P('fsdp'), may hold values from -1 to 1
- norm_ffn: bfloat16 [2048], P('fsdp'), may hold values from 0.29882812 to 3
- gate_up_weight: bfloat16 [2048, 11264], P('fsdp'), may hold values from -0.125 to 0.125
- down_weight: bfloat16 [5632, 2048], P('fsdp'), may hold values from -0.078125 to 0.078125
- cotangent: bfloat16 [8, 1024, 2048], P('fsdp', 'seq'), may hold values from -6 to 6
Outputs:
- out: bfloat16 [8, 1024, 2048], P('fsdp', 'seq')
- grad_input: bfloat16 [8, 1024, 2048], P('fsdp', 'seq')
- grad_norm_attn: float32 [2048], P('fsdp')
- grad_qkv_weight: float32 [2048, 2560], P('fsdp')
- grad_out_weight: float32 [2048, 2048], P('fsdp')
- grad_norm_ffn: float32 [2048], P('fsdp')
- grad_gate_up_weight: float32 [2048, 11264], P('fsdp')
- grad_down_weight: float32 [5632, 2048], P('fsdp')
All inputs are finite; a program needn't handle non-finite values.
Results may differ from a plain program's by a relative error of at most 0.017.
The roundings to bfloat16 on the way count: a program that leaves them out, or rounds other values in their place, can miss the bound.
Values may be sent and summed in bfloat16 or wider, within the bound.
No kernel may reach another device: no remote copies, remote signals or barrier semaphores. Data moves between devices by JAX's collectives and lax.ppermute only.
A program may use at most 512 MiB of HBM per device.

v0:
```python
import jax
import jax.numpy as jnp
from jax import lax
from jax.sharding import PartitionSpec as P

HEADS = 32
KVH = 4
HD = 64
FF = 5632


epsilon = 1e-05
masked_value = -1e30
contract_last = (((1,), (1,)), ((), ()))
contract_first = (((0,), (0,)), ((), ()))


def angle_tables(positions):
    half_dim = HD // 2
    inverse = 10000.0 ** (-jnp.arange(half_dim, dtype=jnp.float32) * 2.0 / HD)
    angles = positions.astype(jnp.float32)[:, None] * inverse[None, :]
    return (jnp.cos(angles), jnp.sin(angles))


def rotate(values, cosine, sine):
    half_dim = values.shape[-1] // 2
    first, second = (values[..., :half_dim], values[..., half_dim:])
    cos_wide, sin_wide = (cosine[:, None, :], sine[:, None, :])
    return jnp.concatenate(
        [first * cos_wide - second * sin_wide, second * cos_wide + first * sin_wide], -1
    )


def unrotate(incoming, cosine, sine):
    half_dim = incoming.shape[-1] // 2
    first, second = (incoming[..., :half_dim], incoming[..., half_dim:])
    cos_wide, sin_wide = (cosine[:, None, :], sine[:, None, :])
    return jnp.concatenate(
        [first * cos_wide + second * sin_wide, second * cos_wide - first * sin_wide], -1
    )


def norm_factor(values):
    return lax.rsqrt(jnp.mean(values * values, axis=-1, keepdims=True) + epsilon)


def norm_back(incoming, inputs, factor, gain):
    weighted = incoming * gain
    gain_grad = jnp.sum(incoming * (inputs * factor), axis=0)
    input_grad = weighted * factor - inputs * (factor * factor * factor) * jnp.mean(
        weighted * inputs, axis=-1, keepdims=True
    )
    return (gain_grad, input_grad)


def on_device(
    hidden_in, norm_attn, qkv_weight, out_weight, norm_ffn, gate_up_weight, down_weight, cotangent
):
    groups = lax.axis_size("seq")
    width = hidden_in.shape[2]
    tok_rows = hidden_in.shape[0] * hidden_in.shape[1]
    length = hidden_in.shape[1] * groups
    q_width = HEADS * HD
    kv_width = KVH * HD
    per_dev = HEADS // groups
    copies = groups // KVH
    key_scale = HD ** (-0.5)
    block_rows = min(512, length)
    block_count = length // block_rows
    gain_one, full_qkv, full_out = (
        lax.all_gather(norm_attn, "fsdp", axis=0, tiled=True),
        lax.all_gather(qkv_weight, "fsdp", axis=0, tiled=True),
        lax.all_gather(out_weight, "fsdp", axis=0, tiled=True),
    )
    inputs = hidden_in.reshape(tok_rows, width).astype(jnp.float32)
    factor_one = norm_factor(inputs)
    normed_one = (inputs * factor_one * gain_one.astype(jnp.float32)).astype(jnp.bfloat16)
    joined = jnp.dot(normed_one, full_qkv, preferred_element_type=jnp.float32)
    positions = lax.axis_index("seq") * tok_rows + jnp.arange(tok_rows, dtype=jnp.int32)
    cosine, sine = angle_tables(positions)
    queries = rotate(joined[:, :q_width].reshape(tok_rows, HEADS, HD), cosine, sine).astype(
        jnp.bfloat16
    )
    keys = rotate(
        joined[:, q_width : q_width + kv_width].reshape(tok_rows, KVH, HD), cosine, sine
    ).astype(jnp.bfloat16)
    values = joined[:, q_width + kv_width :].reshape(tok_rows, KVH, HD).astype(jnp.bfloat16)
    kv_slots = jnp.repeat(jnp.concatenate([keys, values], -1), copies, axis=1)
    head_q, head_kv = (
        lax.all_to_all(
            queries.reshape(tok_rows, groups, per_dev * HD),
            "seq",
            split_axis=1,
            concat_axis=0,
            tiled=True,
        ),
        lax.all_to_all(kv_slots, "seq", split_axis=1, concat_axis=0, tiled=True),
    )
    head_keys = head_kv[:, 0, :HD]
    head_values = head_kv[:, 0, HD:]
    query_blocks = head_q.reshape(block_count, block_rows, per_dev, HD)
    starts = jnp.arange(block_count, dtype=jnp.int32) * block_rows
    key_place = jnp.arange(length, dtype=jnp.int32)

    def scores_of(query_block, start_row):
        scores = (
            jnp.einsum("qhd,kd->hqk", query_block, head_keys, preferred_element_type=jnp.float32)
            * key_scale
        )
        query_place = start_row + jnp.arange(block_rows, dtype=jnp.int32)
        allowed = key_place[None, :] <= query_place[:, None]
        return jnp.where(allowed[None], scores, masked_value)

    def forward_block(block_item):
        query_block, start_row = block_item
        scores = scores_of(query_block, start_row)
        row_max = jnp.max(scores, axis=-1, keepdims=True)
        log_total = row_max + jnp.log(jnp.sum(jnp.exp(scores - row_max), axis=-1, keepdims=True))
        attn_probs = jnp.exp(scores - log_total).astype(jnp.bfloat16)
        block_out = jnp.einsum(
            "hqk,kd->qhd", attn_probs, head_values, preferred_element_type=jnp.float32
        )
        return (block_out.astype(jnp.bfloat16), log_total)

    head_out, log_totals = lax.map(forward_block, (query_blocks, starts))
    attended = lax.all_to_all(
        head_out.reshape(length, 1, per_dev * HD), "seq", split_axis=0, concat_axis=1, tiled=True
    ).reshape(tok_rows, q_width)
    middle = inputs + jnp.dot(attended, full_out, preferred_element_type=jnp.float32)
    gain_two, full_gate_up, full_down = (
        lax.all_gather(norm_ffn, "fsdp", axis=0, tiled=True),
        lax.all_gather(gate_up_weight, "fsdp", axis=0, tiled=True),
        lax.all_gather(down_weight, "fsdp", axis=0, tiled=True),
    )
    factor_two = norm_factor(middle)
    normed_two = (middle * factor_two * gain_two.astype(jnp.float32)).astype(jnp.bfloat16)
    gate_up = jnp.dot(normed_two, full_gate_up, preferred_element_type=jnp.float32)
    gate_pre = gate_up[:, :FF]
    up_proj = gate_up[:, FF:]
    gate_act = jax.nn.silu(gate_pre)
    mixed = (gate_act * up_proj).astype(jnp.bfloat16)
    result = middle + jnp.dot(mixed, full_down, preferred_element_type=jnp.float32)
    out = result.astype(jnp.bfloat16).reshape(hidden_in.shape)
    gain_two, full_gate_up, full_down = (
        lax.all_gather(norm_ffn, "fsdp", axis=0, tiled=True),
        lax.all_gather(gate_up_weight, "fsdp", axis=0, tiled=True),
        lax.all_gather(down_weight, "fsdp", axis=0, tiled=True),
    )
    grad_result = cotangent.reshape(tok_rows, width)
    grad_mixed = lax.dot_general(
        grad_result, full_down, contract_last, preferred_element_type=jnp.float32
    )
    piece = mixed
    grad_down = lax.psum_scatter(
        lax.dot_general(piece, grad_result, contract_first, preferred_element_type=jnp.float32),
        "fsdp",
        scatter_dimension=0,
        tiled=True,
    )
    sigmoid_gate = jax.nn.sigmoid(gate_pre)
    grad_gate = grad_mixed * up_proj * (sigmoid_gate * (1.0 + gate_pre * (1.0 - sigmoid_gate)))
    grad_gate_up = jnp.concatenate([grad_gate, grad_mixed * gate_act], -1).astype(jnp.bfloat16)
    piece = normed_two
    grad_gate_up_w = lax.psum_scatter(
        lax.dot_general(piece, grad_gate_up, contract_first, preferred_element_type=jnp.float32),
        "fsdp",
        scatter_dimension=0,
        tiled=True,
    )
    grad_normed_two = lax.dot_general(
        grad_gate_up, full_gate_up, contract_last, preferred_element_type=jnp.float32
    )
    grad_gain_two, grad_norm_two = norm_back(
        grad_normed_two, middle, factor_two, gain_two.astype(jnp.float32)
    )
    grad_middle = grad_result.astype(jnp.float32) + grad_norm_two
    gain_one, full_qkv, full_out = (
        lax.all_gather(norm_attn, "fsdp", axis=0, tiled=True),
        lax.all_gather(qkv_weight, "fsdp", axis=0, tiled=True),
        lax.all_gather(out_weight, "fsdp", axis=0, tiled=True),
    )
    grad_branch = grad_middle.astype(jnp.bfloat16)
    piece = attended
    grad_out_w = lax.psum_scatter(
        lax.dot_general(piece, grad_branch, contract_first, preferred_element_type=jnp.float32),
        "fsdp",
        scatter_dimension=0,
        tiled=True,
    )
    grad_attended = lax.dot_general(
        grad_branch, full_out, contract_last, preferred_element_type=jnp.float32
    ).astype(jnp.bfloat16)
    head_grad = lax.all_to_all(
        grad_attended.reshape(tok_rows, groups, per_dev * HD),
        "seq",
        split_axis=1,
        concat_axis=0,
        tiled=True,
    )
    grad_blocks = head_grad.reshape(block_count, block_rows, per_dev, HD)

    def backward_block(kv_totals, block_item):
        query_block, grad_block, log_total, start_row = block_item
        scores = scores_of(query_block, start_row)
        attn_weights = jnp.exp(scores - log_total)
        attn_probs = attn_weights.astype(jnp.bfloat16)
        grad_probs = jnp.einsum(
            "qhd,kd->hqk", grad_block, head_values, preferred_element_type=jnp.float32
        )
        row_delta = jnp.sum(grad_probs * attn_weights, axis=-1, keepdims=True)
        grad_scores = (attn_weights * (grad_probs - row_delta)).astype(jnp.bfloat16)
        grad_query = (
            jnp.einsum("hqk,kd->qhd", grad_scores, head_keys, preferred_element_type=jnp.float32)
            * key_scale
        )
        key_total = (
            kv_totals[0]
            + jnp.einsum(
                "hqk,qhd->kd", grad_scores, query_block, preferred_element_type=jnp.float32
            )
            * key_scale
        )
        value_total = kv_totals[1] + jnp.einsum(
            "hqk,qhd->kd", attn_probs, grad_block, preferred_element_type=jnp.float32
        )
        return ((key_total, value_total), grad_query.astype(jnp.bfloat16))

    empty_kv = jnp.zeros((length, HD), jnp.float32)
    (key_total, value_total), grad_queries = lax.scan(
        backward_block, (empty_kv, empty_kv), (query_blocks, grad_blocks, log_totals, starts)
    )
    kv_parts = jnp.concatenate([key_total, value_total], -1).astype(jnp.bfloat16)[:, None, :]
    back_q, back_kv = (
        lax.all_to_all(
            grad_queries.reshape(length, 1, per_dev * HD),
            "seq",
            split_axis=0,
            concat_axis=1,
            tiled=True,
        ),
        lax.all_to_all(kv_parts, "seq", split_axis=0, concat_axis=1, tiled=True),
    )
    kv_summed = back_kv.astype(jnp.float32).reshape(tok_rows, KVH, copies, 2 * HD).sum(axis=2)
    grad_q_tok = unrotate(back_q.astype(jnp.float32).reshape(tok_rows, HEADS, HD), cosine, sine)
    grad_k_tok = unrotate(kv_summed[..., :HD], cosine, sine)
    grad_v_tok = kv_summed[..., HD:]
    grad_joined = jnp.concatenate(
        [
            grad_q_tok.reshape(tok_rows, q_width),
            grad_k_tok.reshape(tok_rows, kv_width),
            grad_v_tok.reshape(tok_rows, kv_width),
        ],
        -1,
    ).astype(jnp.bfloat16)
    piece = normed_one
    grad_qkv_w = lax.psum_scatter(
        lax.dot_general(piece, grad_joined, contract_first, preferred_element_type=jnp.float32),
        "fsdp",
        scatter_dimension=0,
        tiled=True,
    )
    grad_normed_one = lax.dot_general(
        grad_joined, full_qkv, contract_last, preferred_element_type=jnp.float32
    )
    grad_gain_one, grad_norm_one = norm_back(
        grad_normed_one, inputs, factor_one, gain_one.astype(jnp.float32)
    )
    grad_input = (grad_middle + grad_norm_one).astype(jnp.bfloat16).reshape(hidden_in.shape)
    gain_stack = jnp.stack([grad_gain_one, grad_gain_two])
    gain_shards = lax.psum_scatter(gain_stack, "fsdp", scatter_dimension=1, tiled=True)
    gain_sums, qkv_sums, out_sums, gate_up_sums, down_sums = lax.psum(
        (gain_shards, grad_qkv_w, grad_out_w, grad_gate_up_w, grad_down), "seq"
    )
    return (
        out,
        grad_input,
        gain_sums[0],
        qkv_sums,
        out_sums,
        gain_sums[1],
        gate_up_sums,
        down_sums,
    )


def solution(mesh):
    placed = (
        P("fsdp", "seq", None),
        P("fsdp"),
        P("fsdp", None),
        P("fsdp", None),
        P("fsdp"),
        P("fsdp", None),
        P("fsdp", None),
        P("fsdp", "seq", None),
    )
    return jax.shard_map(
        on_device,
        mesh=mesh,
        in_specs=placed,
        out_specs=(
            P("fsdp", "seq", None),
            P("fsdp", "seq", None),
            P("fsdp"),
            P("fsdp", None),
            P("fsdp", None),
            P("fsdp"),
            P("fsdp", None),
            P("fsdp", None),
        ),
        check_vma=False,
    )
```

profile of v0, /device:TPU:0, one launch (start us, length us, event | category | flops | bytes accessed | tf_op | source)
XLA Modules:
  0.0 2433.7 jit_solution(3262695738502591070)
XLA Ops:
  21.5 54.4 %all-gather.7.cloned.1.call-done = bf16[2048,2560]{1,0:T(8,128)(2,1)} async-done(((bf16[256,2560]{1,0:T(8,128)(2,1)}), bf16[2048,2560]{1,0:T(8,128)(2,1)}) %all-gather.7.cloned.1.call-update) | async-done | bytes 10485776 | tf_op jit(solution)/shard_map/all_gather | solution.py:72
  109.3 23.6 all-to-all-done
  134.7 28.1 %while.28 = (s32[]{:T(128)}, bf16[2,512,8,64]{1,3,2,0:T(8,128)(2,1)S(1)}, f32[2,8,512,1]{2,1,3,0:T(8,128)}, s32[2]{0:T(128)S(1)}, bf16[2,512,8,64]{1,3,2,0:T(8,1...) while((s32[]{:T(128)}, ...), condition=%wide.region_4.5_spmd.clone, body=%wide.region_1.4_spmd.clone.sunk | while | flops 1120662016 | bytes 53874808 | solution.py:125
  196.6 16.2 all-to-all-done.2
  229.8 119.0 %all-gather.11.cloned.1.call-done = bf16[2048,11264]{1,0:T(8,128)(2,1)} async-done(((bf16[256,11264]{1,0:T(8,128)(2,1)}), bf16[2048,11264]{1,0:T(8,128)(2,1)}) %all-gather.11.cloned.1.call-update) | async-done | bytes 46137360 | tf_op jit(solution)/shard_map/all_gather | solution.py:132
  348.8 26.2 %fusion.93 = f32[256,11264]{1,0:T(8,128)} fusion(bf16[2048,11264]{1,0:T(8,128)(2,1)} %all-gather.11.cloned.1.call-done, f32[256,2048]{1,0:T(8,128)} %get-tuple-element.304, f32[2048]{0:T(1024)S(1)} %bitcast.258, f32[256]{0:T(256)S(1)} %get-tuple-element.302), kind=kOutput, calls=%fused_computation.144 | convolution fusion | flops 11812732928 | bytes 59778048 | tf_op jit(solution)/shard_map/dot_general | solution.py:137
  375.0 92.1 %all-gather.13.cloned.1.call-done = bf16[5632,2048]{1,0:T(8,128)(2,1)} async-done(((bf16[704,2048]{1,0:T(8,128)(2,1)}), bf16[5632,2048]{1,0:T(8,128)(2,1)}) %all-gather.13.cloned.1.call-update) | async-done | bytes 23068688 | tf_op jit(solution)/shard_map/all_gather | solution.py:133
  467.1 18.4 multiply_convert_fusion.1
  485.5 22.1 multiply_reduce_fusion
  535.2 26.2 %all-to-all-done.3 = bf16[256,4,512]{0,2,1:T(8,128)(2,1)S(1)} async-done(((bf16[256,4,512]{0,2,1:T(8,128)(2,1)}), bf16[256,4,512]{0,2,1:T(8,128)(2,1)S(1)}, u32[]{:S(2)}, u32[]{:S(2)}) %all-to-all-start.3) | async-done | bytes 1048608 | tf_op jit(solution)/shard_map/all_to_all | solution.py:193
  565.1 88.7 %while.29 = (s32[]{:T(128)}, f32[1024,64]{0,1:T(8,128)}, f32[1024,64]{0,1:T(8,128)}, bf16[2,512,8,64]{1,3,2,0:T(8,128)(2,1)}, s32[2]{0:T(128)S(1)}, /*index=5*/b...) while((s32[]{:T(128)}, f32[1024,64]{0,1:T(8,128)}, ...), condition=%wide.region_9.10_spmd.clone, body=%wide.region_7.9_spmd.clone.sunk | while | flops 2723475968 | bytes 172052976 | solution.py:229
  572.3 10.3 fusion.140
  616.8 10.3 fusion.140
  685.6 23.5 all-to-all-done.4
  725.9 28.9 %fusion.77 = f32[5632,2048]{1,0:T(8,128)} fusion(bf16[256,5632]{1,0:T(8,128)(2,1)} %get-tuple-element.284, bf16[1,256,2048]{2,1,0:T(8,128)(2,1)S(1)} %copy-done.19), kind=kOutput, calls=%fused_computation.101 | convolution fusion | flops 5905580032 | bytes 50069504 | tf_op jit(solution)/shard_map/dot_general | solution.py:155
  756.4 36.9 %fusion.62 = f32[2048,11264]{1,0:T(8,128)} fusion(bf16[256,5632]{1,0:T(8,128)(2,1)} %get-tuple-element.283, bf16[256,5632]{1,0:T(8,128)(2,1)} %get-tuple-element.282, f32[256,2048]{1,0:T(8,128)S(1)} %copy-done.6, f32[2048]{0:T(1024)S(1)} %bitcast.261, f32[256]{0:T(256)S(1)} %copy-done.32), kind=kOutput, calls=%fused_computation.75 | convolution fusion | flops 11824267264 | bytes 100148224 | tf_op jit(solution)/shard_map/dot_general | solution.py:165
  804.7 54.2 %reduce-scatter.10.cloned.1.call-done = f32[256,2560]{1,0:T(8,128)} async-done(((f32[2048,2560]{1,0:T(8,128)}), f32[256,2560]{1,0:T(8,128)}) %reduce-scatter.10.cloned.1.call-update) | async-done | bytes 2621456 | tf_op jit(solution)/shard_map/reduce_scatter | solution.py:256
  858.9 268.0 %reduce-scatter.14.cloned.1.call-done = f32[704,2048]{1,0:T(8,128)} async-done(((f32[5632,2048]{1,0:T(8,128)}), f32[704,2048]{1,0:T(8,128)}) %reduce-scatter.14.cloned.1.call-update) | async-done | bytes 5767184 | tf_op jit(solution)/shard_map/reduce_scatter | solution.py:154
  1126.9 505.2 %reduce-scatter.18.cloned.1.call-done = f32[256,11264]{1,0:T(8,128)} async-done(((f32[2048,11264]{1,0:T(8,128)}), f32[256,11264]{1,0:T(8,128)}) %reduce-scatter.18.cloned.1.call-update) | async-done | bytes 11534352
  1632.2 12.5 fusion.67
  1646.4 25.7 %reduce-scatter.16.cloned.1.call-done = f32[256,2]{1,0:T(8,128)} async-done(((f32[2048,2]{1,0:T(8,128)}), f32[256,2]{1,0:T(8,128)}) %reduce-scatter.16.cloned.1.call-update) | async-done | bytes 2064
  1673.0 11.9 psum.35
  1685.5 723.1 %all-reduce.4.cloned.1.call-done = (f32[256,2560]{1,0:T(8,128)}, f32[256,2048]{1,0:T(8,128)}, f32[256,11264]{1,0:T(8,128)}, f32[704,2048]{1,0:T(8,128)}) async-done(((f32[256,2560]{1,0:T(8,128)}, f32[256,2048]{1,0:T(8,128)}, f32[256,11264]{1,0:T(8,128)}, f32[704,2048]{1,0:T(8,128)}), (f32[256,2560]{1,0:T(8,128)}, f32[256,2048]{1,0:T(8,128)}, f32[256,11264]{1,0:T(8,128)}, ...) | async-done | bytes 22020112 | tf_op jit(solution)/shard_map/psum | solution.py:271
  2413.5 10.7 copy.141
  (264 shorter events, 299.1 us)
Async XLA Ops:
  7.2 68.7 %all-gather.7.cloned.1.call-start = ((), (), s32[]{:S(2)}) async-start(), calls=%async_computation.11 | async-start | bytes 11796480 | tf_op jit(solution)/shard_map/all_gather | solution.py:72
  7.9 212.2 %all-gather.9.cloned.1.call-start = ((), (), s32[]{:S(2)}) async-start(), calls=%async_computation.12 | async-start | bytes 9437184 | tf_op jit(solution)/shard_map/all_gather | solution.py:73
  8.7 340.2 %all-gather.11.cloned.1.call-start = ((), (), s32[]{:S(2)}) async-start(), calls=%async_computation.13 | async-start | bytes 51904512 | tf_op jit(solution)/shard_map/all_gather | solution.py:132
  9.4 457.7 %all-gather.13.cloned.1.call-start = ((), (), s32[]{:S(2)}) async-start(), calls=%async_computation.14 | async-start | bytes 25952256 | tf_op jit(solution)/shard_map/all_gather | solution.py:133
  20.4 61.2 %copy-start.33 = (f32[8,1,256]{2,1,0:T(1,128)}, f32[8,1,256]{2,1,0:T(1,128)S(1)}, u32[]{:S(2)}) copy-start(f32[8,1,256]{2,1,0:T(1,128)S(1)} %convert_element_type.138) | copy-start | bytes 24580
  21.3 60.2 %copy-start.36 = (f32[256]{0:T(256)}, f32[256]{0:T(256)S(1)}, u32[]{:S(2)}) copy-start(f32[256]{0:T(256)S(1)} %get-tuple-element.300) | copy-start | bytes 3076
  21.5 74.3 %copy-start.25 = (f32[256,32]{0,1:T(8,128)}, f32[256,32]{0,1:T(8,128)S(1)}, u32[]{:S(2)}) copy-start(f32[256,32]{0,1:T(8,128)S(1)} %get-tuple-element.297) | copy-start | bytes 98308
  21.5 74.3 %copy-start.27 = (f32[256,32]{0,1:T(8,128)}, f32[256,32]{0,1:T(8,128)S(1)}, u32[]{:S(2)}) copy-start(f32[256,32]{0,1:T(8,128)S(1)} %get-tuple-element.298) | copy-start | bytes 98308
  91.2 13.9 all-to-all-start.1
  105.1 27.7 %all-to-all-start = ((bf16[256,4,512]{0,2,1:T(8,128)(2,1)}), bf16[256,4,512]{0,2,1:T(8,128)(2,1)S(1)}, u32[]{:S(2)}, u32[]{:S(2)}) async-start(bf16[256,4,512]{0,2,1:T(8,128)(2,1)} %bitcast.4), calls=%async_computation | async-start | bytes 2097152 | tf_op jit(solution)/shard_map/all_to_all | solution.py:90
  184.1 28.7 %all-to-all-start.2 = ((bf16[4,2,65536]{2,1,0:T(2,128)(2,1)}), bf16[4,2,65536]{2,1,0:T(2,128)(2,1)S(1)}, u32[]{:S(2)}, u32[]{:S(2)}) async-start(bf16[4,2,65536]{2,1,0:T(2,128)(2,1)} %reshape.337), calls=%async_computation.2 | async-start | bytes 2097152 | tf_op jit(solution)/shard_map/all_to_all | solution.py:126
  187.6 617.1 %reduce-scatter.12.cloned.1.call-start = ((), (), s32[]{:S(2)}) async-start(), calls=%async_computation.16 | async-start | bytes 18874368 | tf_op jit(solution)/shard_map/reduce_scatter | solution.py:184
  196.6 311.0 %copy-start.23 = (f32[8,1,256]{2,1,0:T(1,128)}, f32[8,1,256]{2,1,0:T(1,128)S(1)}, u32[]{:S(2)}) copy-start(f32[8,1,256]{2,1,0:T(1,128)S(1)} %convert_element_type.139) | copy-start | bytes 24580
  229.8 277.8 %copy-start.31 = (f32[256]{0:T(256)}, f32[256]{0:T(256)S(1)}, u32[]{:S(2)}) copy-start(f32[256]{0:T(256)S(1)} %get-tuple-element.302) | copy-start | bytes 3076
  375.0 110.5 %copy-start.5 = (f32[256,2048]{1,0:T(8,128)S(1)}, f32[256,2048]{1,0:T(8,128)}, u32[]{:S(2)}) copy-start(f32[256,2048]{1,0:T(8,128)} %get-tuple-element.304) | copy-start | bytes 6291460
  530.5 30.9 %all-to-all-start.3 = ((bf16[256,4,512]{0,2,1:T(8,128)(2,1)}), bf16[256,4,512]{0,2,1:T(8,128)(2,1)S(1)}, u32[]{:S(2)}, u32[]{:S(2)}) async-start(bf16[256,4,512]{0,2,1:T(8,128)(2,1)} %bitcast.19), calls=%async_computation.3 | async-start | bytes 2097152 | tf_op jit(solution)/shard_map/all_to_all | solution.py:193
  592.1 13.9 slice-start
  656.8 22.2 all-to-all-start.5
  679.0 30.2 %all-to-all-start.4 = ((bf16[4,2,65536]{2,1,0:T(2,128)(2,1)}), bf16[4,2,65536]{2,1,0:T(2,128)(2,1)S(1)}, u32[]{:S(2)}, u32[]{:S(2)}) async-start(bf16[4,2,65536]{2,1,0:T(2,128)(2,1)} %reshape.341), calls=%async_computation.4 | async-start | bytes 2097152 | tf_op jit(solution)/shard_map/all_to_all | solution.py:234
  684.2 174.7 %reduce-scatter.10.cloned.1.call-start = ((), (), s32[]{:S(2)}) async-start(), calls=%async_computation.15 | async-start | bytes 23592960 | tf_op jit(solution)/shard_map/reduce_scatter | solution.py:256
  724.7 402.2 %reduce-scatter.14.cloned.1.call-start = ((), (), s32[]{:S(2)}) async-start(), calls=%async_computation.17 | async-start | bytes 51904512 | tf_op jit(solution)/shard_map/reduce_scatter | solution.py:154
  754.8 877.4 %reduce-scatter.18.cloned.1.call-start = ((), (), s32[]{:S(2)}) async-start(), calls=%async_computation.19 | async-start | bytes 103809024
  793.3 878.8 %reduce-scatter.16.cloned.1.call-start = ((), (), s32[]{:S(2)}) async-start(), calls=%async_computation.18 | async-start | bytes 1179648
  804.6 1603.9 %all-reduce.4.cloned.1.call-start = ((), (), s32[]{:S(2)}) async-start(), calls=%async_computation.20 | async-start | bytes 44040192 | tf_op jit(solution)/shard_map/psum | solution.py:271
  (49 other events, 256.4 us)
Sparse Core Ops, SparseCore 0:
  9.9 65.9 all-gather.6
  77.8 54.3 all-gather.8
  134.1 214.6 all-gather.10
  350.6 116.4 all-gather.12
  519.8 115.9 reduce-scatter.11
  724.8 134.0 reduce-scatter.9
  862.6 264.3 reduce-scatter.13
  1131.0 501.1 reduce-scatter.17
  1635.9 36.0 reduce-scatter.15
  1674.8 733.6 all-reduce.3
where the time goes:
time: 2440 us; the launch traced here: 2430 us
  waiting for transfers between devices  1940 us (80%)
  matrix products  269 us (11%)
  local copies, waits for them, and re-layouts  87.3 us (4%)
  other arithmetic  63.6 us (3%)
  blocking collectives  31.1 us (1%)
  starting transfers between devices  26 us (1%)
    psum x1, waiting for transfers between devices, on_device(): lax.psum((gain_shards, grad_qkv_w, grad_out_w, grad_gate_up_w, grad_down)...  723 us
    unnamed x12, waiting for transfers between devices  534 us
    reduce_scatter x1, waiting for transfers between devices, on_device(): lax.psum_scatter(lax.dot_general(piece, grad_result, contract_first, pref...  268 us
    all_gather x1, waiting for transfers between devices, on_device(): lax.all_gather(gate_up_weight, 'fsdp', axis=0, tiled=True)  119 us
    all_gather x1, waiting for transfers between devices, on_device(): lax.all_gather(down_weight, 'fsdp', axis=0, tiled=True)  92.1 us
    all_gather x1, waiting for transfers between devices, on_device(): lax.all_gather(qkv_weight, 'fsdp', axis=0, tiled=True)  54.4 us
    reduce_scatter x1, waiting for transfers between devices, on_device(): lax.psum_scatter(lax.dot_general(piece, grad_joined, contract_first, pref...  54.2 us
  transfers between devices with their start and end apart: 16, of which 13 were waited for; matrix products, arithmetic and copies ran while one was open for 14% of the time, Pallas kernels for 0%

commit v1 on v0

v1 whole, which is shorter than its diff:
```python
import functools

import jax
import jax.numpy as jnp
from jax import lax
from jax.experimental import pallas as pl
from jax.experimental.pallas import tpu as pltpu
from jax.sharding import PartitionSpec as P

HEADS = 32
KVH = 4
HD = 64
FF = 5632

epsilon = 1e-05
masked_value = -1e30
log2e = 1.4426950408889634
contract_last = (((1,), (1,)), ((), ()))
contract_first = (((0,), (0,)), ((), ()))
bf16 = jnp.bfloat16
f32 = jnp.float32


def send(x, k):
    n = lax.axis_size("fsdp")
    return lax.ppermute(x, "fsdp", [(i, i ^ k) for i in range(n)])


def chip_bits():
    n = lax.axis_size("fsdp")
    return [1 << i for i in range(1, n.bit_length() - 1)]


def piece_order():
    n = lax.axis_size("fsdp")
    return list(range(0, n, 2)) + list(range(1, n, 2))


def gather_pieces(x):
    bits = chip_bits()
    pieces = {0: x}
    rest = bits
    if len(bits) >= 2:
        a, b = bits[:2]
        rest = bits[2:]
        half = x.shape[0] // 2
        pieces[a], pieces[b] = send(x, a), send(x, b)
        lower = send(pieces[b][:half], a)
        upper = send(pieces[a][half:], b)
        pieces[a | b] = jnp.concatenate([lower, upper], 0)
    for b in rest:
        for k in list(pieces):
            pieces[k | b] = send(pieces[k], b)
    for k in list(pieces):
        pieces[k | 1] = send(pieces[k], 1)
    return pieces


def gather_rows(x):
    pieces = gather_pieces(x)
    return jnp.concatenate([pieces[k] for k in piece_order()], 0)


def scatter_sum(whole):
    n = lax.axis_size("fsdp")
    rows = whole.shape[0] // n
    bits = chip_bits()
    even, odd = whole[: n // 2 * rows], whole[n // 2 * rows :]
    got = send(odd, 1)
    total = {
        k: even[i * rows : (i + 1) * rows].astype(f32) + got[i * rows : (i + 1) * rows].astype(f32)
        for i, k in enumerate(piece_order()[: n // 2])
    }
    for b in reversed(bits[2:] if len(bits) >= 2 else bits):
        for k in [k for k in total if not k & b]:
            total[k] = total[k] + send(total.pop(k | b).astype(bf16), b).astype(f32)
    if len(bits) < 2:
        return total[0]
    a, b = bits[:2]
    half = rows // 2
    far = total[a | b].astype(bf16)
    lower, upper = send(far[:half], a), send(far[half:], b)
    to_b = jnp.concatenate([total[b][:half] + lower.astype(f32), total[b][half:]], 0).astype(bf16)
    to_a = jnp.concatenate([total[a][:half], total[a][half:] + upper.astype(f32)], 0).astype(bf16)
    return total[0] + send(to_a, a).astype(f32) + send(to_b, b).astype(f32)


def line_sum(x):
    n = lax.axis_size("seq")
    if n == 1:
        return x
    if n % 2:
        return lax.psum(x.astype(f32), "seq").astype(bf16)
    me = lax.axis_index("seq")
    mid = n // 2
    total = x

    def add(one, two):
        return (one.astype(f32) + two.astype(f32)).astype(bf16)

    for i in range(mid - 1):
        total = add(total, lax.ppermute(total, "seq", [(i, i + 1), (n - 1 - i, n - 2 - i)]))
    total = add(total, lax.ppermute(total, "seq", [(mid - 1, mid), (mid, mid - 1)]))
    for i in range(mid - 1):
        got = lax.ppermute(total, "seq", [(mid - 1 - i, mid - 2 - i), (mid + i, mid + 1 + i)])
        taken = (me == mid - 2 - i) | (me == mid + 1 + i)
        total = jnp.where(taken, got, total)
    return total


def turn_kernel(sign, x_ref, cos_ref, sin_ref, o_ref):
    x = x_ref[...].astype(f32)
    width = x.shape[1]
    lane = lax.broadcasted_iota(jnp.int32, x.shape, 1)
    first = (lane % HD) < HD // 2
    other = jnp.where(
        first, -pltpu.roll(x, width - HD // 2, 1), pltpu.roll(x, HD // 2, 1)
    )
    o_ref[...] = (x * cos_ref[...] + sign * other * sin_ref[...]).astype(o_ref.dtype)


def turn(x, cos_wide, sin_wide, sign):
    rows, width = x.shape
    block = cos_wide.shape[1]
    return pl.pallas_call(
        functools.partial(turn_kernel, float(sign)),
        out_shape=jax.ShapeDtypeStruct((rows, width), bf16),
        grid=(width // block,),
        in_specs=[
            pl.BlockSpec((rows, block), lambda i: (0, i)),
            pl.BlockSpec((rows, block), lambda i: (0, 0)),
            pl.BlockSpec((rows, block), lambda i: (0, 0)),
        ],
        out_specs=pl.BlockSpec((rows, block), lambda i: (0, i)),
    )(x, cos_wide, sin_wide)


def mask_bias(start, length, rows):
    key_place = lax.broadcasted_iota(jnp.int32, (length, rows), 0)
    query_place = start + lax.broadcasted_iota(jnp.int32, (length, rows), 1)
    return jnp.where(key_place <= query_place, 0.0, masked_value).astype(f32)


def attend_kernel(per_kv, start_ref, q_ref, k_ref, v_ref, o_ref, lse_ref):
    length, rows = k_ref.shape[1], q_ref.shape[0]
    scale2 = HD**-0.5 * log2e
    bias = mask_bias(start_ref[0], length, rows)
    keys = k_ref[0]
    values_t = v_ref[0].astype(f32).T.astype(bf16)
    q_t = q_ref[...].astype(f32).T.astype(bf16)
    outs = []
    for h in range(per_kv):
        scores = (
            jnp.dot(keys, q_t[h * HD : (h + 1) * HD], preferred_element_type=f32) + bias
        )
        top = jnp.max(scores, axis=0, keepdims=True)
        weights = jnp.exp2((scores - top) * scale2)
        total = jnp.sum(weights, axis=0, keepdims=True)
        probs = (weights * (1.0 / total)).astype(bf16)
        outs.append(jnp.dot(values_t, probs, preferred_element_type=f32))
        lse_ref[0, h : h + 1, :] = top * scale2 + jnp.log2(total)
    o_ref[...] = jnp.concatenate(outs, 0).T.astype(bf16)


def attend(start, queries, keys, values):
    rows, width = queries.shape
    length = keys.shape[1]
    per_kv = HEADS // KVH
    block = per_kv * HD
    return pl.pallas_call(
        functools.partial(attend_kernel, per_kv),
        out_shape=(
            jax.ShapeDtypeStruct((rows, width), bf16),
            jax.ShapeDtypeStruct((KVH, per_kv, rows), f32),
        ),
        grid=(KVH,),
        in_specs=[
            pl.BlockSpec(memory_space=pltpu.SMEM),
            pl.BlockSpec((rows, block), lambda i: (0, i)),
            pl.BlockSpec((1, length, HD), lambda i: (i, 0, 0)),
            pl.BlockSpec((1, length, HD), lambda i: (i, 0, 0)),
        ],
        out_specs=(
            pl.BlockSpec((rows, block), lambda i: (0, i)),
            pl.BlockSpec((1, per_kv, rows), lambda i: (i, 0, 0)),
        ),
        compiler_params=pltpu.CompilerParams(vmem_limit_bytes=40 << 20),
        cost_estimate=pl.CostEstimate(
            flops=4 * HEADS * rows * length * HD * 4,
            bytes_accessed=4 * rows * width,
            transcendentals=HEADS * rows * length,
        ),
    )(start, queries, keys, values)


def attend_back_kernel(
    per_kv, start_ref, q_ref, k_ref, v_ref, g_ref, lse_ref, dq_ref, dk_ref, dv_ref
):
    length, rows = k_ref.shape[1], q_ref.shape[0]
    scale = HD**-0.5
    scale2 = scale * log2e
    bias = mask_bias(start_ref[0], length, rows)
    keys, values = k_ref[0], v_ref[0]
    keys_t = keys.astype(f32).T.astype(bf16)
    q_t = q_ref[...].astype(f32).T.astype(bf16)
    g_t = g_ref[...].astype(f32).T.astype(bf16)
    dk = jnp.zeros((length, HD), f32)
    dv = jnp.zeros((length, HD), f32)
    outs = []
    for h in range(per_kv):
        q_h, g_h = q_t[h * HD : (h + 1) * HD], g_t[h * HD : (h + 1) * HD]
        scores = jnp.dot(keys, q_h, preferred_element_type=f32) + bias
        weights = jnp.exp2(scores * scale2 - lse_ref[0, h : h + 1, :])
        grad_p = jnp.dot(values, g_h, preferred_element_type=f32)
        delta = jnp.sum(grad_p * weights, axis=0, keepdims=True)
        grad_s = (weights * (grad_p - delta)).astype(bf16)
        outs.append(jnp.dot(keys_t, grad_s, preferred_element_type=f32))
        dk += lax.dot_general(grad_s, q_h, contract_last, preferred_element_type=f32)
        dv += lax.dot_general(
            weights.astype(bf16), g_h, contract_last, preferred_element_type=f32
        )
    dq_ref[...] = (jnp.concatenate(outs, 0) * scale).T.astype(bf16)
    dk_ref[0] = (dk * scale).astype(bf16)
    dv_ref[0] = dv.astype(bf16)


def attend_back(start, queries, keys, values, grads, lse):
    rows, width = queries.shape
    length = keys.shape[1]
    per_kv = HEADS // KVH
    block = per_kv * HD
    wide = pl.BlockSpec((rows, block), lambda i: (0, i))
    narrow = pl.BlockSpec((1, length, HD), lambda i: (i, 0, 0))
    return pl.pallas_call(
        functools.partial(attend_back_kernel, per_kv),
        out_shape=(
            jax.ShapeDtypeStruct((rows, width), bf16),
            jax.ShapeDtypeStruct((KVH, length, HD), bf16),
            jax.ShapeDtypeStruct((KVH, length, HD), bf16),
        ),
        grid=(KVH,),
        in_specs=[
            pl.BlockSpec(memory_space=pltpu.SMEM),
            wide,
            narrow,
            narrow,
            wide,
            pl.BlockSpec((1, per_kv, rows), lambda i: (i, 0, 0)),
        ],
        out_specs=(wide, narrow, narrow),
        compiler_params=pltpu.CompilerParams(vmem_limit_bytes=48 << 20),
        cost_estimate=pl.CostEstimate(
            flops=10 * HEADS * rows * length * HD * 4,
            bytes_accessed=6 * rows * width,
            transcendentals=HEADS * rows * length,
        ),
    )(start, queries, keys, values, grads, lse)


def angle_tables(positions, heads):
    half_dim = HD // 2
    inverse = 10000.0 ** (-jnp.arange(half_dim, dtype=f32) * 2.0 / HD)
    angles = positions.astype(f32)[:, None] * inverse[None, :]
    return tuple(jnp.tile(t, (1, 2 * heads)) for t in (jnp.cos(angles), jnp.sin(angles)))


def norm_factor(values):
    return lax.rsqrt(jnp.mean(values * values, axis=-1, keepdims=True) + epsilon)


def norm_back(incoming, inputs, factor, gain):
    weighted = incoming * gain
    gain_grad = jnp.sum(incoming * (inputs * factor), axis=0)
    input_grad = weighted * factor - inputs * (factor * factor * factor) * jnp.mean(
        weighted * inputs, axis=-1, keepdims=True
    )
    return (gain_grad, input_grad)


def dot(one, two):
    return jnp.dot(one, two, preferred_element_type=f32)


def dot_last(one, two):
    return lax.dot_general(one, two, contract_last, preferred_element_type=f32)


def dot_first(one, two):
    return lax.dot_general(one, two, contract_first, preferred_element_type=f32)


def on_device(
    hidden_in, norm_attn, qkv_weight, out_weight, norm_ffn, gate_up_weight, down_weight, cotangent
):
    n = lax.axis_size("fsdp")
    me = lax.axis_index("fsdp")
    order = piece_order()
    width = hidden_in.shape[2]
    rows = hidden_in.shape[0] * hidden_in.shape[1]
    q_width = HEADS * HD
    kv_width = KVH * HD
    share = FF // n
    block = width // n
    seq_at = lax.axis_index("seq")

    def to_order(x):
        size = x.shape[1] // n
        return jnp.concatenate(
            [lax.dynamic_slice_in_dim(x, (me ^ k) * size, size, 1) for k in order], 1
        )

    def from_order(x):
        size = x.shape[1] // n
        where = {k: i for i, k in enumerate(order)}
        place = jnp.zeros((n,), jnp.int32)
        place = jnp.array([where[k] for k in range(n)], jnp.int32)[me ^ jnp.arange(n)]
        return jnp.concatenate(
            [lax.dynamic_slice_in_dim(x, place[j] * size, size, 1) for j in range(n)], 1
        )

    gains = lax.all_gather(jnp.stack([norm_attn, norm_ffn]), "fsdp", axis=1, tiled=True)
    gain_one, gain_two = gains[0].astype(f32), gains[1].astype(f32)
    full_qkv = gather_rows(qkv_weight)

    inputs = hidden_in.reshape(rows, width).astype(f32)
    factor_one = norm_factor(inputs)
    normed_one = to_order((inputs * factor_one * gain_one).astype(bf16))
    joined = dot(normed_one, full_qkv)
    positions = seq_at * rows + jnp.arange(rows, dtype=jnp.int32)
    cos_wide, sin_wide = angle_tables(positions, KVH)
    turned = turn(joined[:, : q_width + kv_width], cos_wide, sin_wide, 1)
    queries = turned[:, :q_width]
    keys_values = jnp.concatenate(
        [turned[:, q_width:], joined[:, q_width + kv_width :].astype(bf16)], 1
    )
    all_kv = lax.all_gather(keys_values, "seq", axis=0, tiled=True)
    length = all_kv.shape[0]
    all_kv = all_kv.reshape(length, 2, KVH, HD).transpose(1, 2, 0, 3)
    all_keys, all_values = all_kv[0], all_kv[1]
    start = (seq_at * rows).astype(jnp.int32).reshape(1)
    attended, lse = attend(start, queries, all_keys, all_values)

    full_out = gather_rows(out_weight)
    attended_x = to_order(attended)
    middle = inputs + dot(attended_x, full_out)

    by_owner = gate_up_weight.reshape(block, 2, n, share).transpose(2, 0, 1, 3)
    by_owner = by_owner.reshape(n, block, 2 * share)
    mine = jnp.zeros((width, 2 * share), bf16)
    for k in range(n):
        part = lax.dynamic_index_in_dim(by_owner, me ^ k, 0, keepdims=False)
        part = send(part, k) if k else part
        mine = lax.dynamic_update_slice_in_dim(mine, part, (me ^ k) * block, 0)

    factor_two = norm_factor(middle)
    normed_two = (middle * factor_two * gain_two).astype(bf16)
    tokens = gather_rows(normed_two)
    grad_result = cotangent.reshape(rows, width)
    grads = gather_rows(grad_result)

    gate_pre = dot(tokens, mine[:, :share])
    up_proj = dot(tokens, mine[:, share:])
    sigmoid_gate = jax.nn.sigmoid(gate_pre)
    gate_act = gate_pre * sigmoid_gate
    mixed = (gate_act * up_proj).astype(bf16)
    grad_mixed = dot_last(grads, down_weight)
    grad_gate = grad_mixed * up_proj * (sigmoid_gate * (1.0 + gate_pre * (1.0 - sigmoid_gate)))
    grad_gate_up = jnp.concatenate([grad_gate, grad_mixed * gate_act], -1).astype(bf16)

    grad_normed_two = scatter_sum(dot_last(grad_gate_up, mine).astype(bf16))
    result = middle + scatter_sum(dot(mixed, down_weight).astype(bf16))
    out = result.astype(bf16).reshape(hidden_in.shape)

    pieces = 4 if share % 64 == 0 else 2
    grad_down = dot_first(mixed, grads).astype(bf16)
    size = share // pieces
    down_sums = jnp.concatenate(
        [line_sum(grad_down[i * size : (i + 1) * size]) for i in range(pieces)], 0
    ).astype(f32)

    grad_gate_up_w = dot_first(tokens, grad_gate_up).astype(bf16)
    landed = jnp.zeros((n, block, 2 * share), bf16)
    for k in range(n):
        part = lax.dynamic_slice_in_dim(grad_gate_up_w, (me ^ k) * block, block, 0)
        part = line_sum(send(part, k) if k else part)
        landed = lax.dynamic_update_index_in_dim(landed, part, me ^ k, 0)
    gate_up_sums = (
        landed.reshape(n, block, 2, share).transpose(1, 2, 0, 3).reshape(block, 2 * FF).astype(f32)
    )

    grad_gain_two, grad_norm_two = norm_back(grad_normed_two, middle, factor_two, gain_two)
    grad_middle = grad_result.astype(f32) + grad_norm_two
    grad_branch = grad_middle.astype(bf16)
    grad_attended = from_order(dot_last(grad_branch, full_out).astype(bf16))
    out_sums = line_sum(
        scatter_sum(dot_first(attended_x, grad_branch).astype(bf16)).astype(bf16)
    ).astype(f32)

    grad_queries, grad_keys, grad_values = attend_back(
        start, queries, all_keys, all_values, grad_attended, lse
    )
    kv_parts = jnp.stack([grad_keys, grad_values]).transpose(2, 0, 1, 3).reshape(length, 2 * kv_width)
    kv_sums = lax.psum_scatter(kv_parts, "seq", scatter_dimension=0, tiled=True)
    unturned = turn(
        jnp.concatenate([grad_queries, kv_sums[:, :kv_width]], 1), cos_wide, sin_wide, -1
    )
    grad_joined = jnp.concatenate([unturned, kv_sums[:, kv_width:]], 1)
    qkv_sums = line_sum(
        scatter_sum(dot_first(normed_one, grad_joined).astype(bf16)).astype(bf16)
    ).astype(f32)
    grad_normed_one = from_order(dot_last(grad_joined, full_qkv))
    grad_gain_one, grad_norm_one = norm_back(grad_normed_one, inputs, factor_one, gain_one)
    grad_input = (grad_middle + grad_norm_one).astype(bf16).reshape(hidden_in.shape)

    gain_stack = jnp.stack([grad_gain_one, grad_gain_two])
    gain_sums = lax.psum(
        lax.psum_scatter(gain_stack, "fsdp", scatter_dimension=1, tiled=True), "seq"
    )
    return (
        out,
        grad_input,
        gain_sums[0],
        qkv_sums,
        out_sums,
        gain_sums[1],
        gate_up_sums,
        down_sums,
    )


def solution(mesh):
    placed = (
        P("fsdp", "seq", None),
        P("fsdp"),
        P("fsdp", None),
        P("fsdp", None),
        P("fsdp"),
        P("fsdp", None),
        P("fsdp", None),
        P("fsdp", "seq", None),
    )
    return jax.shard_map(
        on_device,
        mesh=mesh,
        in_specs=placed,
        out_specs=(
            P("fsdp", "seq", None),
            P("fsdp", "seq", None),
            P("fsdp"),
            P("fsdp", None),
            P("fsdp", None),
            P("fsdp"),
            P("fsdp", None),
            P("fsdp", None),
        ),
        check_vma=False,
    )
```

time: 2440 us -> 1240 us (0.51)
  waiting for transfers between devices: 1940 us -> 589 us
  matrix products: 269 us -> 107 us
  starting transfers between devices: 26 us -> 124 us
  Pallas kernels: 0 us -> 72.4 us
  local copies, waits for them, and re-layouts: 87.3 us -> 143 us
  other arithmetic: 63.6 us -> 103 us
  blocking collectives: 31.1 us -> 65 us
    psum x1 -> x0, waiting for transfers between devices: 723 us -> none  [on_device(): lax.psum((gain_shards, grad_qkv_w, grad_out_w, grad_gate_up_w, grad_down)...]
    ppermute x0 -> x108, waiting for transfers between devices: none -> 552 us  [the longest x66 220 us: send(): return lax.ppermute(x, 'fsdp', [(i, i ^ k) for i in range(n)])]
    unnamed x12 -> x4, waiting for transfers between devices: 534 us -> 26 us
    reduce_scatter x3 -> x1, waiting for transfers between devices: 322 us -> 0.01 us  [on_device(): kv_sums = lax.psum_scatter(kv_parts, 'seq', scatter_dimension=0, tiled=True)]
    all_gather x4 -> x1, waiting for transfers between devices: 265 us -> 11.7 us  [on_device(): all_kv = lax.all_gather(keys_values, 'seq', axis=0, tiled=True)]
    dot_general x26 -> x13, matrix products: 269 us -> 107 us  [the longest x4 38.4 us: dot_last(): return lax.dot_general(one, two, contract_last, preferred_element_type=f32)]
    ppermute x0 -> x108, starting transfers between devices: none -> 124 us  [the longest x66 50.8 us: send(): return lax.ppermute(x, 'fsdp', [(i, i ^ k) for i in range(n)])]
    all_to_all x6 -> x0, waiting for transfers between devices: 97.4 us -> none  [the longest x1 26.2 us: on_device(): lax.all_to_all(grad_attended.reshape(tok_rows, groups, per_dev * HD), 'se...]
  transfers between devices with their start and end apart: 16 -> 111, of which waited for: 13 -> 41; matrix products, arithmetic and copies ran while one was open for 14% -> 22% of each run, Pallas kernels for 0% -> 6%
where the time goes in v1:
time: 1240 us; the launch traced here: 1230 us
  waiting for transfers between devices  589 us (48%)
  local copies, waits for them, and re-layouts  143 us (12%)
  starting transfers between devices  124 us (10%)
  matrix products  107 us (9%)
  other arithmetic  103 us (8%)
  Pallas kernels  72.4 us (6%)
  blocking collectives  65 us (5%)
  between operations  21.5 us (2%)
    ppermute x66, waiting for transfers between devices, send(): return lax.ppermute(x, 'fsdp', [(i, i ^ k) for i in range(n)])  220 us
    ppermute x14, waiting for transfers between devices, line_sum(): lax.ppermute(total, 'seq', [(mid - 1 - i, mid - 2 - i), (mid + i, mid + 1...  188 us
    ppermute x14, waiting for transfers between devices, line_sum(): lax.ppermute(total, 'seq', [(i, i + 1), (n - 1 - i, n - 2 - i)])  143 us
    unnamed x209, local copies, waits for them, and re-layouts  66.2 us
    ppermute x66, starting transfers between devices, send(): return lax.ppermute(x, 'fsdp', [(i, i ^ k) for i in range(n)])  50.8 us
    ppermute x14, starting transfers between devices, line_sum(): lax.ppermute(total, 'seq', [(i, i + 1), (n - 1 - i, n - 2 - i)])  41.8 us
    all_gather x1, blocking collectives, on_device(): lax.all_gather(jnp.stack([norm_attn, norm_ffn]), 'fsdp', axis=1, tiled=True)  41.3 us
    dot_general x4, matrix products, dot_last(): return lax.dot_general(one, two, contract_last, preferred_element_type=f32)  38.4 us
  transfers between devices with their start and end apart: 111, of which 41 were waited for; matrix products, arithmetic and copies ran while one was open for 22% of the time, Pallas kernels for 6%

profile of v1, /device:TPU:0, one launch (start us, length us, event | category | flops | bytes accessed | tf_op | source)
XLA Modules:
  0.0 1226.3 jit_solution(3293967309115310192)
XLA Ops:
  40.7 41.3 %all_gather.6 = bf16[2,2048]{1,0:T(2,128)(2,1)S(1)} all-gather(bf16[2,256]{1,0:T(2,128)(2,1)S(1)} %pad_maximum_fusion.21), channel_id=1, replica_groups=mesh['fsdp'=8,'seq'=4] {'fsdp'}, dimensions={1}, use_global_device_ids=true | all-gather | bytes 9216 | tf_op jit(solution)/shard_map/all_gather | solution.py:321
  113.4 56.7 %collective-permute-done.29 = bf16[256,1408]{0,1:T(8,128)(2,1)S(1)} collective-permute-done((bf16[256,1408]{0,1:T(8,128)(2,1)S(1)}, bf16[256,1408]{0,1:T(8,128)(2,1)S(1)}, u32[]{:S(2)}, u32[]{:S(2)}) %collective-permute-start.29) | collective-permute-done | bytes 720928 | tf_op jit(solution)/shard_map/ppermute | solution.py:26
  262.9 11.7 all-gather.2.cloned.1.call-done
  281.4 26.7 %shard_map.162 = (bf16[256,2048]{1,0:T(8,128)(2,1)S(1)}, f32[4,8,256]{2,1,0:T(8,128)S(1)}) custom-call(s32[1]{0:T(128)} %bitcast.1.start_ref, bf16[256,2048]{1,0:T(8,128)(2,1)S(1)} %copy-done.2, bf16[4,1024,64]{2,1,0:T(8,128)(2,1)S(1)} %get-tuple-element.81.k_ref, bf16[4,1024,64]{2,1,0:T(8,128)(2,1)S(1)} %get-tuple-element.80.v_ref), custom_call_target="tpu_custom_call" | custom-call | flops 8589934592 | bytes 2097152 | tf_op jit(solution)/shard_map/pallas_call | solution.py:170
  367.5 15.4 %multiply_convert_fusion.1 = (bf16[2048,704]{0,1:T(8,128)(2,1)}, bf16[2048,704]{0,1:T(8,128)(2,1)}, bf16[2048,704]{0,1:T(8,128)(2,1)}) fusion(f32[2048,704]{0,1:T(8,128)S(1)} %fusion.42, f32[2048,704]{0,1:T(8,128)} %fusion.1, bf16[2048,2048]{1,0:T(8,128)(2,1)} %copy-done.53, bf16[2048,1408]{0,1:T(8,128)(2,1)S(1)} %bitcast.114), kind=kOutput, calls=%fused_computation.9 | convolution fusion | flops 5927206912 | bytes 31457280 | tf_op jit(solution)/shard_map/dot_general | solution.py:281
  392.7 14.7 %convolution_convert_fusion.1 = bf16[2048,1408]{0,1:T(8,128)(2,1)S(1)} fusion(bf16[2048,2048]{1,0:T(8,128)(2,1)} %copy-done.53, bf16[2048,704]{0,1:T(8,128)(2,1)S(1)} %copy-done.65, bf16[2048,704]{0,1:T(8,128)(2,1)S(1)} %copy-done.64), kind=kOutput, calls=%fused_computation.3 | convolution fusion | flops 11825577984 | bytes 19922944 | tf_op jit(solution)/shard_map/dot_general | solution.py:289
  415.3 17.3 %convolution_convert_fusion.3 = bf16[2048,2048]{1,0:T(8,128)(2,1)S(1)} fusion(bf16[2048,1408]{0,1:T(8,128)(2,1)} %copy-done.24, bf16[2048,704]{0,1:T(8,128)(2,1)} %get-tuple-element.53, bf16[2048,704]{0,1:T(8,128)(2,1)} %get-tuple-element.52), kind=kOutput, calls=%fused_computation.5 | convolution fusion | flops 11826888704 | bytes 19922944 | tf_op jit(solution)/shard_map/dot_general | solution.py:285
  453.3 14.6 %collective-permute-done.105 = bf16[176,2048]{1,0:T(8,128)(2,1)S(1)} collective-permute-done((bf16[176,2048]{1,0:T(8,128)(2,1)}, bf16[176,2048]{1,0:T(8,128)(2,1)S(1)}, u32[]{:S(2)}, u32[]{:S(2)}) %collective-permute-start.105) | collective-permute-done | bytes 720928 | tf_op jit(solution)/shard_map/ppermute | solution.py:102
  467.9 15.4 %collective-permute-done.102 = bf16[176,2048]{1,0:T(8,128)(2,1)} collective-permute-done((bf16[176,2048]{1,0:T(8,128)(2,1)}, bf16[176,2048]{1,0:T(8,128)(2,1)}, u32[]{:S(2)}, u32[]{:S(2)}) %collective-permute-start.102) | collective-permute-done | bytes 720928 | tf_op jit(solution)/shard_map/ppermute | solution.py:102
  483.8 14.0 %collective-permute-done.99 = bf16[176,2048]{1,0:T(8,128)(2,1)} collective-permute-done((bf16[176,2048]{1,0:T(8,128)(2,1)}, bf16[176,2048]{1,0:T(8,128)(2,1)}, u32[]{:S(2)}, u32[]{:S(2)}) %collective-permute-start.99) | collective-permute-done | bytes 720928 | tf_op jit(solution)/shard_map/ppermute | solution.py:102
  597.0 12.8 %collective-permute-done.69 = bf16[256,1408]{0,1:T(8,128)(2,1)S(1)} collective-permute-done((bf16[256,1408]{0,1:T(8,128)(2,1)S(1)}, bf16[256,1408]{0,1:T(8,128)(2,1)S(1)}, u32[]{:S(2)}, u32[]{:S(2)}) %collective-permute-start.69) | collective-permute-done | bytes 720928 | tf_op jit(solution)/shard_map/ppermute | solution.py:102
  626.3 111.8 %collective-permute-done.98 = bf16[176,2048]{1,0:T(8,128)(2,1)S(1)} collective-permute-done((bf16[176,2048]{1,0:T(8,128)(2,1)S(1)}, bf16[176,2048]{1,0:T(8,128)(2,1)S(1)}, u32[]{:S(2)}, u32[]{:S(2)}) %collective-permute-start.98) | collective-permute-done | bytes 720928 | tf_op jit(solution)/shard_map/ppermute | solution.py:105
  739.8 15.0 %collective-permute-done.101 = bf16[176,2048]{1,0:T(8,128)(2,1)S(1)} collective-permute-done((bf16[176,2048]{1,0:T(8,128)(2,1)S(1)}, bf16[176,2048]{1,0:T(8,128)(2,1)S(1)}, u32[]{:S(2)}, u32[]{:S(2)}) %collective-permute-start.101) | collective-permute-done | bytes 720928 | tf_op jit(solution)/shard_map/ppermute | solution.py:105
  800.2 12.1 collective-permute-done.48
  846.0 31.9 %shard_map.163 = (bf16[256,2048]{1,0:T(8,128)(2,1)S(1)}, bf16[4,1024,64]{2,1,0:T(8,128)(2,1)S(1)}, bf16[4,1024,64]{2,1,0:T(8,128)(2,1)S(1)}) custom-call(s32[1]{0:T(128)} %bitcast.1.start_ref, bf16[256,2048]{1,0:T(8,128)(2,1)S(1)} %copy-done.3, bf16[4,1024,64]{2,1,0:T(8,128)(2,1)S(1)} %copy-done.6, bf16[4,1024,64]{2,1,0:T(8,128)(2,1)} %copy-done.4, ...), custom_call_target="tpu_custom_call" | custom-call | flops 21474836480 | bytes 3145728 | tf_op jit(solution)/shard_map/pallas_call | solution.py:234
  896.6 33.9 %collective-permute-done.71 = bf16[256,1408]{0,1:T(8,128)(2,1)S(1)} collective-permute-done((bf16[256,1408]{0,1:T(8,128)(2,1)}, bf16[256,1408]{0,1:T(8,128)(2,1)S(1)}, u32[]{:S(2)}, u32[]{:S(2)}) %collective-permute-start.71) | collective-permute-done | bytes 720928 | tf_op jit(solution)/shard_map/ppermute | solution.py:105
  967.1 13.7 %collective-permute-done.87 = bf16[256,1408]{0,1:T(8,128)(2,1)S(1)} collective-permute-done((bf16[256,1408]{0,1:T(8,128)(2,1)S(1)}, bf16[256,1408]{0,1:T(8,128)(2,1)S(1)}, u32[]{:S(2)}, u32[]{:S(2)}) %collective-permute-start.87) | collective-permute-done | bytes 720928 | tf_op jit(solution)/shard_map/ppermute | solution.py:105
  981.9 13.6 %collective-permute-done.91 = bf16[256,1408]{0,1:T(8,128)(2,1)S(1)} collective-permute-done((bf16[256,1408]{0,1:T(8,128)(2,1)S(1)}, bf16[256,1408]{0,1:T(8,128)(2,1)S(1)}, u32[]{:S(2)}, u32[]{:S(2)}) %collective-permute-start.91) | collective-permute-done | bytes 720928 | tf_op jit(solution)/shard_map/ppermute | solution.py:105
  1022.7 11.9 copy.42
  1062.9 24.6 %collective-permute-done.50 = bf16[128,2560]{1,0:T(8,128)(2,1)S(1)} collective-permute-done((bf16[128,2560]{1,0:T(8,128)(2,1)S(1)}, bf16[128,2560]{1,0:T(8,128)(2,1)S(1)}, u32[]{:S(2)}, u32[]{:S(2)}) %collective-permute-start.50) | collective-permute-done | bytes 655392 | tf_op jit(solution)/shard_map/ppermute | solution.py:26
  1098.7 15.2 %collective-permute-done.53 = bf16[256,2560]{1,0:T(8,128)(2,1)S(1)} collective-permute-done((bf16[256,2560]{1,0:T(8,128)(2,1)S(1)}, bf16[256,2560]{1,0:T(8,128)(2,1)S(1)}, u32[]{:S(2)}, u32[]{:S(2)}) %collective-permute-start.53) | collective-permute-done | bytes 1310752 | tf_op jit(solution)/shard_map/ppermute | solution.py:26
  1122.6 22.6 %collective-permute-done.54 = bf16[256,2560]{1,0:T(8,128)(2,1)S(1)} collective-permute-done((bf16[256,2560]{1,0:T(8,128)(2,1)S(1)}, bf16[256,2560]{1,0:T(8,128)(2,1)S(1)}, u32[]{:S(2)}, u32[]{:S(2)}) %collective-permute-start.54) | collective-permute-done | bytes 1310752 | tf_op jit(solution)/shard_map/ppermute | solution.py:102
  1162.3 26.0 %reduce-scatter.7.cloned.1.call-done = f32[256,2]{1,0:T(8,128)} async-done(((f32[2048,2]{1,0:T(8,128)}), f32[256,2]{1,0:T(8,128)}) %reduce-scatter.7.cloned.1.call-update) | async-done | bytes 2064
  1189.2 23.7 %psum.7 = f32[2,256]{1,0:T(2,128)S(1)} all-reduce(f32[2,256]{1,0:T(2,128)S(1)} %copy.44), channel_id=1, replica_groups=mesh['fsdp'=8,'seq'=4] {'seq'}, use_global_device_ids=true, to_apply=%region_8.9 | all-reduce | flops 512 | bytes 4096 | tf_op jit(solution)/shard_map/psum | solution.py:416
  (587 shorter events, 608.1 us)
Async XLA Ops:
  7.2 267.4 %all-gather.2.cloned.1.call-start = ((), (), s32[]{:S(2)}) async-start(), calls=%async_computation.2 | async-start | bytes 1310720 | tf_op jit(solution)/shard_map/all_gather | solution.py:336
  26.1 71.7 %collective-permute-start.30 = (bf16[256,1408]{0,1:T(8,128)(2,1)}, bf16[256,1408]{0,1:T(8,128)(2,1)}, u32[]{:S(2)}, u32[]{:S(2)}) collective-permute-start(bf16[256,1408]{0,1:T(8,128)(2,1)} %get-tuple-element.63), channel_id=1, source_target_pairs={{0,28},{4,24},{8,20},{12,16},{16,12},{20,8},{24,4},{28,0},{1,29},{... | collective-permute-start | bytes 2162696 | tf_op jit(solution)/shard_map/ppermute | solution.py:26
  29.5 69.1 %collective-permute-start.28 = (bf16[256,1408]{0,1:T(8,128)(2,1)}, bf16[256,1408]{0,1:T(8,128)(2,1)}, u32[]{:S(2)}, u32[]{:S(2)}) collective-permute-start(bf16[256,1408]{0,1:T(8,128)(2,1)} %get-tuple-element.65), channel_id=1, source_target_pairs={{0,20},{4,16},{8,28},{12,24},{16,4},{20,0},{24,12},{28,8},{1,21},{... | collective-permute-start | bytes 2162696 | tf_op jit(solution)/shard_map/ppermute | solution.py:26
  30.2 69.7 %collective-permute-start.27 = (bf16[256,1408]{0,1:T(8,128)(2,1)}, bf16[256,1408]{0,1:T(8,128)(2,1)}, u32[]{:S(2)}, u32[]{:S(2)}) collective-permute-start(bf16[256,1408]{0,1:T(8,128)(2,1)} %get-tuple-element.66), channel_id=1, source_target_pairs={{0,16},{4,20},{8,24},{12,28},{16,0},{20,4},{24,8},{28,12},{1,17},{... | collective-permute-start | bytes 2162696 | tf_op jit(solution)/shard_map/ppermute | solution.py:26
  93.3 78.3 %collective-permute-start.37 = (bf16[256,2048]{1,0:T(8,128)(2,1)S(1)}, bf16[256,2048]{1,0:T(8,128)(2,1)}, u32[]{:S(2)}, u32[]{:S(2)}) collective-permute-start(bf16[256,2048]{1,0:T(8,128)(2,1)S(1)} %bitcast.116), channel_id=1, source_target_pairs={{0,16},{4,20},{8,24},{12,28},{16,0},{20,4},{24,8},{28,12},{1,17},{... | collective-permute-start | bytes 3145736 | tf_op jit(solution)/shard_map/ppermute | solution.py:26
  97.9 83.0 %collective-permute-start.36 = (bf16[256,2048]{1,0:T(8,128)(2,1)S(1)}, bf16[256,2048]{1,0:T(8,128)(2,1)}, u32[]{:S(2)}, u32[]{:S(2)}) collective-permute-start(bf16[256,2048]{1,0:T(8,128)(2,1)S(1)} %bitcast.117), channel_id=1, source_target_pairs={{0,8},{4,12},{8,0},{12,4},{16,24},{20,28},{24,16},{28,20},{1,9},{5... | collective-permute-start | bytes 3145736 | tf_op jit(solution)/shard_map/ppermute | solution.py:26
  98.5 77.0 %collective-permute-start.9 = (bf16[256,2048]{1,0:T(8,128)(2,1)}, bf16[256,2048]{1,0:T(8,128)(2,1)}, u32[]{:S(2)}, u32[]{:S(2)}) collective-permute-start(bf16[256,2048]{1,0:T(8,128)(2,1)} %param.13), channel_id=1, source_target_pairs={{0,16},{4,20},{8,24},{12,28},{16,0},{20,4},{24,8},{28,12},{1,17},{... | collective-permute-start | bytes 3145736 | tf_op jit(solution)/shard_map/ppermute | solution.py:26
  99.9 77.9 %collective-permute-start.8 = (bf16[256,2048]{1,0:T(8,128)(2,1)}, bf16[256,2048]{1,0:T(8,128)(2,1)}, u32[]{:S(2)}, u32[]{:S(2)}) collective-permute-start(bf16[256,2048]{1,0:T(8,128)(2,1)} %param.13), channel_id=1, source_target_pairs={{0,8},{4,12},{8,0},{12,4},{16,24},{20,28},{24,16},{28,20},{1,9},{5... | collective-permute-start | bytes 3145736 | tf_op jit(solution)/shard_map/ppermute | solution.py:26
  175.5 77.3 %collective-permute-start.12 = (bf16[256,2048]{1,0:T(8,128)(2,1)}, bf16[256,2048]{1,0:T(8,128)(2,1)}, u32[]{:S(2)}, u32[]{:S(2)}) collective-permute-start(bf16[256,2048]{1,0:T(8,128)(2,1)} %param.13), channel_id=1, source_target_pairs={{0,4},{4,0},{8,12},{12,8},{16,20},{20,16},{24,28},{28,24},{1,5},{5... | collective-permute-start | bytes 3145736 | tf_op jit(solution)/shard_map/ppermute | solution.py:26
  246.2 692.4 %reduce-scatter.5.cloned.1.call-start = ((), (), s32[]{:S(2)}) async-start(), calls=%async_computation.3 | async-start | bytes 1310720 | tf_op jit(solution)/shard_map/reduce_scatter | solution.py:403
  432.6 73.0 %collective-permute-start.88 = (bf16[256,1408]{0,1:T(8,128)(2,1)}, bf16[256,1408]{0,1:T(8,128)(2,1)S(1)}, u32[]{:S(2)}, u32[]{:S(2)}) collective-permute-start(bf16[256,1408]{0,1:T(8,128)(2,1)} %get-tuple-element.56), channel_id=1, source_target_pairs={{0,24},{4,28},{8,16},{12,20},{16,8},{20,12},{24,0},{28,4},{1,25},{... | collective-permute-start | bytes 2162696 | tf_op jit(solution)/shard_map/ppermute | solution.py:26
  434.5 71.1 %collective-permute-start.65 = (bf16[256,1408]{0,1:T(8,128)(2,1)S(1)}, bf16[256,1408]{0,1:T(8,128)(2,1)S(1)}, u32[]{:S(2)}, u32[]{:S(2)}) collective-permute-start(bf16[256,1408]{0,1:T(8,128)(2,1)S(1)} %get-tuple-element.62), channel_id=1, source_target_pairs={{0,1},{3,2},{4,5},{7,6},{8,9},{11,10},{12,13},{15,14},{16,17},{19,... | collective-permute-start | bytes 2162696 | tf_op jit(solution)/shard_map/ppermute | solution.py:102
  538.9 221.4 %collective-permute-start.44 = (bf16[1024,2048]{1,0:T(8,128)(2,1)S(1)}, bf16[1024,2048]{1,0:T(8,128)(2,1)S(1)}, u32[]{:S(2)}, u32[]{:S(2)}) collective-permute-start(bf16[1024,2048]{1,0:T(8,128)(2,1)S(1)} %slice.473), channel_id=1, source_target_pairs={{0,4},{4,0},{8,12},{12,8},{16,20},{20,16},{24,28},{28,24},{1,5},{5... | collective-permute-start | bytes 12582920 | tf_op jit(solution)/shard_map/ppermute | solution.py:26
  554.4 210.8 %collective-permute-start.31 = (bf16[1024,2048]{1,0:T(8,128)(2,1)}, bf16[1024,2048]{1,0:T(8,128)(2,1)}, u32[]{:S(2)}, u32[]{:S(2)}) collective-permute-start(bf16[1024,2048]{1,0:T(8,128)(2,1)} %slice.456), channel_id=1, source_target_pairs={{0,4},{4,0},{8,12},{12,8},{16,20},{20,16},{24,28},{28,24},{1,5},{5... | collective-permute-start | bytes 12582920 | tf_op jit(solution)/shard_map/ppermute | solution.py:26
  619.8 137.2 %collective-permute-start.74 = (bf16[256,1408]{0,1:T(8,128)(2,1)S(1)}, bf16[256,1408]{0,1:T(8,128)(2,1)S(1)}, u32[]{:S(2)}, u32[]{:S(2)}) collective-permute-start(bf16[256,1408]{0,1:T(8,128)(2,1)S(1)} %add_convert_fusion.30), channel_id=1, source_target_pairs={{1,2},{2,1},{5,6},{6,5},{9,10},{10,9},{13,14},{14,13},{17,18},{18,... | collective-permute-start | bytes 2162696 | tf_op jit(solution)/shard_map/ppermute | solution.py:103
  621.6 116.5 %collective-permute-start.98 = (bf16[176,2048]{1,0:T(8,128)(2,1)S(1)}, bf16[176,2048]{1,0:T(8,128)(2,1)S(1)}, u32[]{:S(2)}, u32[]{:S(2)}) collective-permute-start(bf16[176,2048]{1,0:T(8,128)(2,1)S(1)} %add_convert_fusion.17), channel_id=1, source_target_pairs={{1,0},{2,3},{5,4},{6,7},{9,8},{10,11},{13,12},{14,15},{17,16},{18,... | collective-permute-start | bytes 2162696 | tf_op jit(solution)/shard_map/ppermute | solution.py:105
  623.9 130.8 %collective-permute-start.101 = (bf16[176,2048]{1,0:T(8,128)(2,1)S(1)}, bf16[176,2048]{1,0:T(8,128)(2,1)S(1)}, u32[]{:S(2)}, u32[]{:S(2)}) collective-permute-start(bf16[176,2048]{1,0:T(8,128)(2,1)S(1)} %add_convert_fusion.15), channel_id=1, source_target_pairs={{1,0},{2,3},{5,4},{6,7},{9,8},{10,11},{13,12},{14,15},{17,16},{18,... | collective-permute-start | bytes 2162696 | tf_op jit(solution)/shard_map/ppermute | solution.py:105
  754.8 135.3 %collective-permute-start.67 = (bf16[256,1408]{0,1:T(8,128)(2,1)}, bf16[256,1408]{0,1:T(8,128)(2,1)}, u32[]{:S(2)}, u32[]{:S(2)}) collective-permute-start(bf16[256,1408]{0,1:T(8,128)(2,1)} %add_convert_fusion.33), channel_id=1, source_target_pairs={{1,0},{2,3},{5,4},{6,7},{9,8},{10,11},{13,12},{14,15},{17,16},{18,... | collective-permute-start | bytes 2162696 | tf_op jit(solution)/shard_map/ppermute | solution.py:105
  812.3 70.8 %collective-permute-start.107 = (bf16[176,2048]{1,0:T(8,128)(2,1)S(1)}, bf16[176,2048]{1,0:T(8,128)(2,1)}, u32[]{:S(2)}, u32[]{:S(2)}) collective-permute-start(bf16[176,2048]{1,0:T(8,128)(2,1)S(1)} %add_convert_fusion.11), channel_id=1, source_target_pairs={{1,0},{2,3},{5,4},{6,7},{9,8},{10,11},{13,12},{14,15},{17,16},{18,... | collective-permute-start | bytes 2162696 | tf_op jit(solution)/shard_map/ppermute | solution.py:105
  820.0 176.4 %collective-permute-start.95 = (bf16[256,1408]{0,1:T(8,128)(2,1)}, bf16[256,1408]{0,1:T(8,128)(2,1)}, u32[]{:S(2)}, u32[]{:S(2)}) collective-permute-start(bf16[256,1408]{0,1:T(8,128)(2,1)} %add_convert_fusion.19), channel_id=1, source_target_pairs={{1,0},{2,3},{5,4},{6,7},{9,8},{10,11},{13,12},{14,15},{17,16},{18,... | collective-permute-start | bytes 2162696 | tf_op jit(solution)/shard_map/ppermute | solution.py:105
  826.6 136.8 %collective-permute-start.83 = (bf16[256,1408]{0,1:T(8,128)(2,1)}, bf16[256,1408]{0,1:T(8,128)(2,1)}, u32[]{:S(2)}, u32[]{:S(2)}) collective-permute-start(bf16[256,1408]{0,1:T(8,128)(2,1)} %add_convert_fusion.25), channel_id=1, source_target_pairs={{1,0},{2,3},{5,4},{6,7},{9,8},{10,11},{13,12},{14,15},{17,16},{18,... | collective-permute-start | bytes 2162696 | tf_op jit(solution)/shard_map/ppermute | solution.py:105
  832.5 127.5 %collective-permute-start.79 = (bf16[256,1408]{0,1:T(8,128)(2,1)}, bf16[256,1408]{0,1:T(8,128)(2,1)}, u32[]{:S(2)}, u32[]{:S(2)}) collective-permute-start(bf16[256,1408]{0,1:T(8,128)(2,1)} %add_convert_fusion.27), channel_id=1, source_target_pairs={{1,0},{2,3},{5,4},{6,7},{9,8},{10,11},{13,12},{14,15},{17,16},{18,... | collective-permute-start | bytes 2162696 | tf_op jit(solution)/shard_map/ppermute | solution.py:105
  883.0 305.2 %reduce-scatter.7.cloned.1.call-start = ((), (), s32[]{:S(2)}) async-start(), calls=%async_computation.4 | async-start | bytes 1179648
  957.3 82.2 %collective-permute-start.49 = (bf16[1024,2560]{1,0:T(8,128)(2,1)}, bf16[1024,2560]{1,0:T(8,128)(2,1)}, u32[]{:S(2)}, u32[]{:S(2)}) collective-permute-start(bf16[1024,2560]{1,0:T(8,128)(2,1)} %slice.491), channel_id=1, source_target_pairs={{0,4},{4,0},{8,12},{12,8},{16,20},{20,16},{24,28},{28,24},{1,5},{5... | collective-permute-start | bytes 15728648 | tf_op jit(solution)/shard_map/ppermute | solution.py:26
  (160 other events, 4759.6 us)
Sparse Core Ops, SparseCore 0:
  246.3 28.2 all-gather.1
  883.2 43.1 reduce-scatter.4
  1151.6 36.5 reduce-scatter.6

commit v2 on v1

v2 whole, which is shorter than its diff:
```python
import functools

import jax
import jax.numpy as jnp
from jax import lax
from jax.experimental import pallas as pl
from jax.experimental.pallas import tpu as pltpu
from jax.sharding import PartitionSpec as P

HEADS = 32
KVH = 4
HD = 64
FF = 5632

epsilon = 1e-05
masked_value = -1e30
log2e = 1.4426950408889634
contract_last = (((1,), (1,)), ((), ()))
contract_first = (((0,), (0,)), ((), ()))
bf16 = jnp.bfloat16
f32 = jnp.float32


def send(x, k):
    n = lax.axis_size("fsdp")
    return lax.ppermute(x, "fsdp", [(i, i ^ k) for i in range(n)])


def chip_bits():
    n = lax.axis_size("fsdp")
    return [1 << i for i in range(1, n.bit_length() - 1)]


def piece_order():
    n = lax.axis_size("fsdp")
    return list(range(0, n, 2)) + list(range(1, n, 2))


def gather_small(x):
    n, me = lax.axis_size("fsdp"), lax.axis_index("fsdp")
    for k in (1 << i for i in range(n.bit_length() - 1)):
        got = send(x, k)
        x = jnp.where(
            me & k == 0, jnp.concatenate([x, got], 1), jnp.concatenate([got, x], 1)
        )
    return x


def neighbour(x):
    n = lax.axis_size("seq")
    return lax.ppermute(x, "seq", [(i, i ^ 1) for i in range(n)])


def after(x, *others):
    return lax.optimization_barrier((x, *others))[0]


def added(one, two):
    return (one.astype(f32) + two.astype(f32)).astype(bf16)


def line_sum(x):
    n = lax.axis_size("seq")
    if n == 1:
        return x
    if n % 2:
        return lax.psum(x.astype(f32), "seq").astype(bf16)
    me = lax.axis_index("seq")
    mid = n // 2
    total = x
    for i in range(mid - 1):
        total = added(total, lax.ppermute(total, "seq", [(i, i + 1), (n - 1 - i, n - 2 - i)]))
    total = added(total, lax.ppermute(total, "seq", [(mid - 1, mid), (mid, mid - 1)]))
    for i in range(mid - 1):
        got = lax.ppermute(total, "seq", [(mid - 1 - i, mid - 2 - i), (mid + i, mid + 1 + i)])
        taken = (me == mid - 2 - i) | (me == mid + 1 + i)
        total = jnp.where(taken, got, total)
    return total


def line_step(live, new=None, cross=None, out=None):
    if lax.axis_size("seq") != 4:
        if new is not None:
            live["o" + new] = live["t" + new] = line_sum(live["z" + new])
        return
    inward, outward, across = [(0, 1), (3, 2)], [(1, 0), (2, 3)], [(1, 2), (2, 1)]
    x = total = None
    if out is not None:
        total = live["t" + out] = added(live["p" + out], live["x" + out])
    if new is not None:
        x = live["z" + new]
    if x is not None and total is not None and x.shape == total.shape:
        got = lax.ppermute(jnp.where(is_outer(), x, total), "seq", inward + outward)
        live["i" + new] = live["o" + out] = got
    else:
        if x is not None:
            live["i" + new] = lax.ppermute(x, "seq", inward)
        if total is not None:
            live["o" + out] = lax.ppermute(total, "seq", outward)
    if cross is not None:
        part = live["p" + cross] = added(live["z" + cross], live["i" + cross])
        live["x" + cross] = lax.ppermute(part, "seq", across)


def is_outer():
    me, n = lax.axis_index("seq"), lax.axis_size("seq")
    return (me == 0) | (me == n - 1)


def small_sum(x):
    for axis in ("fsdp", "seq"):
        n = lax.axis_size(axis)
        if n & (n - 1):
            x = lax.psum(x, axis)
            continue
        for k in (1 << i for i in range(n.bit_length() - 1)):
            x = x + lax.ppermute(x, axis, [(i, i ^ k) for i in range(n)])
    return x


def copy_kernel(table_ref, x_ref, o_ref):
    o_ref[...] = x_ref[...].astype(o_ref.dtype)


def pick(x, table, size, dtype=None, rows_at=None):
    rows, count = x.shape[0], table.shape[0]
    if size % 128:
        return jnp.concatenate(
            [lax.dynamic_slice_in_dim(x, table[i] * size, size, 1) for i in range(count)], 1
        ).astype(dtype or x.dtype)
    if rows_at is not None:
        rows = rows_at[1]
    row = jnp.zeros((), jnp.int32) if rows_at is None else rows_at[0]
    table = jnp.concatenate([table, row.reshape(1)]).astype(jnp.int32)
    return pl.pallas_call(
        copy_kernel,
        out_shape=jax.ShapeDtypeStruct((rows, count * size), dtype or x.dtype),
        grid_spec=pltpu.PrefetchScalarGridSpec(
            num_scalar_prefetch=1,
            grid=(count,),
            in_specs=[pl.BlockSpec((rows, size), lambda i, table: (table[count], table[i]))],
            out_specs=pl.BlockSpec((rows, size), lambda i, table: (0, i)),
        ),
        cost_estimate=pl.CostEstimate(
            flops=0, transcendentals=0, bytes_accessed=rows * count * size * 4
        ),
    )(table, x)


def blank_kernel(o_ref):
    pass


def blank(shape, dtype):
    return pl.pallas_call(
        blank_kernel,
        out_shape=jax.ShapeDtypeStruct(shape, dtype),
        out_specs=pl.BlockSpec(memory_space=pl.ANY),
    )()


def turn_kernel(sign, x_ref, cos_ref, sin_ref, o_ref):
    x = x_ref[...].astype(f32)
    width = x.shape[1]
    lane = lax.broadcasted_iota(jnp.int32, x.shape, 1)
    first = (lane % HD) < HD // 2
    other = jnp.where(
        first, -pltpu.roll(x, width - HD // 2, 1), pltpu.roll(x, HD // 2, 1)
    )
    o_ref[...] = (x * cos_ref[...] + sign * other * sin_ref[...]).astype(o_ref.dtype)


def turn(x, cos_wide, sin_wide, sign):
    return pl.pallas_call(
        functools.partial(turn_kernel, float(sign)),
        out_shape=jax.ShapeDtypeStruct(x.shape, bf16),
    )(x, cos_wide, sin_wide)


def place_kernel(info_ref, buffer_ref, got_ref, total_ref, o_ref):
    o_ref[...] = jnp.where(info_ref[0] == 1, got_ref[...], total_ref[...]).astype(f32)


def place(buffer, pair, outer, where, size):
    got, total = pair
    rows = got.shape[0]
    if size % 128:
        picked = jnp.where(outer, got, total).astype(f32)
        for i in range(2):
            buffer = lax.dynamic_update_slice_in_dim(
                buffer, picked[:, i * size : (i + 1) * size], where[i] * size, 1
            )
        return buffer
    info = jnp.concatenate([outer.astype(jnp.int32).reshape(1), where.astype(jnp.int32)])
    own = pl.BlockSpec((rows, size), lambda i, info: (0, i))
    return pl.pallas_call(
        place_kernel,
        out_shape=jax.ShapeDtypeStruct(buffer.shape, f32),
        grid_spec=pltpu.PrefetchScalarGridSpec(
            num_scalar_prefetch=1,
            grid=(2,),
            in_specs=[pl.BlockSpec(memory_space=pl.ANY), own, own],
            out_specs=pl.BlockSpec((rows, size), lambda i, info: (0, info[1 + i])),
        ),
        input_output_aliases={1: 0},
    )(info, buffer, got, total)


def mask_bias(start, length, rows):
    key_place = lax.broadcasted_iota(jnp.int32, (length, rows), 0)
    query_place = start + lax.broadcasted_iota(jnp.int32, (length, rows), 1)
    return jnp.where(key_place <= query_place, 0.0, masked_value).astype(f32)


def turned_t(x, cos, sin):
    one, two = x[: HD // 2], x[HD // 2 :]
    return jnp.concatenate([one * cos - two * sin, two * cos + one * sin], 0)


def kv_head(ref, index):
    both = ref[...]
    return jnp.where(index % 2 == 0, both[:, :HD], both[:, HD:])


def attend_kernel(
    heads, per_kv, info_ref, q_ref, k_ref, v_ref, cos_ref, sin_ref, o_ref, lse_ref, bias_ref
):
    length, rows = k_ref.shape[0], q_ref.shape[0]
    scale2 = HD**-0.5 * log2e
    step = pl.program_id(0)

    @pl.when(step == 0)
    def _():
        bias_ref[...] = mask_bias(info_ref[0], length, rows)

    kv = step * heads // per_kv
    keys = kv_head(k_ref, kv)
    values_t = kv_head(v_ref, kv).astype(f32).T.astype(bf16)
    q_t = q_ref[...].T
    cos, sin = cos_ref[...], sin_ref[...]
    outs = []
    for h in range(heads):
        q_h = turned_t(q_t[h * HD : (h + 1) * HD], cos, sin).astype(bf16)
        scores = jnp.dot(keys, q_h, preferred_element_type=f32) + bias_ref[...]
        top = jnp.max(scores, axis=0, keepdims=True)
        weights = jnp.exp2((scores - top) * scale2)
        total = jnp.sum(weights, axis=0, keepdims=True)
        probs = (weights * (1.0 / total)).astype(bf16)
        outs.append(jnp.dot(values_t, probs, preferred_element_type=f32))
        lse_ref[0, h : h + 1, :] = top * scale2 + jnp.log2(total)
    o_ref[...] = jnp.concatenate(outs, 0).T.astype(bf16)


def attend_specs(n, rows, length):
    heads = HEADS // n
    per_kv = HEADS // KVH
    kv_at = lambda i: (i * heads // per_kv) // 2
    return dict(
        plain=pl.BlockSpec((rows, heads * HD), lambda i, info: (0, i)),
        ordered=pl.BlockSpec((rows, heads * HD), lambda i, info: (0, info[1 + i])),
        keys=pl.BlockSpec((length, 2 * HD), lambda i, info: (0, kv_at(i))),
        values=pl.BlockSpec((length, 2 * HD), lambda i, info: (0, KVH // 2 + kv_at(i))),
        table=pl.BlockSpec((HD // 2, rows), lambda i, info: (0, 0)),
        lse=pl.BlockSpec((1, heads, rows), lambda i, info: (i, 0, 0)),
    )


def attend(info, joined, all_kv, cos_t, sin_t):
    n = lax.axis_size("fsdp")
    rows, length = joined.shape[0], all_kv.shape[0]
    heads = HEADS // n
    spec = attend_specs(n, rows, length)
    return pl.pallas_call(
        functools.partial(attend_kernel, heads, HEADS // KVH),
        out_shape=(
            jax.ShapeDtypeStruct((rows, HEADS * HD), bf16),
            jax.ShapeDtypeStruct((n, heads, rows), f32),
        ),
        grid_spec=pltpu.PrefetchScalarGridSpec(
            num_scalar_prefetch=1,
            grid=(n,),
            in_specs=[spec[k] for k in ("plain", "keys", "values", "table", "table")],
            out_specs=(spec["ordered"], spec["lse"]),
            scratch_shapes=[pltpu.VMEM((length, rows), f32)],
        ),
        compiler_params=pltpu.CompilerParams(vmem_limit_bytes=40 << 20),
        cost_estimate=pl.CostEstimate(
            flops=4 * HEADS * rows * length * HD * 4,
            bytes_accessed=6 * rows * HEADS * HD,
            transcendentals=HEADS * rows * length,
        ),
    )(info, joined, all_kv, all_kv, cos_t, sin_t)


def attend_back_kernel(
    heads, per_kv, info_ref, q_ref, k_ref, v_ref, g_ref, cos_ref, sin_ref, lse_ref,
    dq_ref, dkv_ref, bias_ref, dk_ref, dv_ref,
):
    length, rows = k_ref.shape[0], q_ref.shape[0]
    scale = HD**-0.5
    scale2 = scale * log2e
    step = pl.program_id(0)
    steps = per_kv // heads

    @pl.when(step == 0)
    def _():
        bias_ref[...] = mask_bias(info_ref[0], length, rows)

    @pl.when(step % steps == 0)
    def _():
        dk_ref[...] = jnp.zeros_like(dk_ref)
        dv_ref[...] = jnp.zeros_like(dv_ref)

    kv = step * heads // per_kv
    keys, values = kv_head(k_ref, kv), kv_head(v_ref, kv)
    keys_t = keys.astype(f32).T.astype(bf16)
    q_t = q_ref[...].T
    g_t = g_ref[...].astype(f32).T.astype(bf16)
    cos, sin = cos_ref[...], sin_ref[...]
    outs = []
    dk, dv = dk_ref[...], dv_ref[...]
    for h in range(heads):
        q_h = turned_t(q_t[h * HD : (h + 1) * HD], cos, sin).astype(bf16)
        g_h = g_t[h * HD : (h + 1) * HD]
        scores = jnp.dot(keys, q_h, preferred_element_type=f32) + bias_ref[...]
        weights = jnp.exp2(scores * scale2 - lse_ref[0, h : h + 1, :])
        grad_p = jnp.dot(values, g_h, preferred_element_type=f32)
        delta = jnp.sum(grad_p * weights, axis=0, keepdims=True)
        grad_s = (weights * (grad_p - delta)).astype(bf16)
        grad_q = jnp.dot(keys_t, grad_s, preferred_element_type=f32) * scale
        outs.append(turned_t(grad_q.astype(bf16).astype(f32), cos, -sin))
        dk += lax.dot_general(grad_s, q_h, contract_last, preferred_element_type=f32)
        dv += lax.dot_general(
            weights.astype(bf16), g_h, contract_last, preferred_element_type=f32
        )
    dk_ref[...], dv_ref[...] = dk, dv
    dq_ref[...] = jnp.concatenate(outs, 0).T.astype(bf16)

    @pl.when(step % steps == steps - 1)
    def _():
        dkv_ref[0] = jnp.concatenate([dk * scale, dv], 1).astype(bf16)


def attend_back(info, joined, all_kv, cos_t, sin_t, grads, lse):
    n = lax.axis_size("fsdp")
    rows, length = joined.shape[0], all_kv.shape[0]
    heads, per_kv = HEADS // n, HEADS // KVH
    spec = attend_specs(n, rows, length)
    names = ("plain", "keys", "values", "ordered", "table", "table", "lse")
    return pl.pallas_call(
        functools.partial(attend_back_kernel, heads, per_kv),
        out_shape=(
            jax.ShapeDtypeStruct((rows, HEADS * HD), bf16),
            jax.ShapeDtypeStruct((KVH, length, 2 * HD), bf16),
        ),
        grid_spec=pltpu.PrefetchScalarGridSpec(
            num_scalar_prefetch=1,
            grid=(n,),
            in_specs=[spec[k] for k in names],
            out_specs=(
                spec["plain"],
                pl.BlockSpec((1, length, 2 * HD), lambda i, info: (i * heads // per_kv, 0, 0)),
            ),
            scratch_shapes=[
                pltpu.VMEM((length, rows), f32),
                pltpu.VMEM((length, HD), f32),
                pltpu.VMEM((length, HD), f32),
            ],
        ),
        compiler_params=pltpu.CompilerParams(vmem_limit_bytes=48 << 20),
        cost_estimate=pl.CostEstimate(
            flops=10 * HEADS * rows * length * HD * 4,
            bytes_accessed=8 * rows * HEADS * HD,
            transcendentals=HEADS * rows * length,
        ),
    )(info, joined, all_kv, all_kv, grads, cos_t, sin_t, lse)


def column_chunks(total, size=256):
    return [(c, min(size, total - c)) for c in range(0, total, size)]


def ffn_kernel(n, count, info_ref, *refs):
    x_refs, g_refs, refs = refs[:count], refs[count : 2 * count], refs[2 * count :]
    w_own, w_other, d_own, d_other = refs[:4]
    outs, (x, g, w, d, both, mid, sems) = refs[4 : 4 + 4 * count], refs[4 + 4 * count :]
    mixed_refs, both_refs = outs[:count], outs[count : 2 * count]
    back_refs, out_refs = outs[2 * count : 3 * count], outs[3 * count :]
    me, part = info_ref[0], info_ref[1]
    rows, width = x_refs[0].shape
    cols = d.shape[0]
    share = cols // 2
    block = width // n
    half = block // 2
    evens = range(0, n, 2)

    copies = []
    for source, flip in ((w_own, 0), (w_other, 1)):
        for i, k in enumerate(evens):
            owner = (me ^ (k | flip)) * block
            for j in range(2):
                at = owner if k == 0 else owner + (part if j == 0 else 1 - part) * half
                if k == 0:
                    at = at + j * half
                copies.append(
                    pltpu.make_async_copy(
                        source.at[pl.ds(i * block + j * half, half)],
                        w.at[pl.ds(pl.multiple_of(at, half), half)],
                        sems.at[len(copies)],
                    )
                )
    core = me % 2
    for source, at in ((d_own, core), (d_other, 1 - core)):
        copies.append(
            pltpu.make_async_copy(
                source, d.at[pl.ds(pl.multiple_of(at * share, share), share)], sems.at[len(copies)]
            )
        )
    for copy in copies:
        copy.start()
    for i in range(count):
        x[i * rows : (i + 1) * rows] = x_refs[i][...]
        g[i * rows : (i + 1) * rows] = g_refs[i][...]
    for copy in copies:
        copy.wait()

    def columns(at, size):
        gate_w, up_w = w[:, pl.ds(at, size)], w[:, pl.ds(cols + at, size)]
        gate = jnp.dot(x[...], gate_w, preferred_element_type=f32)
        up = jnp.dot(x[...], up_w, preferred_element_type=f32)
        grad = lax.dot_general(
            g[...], d[pl.ds(at, size)], contract_last, preferred_element_type=f32
        )
        sig = 1.0 / (1.0 + jnp.exp(-gate))
        act = gate * sig
        mid[:, pl.ds(at, size)] = (act * up).astype(bf16)
        both[:, pl.ds(at, size)] = (grad * up * (sig * (1.0 + gate * (1.0 - sig)))).astype(bf16)
        both[:, pl.ds(cols + at, size)] = (grad * act).astype(bf16)

    full = cols // 256
    pl.loop(0, full)(lambda c: columns(pl.multiple_of(c * 256, 256), 256))
    if cols % 256:
        columns(full * 256, cols % 256)
    for i in range(count):
        at = slice(i * rows, (i + 1) * rows)
        mixed_refs[i][...] = mid[at].astype(f32).T.astype(bf16)
        both_refs[i][...] = both[at]

    @pl.loop(0, width // 256)
    def _(t):
        at = pl.multiple_of(t * 256, 256)
        back = lax.dot_general(
            both[...], w[pl.ds(at, 256)], contract_last, preferred_element_type=f32
        ).astype(bf16)
        out = jnp.dot(mid[...], d[:, pl.ds(at, 256)], preferred_element_type=f32).astype(bf16)
        for i in range(count):
            back_refs[i][:, pl.ds(at, 256)] = back[i * rows : (i + 1) * rows]
            out_refs[i][:, pl.ds(at, 256)] = out[i * rows : (i + 1) * rows]


def ffn(info, xs, gs, w_own, w_other, d_own, d_other):
    n = lax.axis_size("fsdp")
    count = len(xs)
    rows, width = xs[0].shape
    cols = 2 * d_own.shape[0]
    if cols % 128:
        return ffn_plain(info, xs, gs, w_own, w_other, d_own, d_other)
    shapes = (
        [jax.ShapeDtypeStruct((cols, rows), bf16)] * count
        + [jax.ShapeDtypeStruct((rows, 2 * cols), bf16)] * count
        + [jax.ShapeDtypeStruct((rows, width), bf16)] * (2 * count)
    )
    vmem, hbm = pl.BlockSpec(memory_space=pltpu.VMEM), pl.BlockSpec(memory_space=pl.ANY)
    outs = pl.pallas_call(
        functools.partial(ffn_kernel, n, count),
        out_shape=shapes,
        in_specs=[pl.BlockSpec(memory_space=pltpu.SMEM)] + [vmem] * (2 * count) + [hbm] * 4,
        out_specs=[vmem] * (4 * count),
        scratch_shapes=[
            pltpu.VMEM((count * rows, width), bf16),
            pltpu.VMEM((count * rows, width), bf16),
            pltpu.VMEM((width, 2 * cols), bf16),
            pltpu.VMEM((cols, width), bf16),
            pltpu.VMEM((count * rows, 2 * cols), bf16),
            pltpu.VMEM((count * rows, cols), bf16),
            pltpu.SemaphoreType.DMA((2 * n + 2,)),
        ],
        compiler_params=pltpu.CompilerParams(vmem_limit_bytes=56 << 20),
        cost_estimate=pl.CostEstimate(
            flops=2 * count * rows * width * cols * 6,
            bytes_accessed=6 * width * cols,
            transcendentals=count * rows * cols,
        ),
    )(info, *xs, *gs, w_own, w_other, d_own, d_other)
    return [outs[i * count : (i + 1) * count] for i in range(4)]


def ffn_plain(info, xs, gs, w_own, w_other, d_own, d_other):
    n = lax.axis_size("fsdp")
    me, part = info[0], info[1]
    width, share = xs[0].shape[1], d_own.shape[0]
    block, cols = width // n, 2 * share
    half = block // 2
    w = jnp.zeros((width, 2 * cols), bf16)
    for source, flip in ((w_own, 0), (w_other, 1)):
        for i, k in enumerate(range(0, n, 2)):
            for j in range(2):
                at = j if k == 0 else (part if j == 0 else 1 - part)
                rows = source[i * block + j * half : i * block + (j + 1) * half]
                w = lax.dynamic_update_slice_in_dim(w, rows, (me ^ (k | flip)) * block + at * half, 0)
    d = jnp.where(
        me % 2 == 0, jnp.concatenate([d_own, d_other], 0), jnp.concatenate([d_other, d_own], 0)
    )
    mixed, both, back, out = [], [], [], []
    for x, g in zip(xs, gs, strict=True):
        gate, up = dot(x, w[:, :cols]), dot(x, w[:, cols:])
        sig = jax.nn.sigmoid(gate)
        act = gate * sig
        grad = dot_last(g, d)
        mid = (act * up).astype(bf16)
        two = jnp.concatenate(
            [grad * up * (sig * (1.0 + gate * (1.0 - sig))), grad * act], 1
        ).astype(bf16)
        mixed.append(mid.T)
        both.append(two)
        back.append(dot_last(two, w).astype(bf16))
        out.append(dot(mid, d).astype(bf16))
    return mixed, both, back, out


def down_grad_kernel(count, info_ref, *refs):
    lefts, rights, rest = refs[:count], refs[count : 2 * count], refs[2 * count :]
    total = sum(
        jnp.dot(one[...], two[...], preferred_element_type=f32)
        for one, two in zip(lefts, rights, strict=True)
    )
    if len(rest) == 2:
        total = total.astype(bf16).astype(f32) + rest[0][...].astype(f32)
    rest[-1][...] = total.astype(bf16)


def down_grad(info, at, mixed, gs, got=None):
    count = len(mixed)
    cols, rows = mixed[0].shape
    width = gs[0].shape[1]
    size = min(512, width)
    out = pl.BlockSpec((cols // 2, size), lambda i, info: (0, i))
    return pl.pallas_call(
        functools.partial(down_grad_kernel, count),
        out_shape=jax.ShapeDtypeStruct((cols // 2, width), bf16),
        grid_spec=pltpu.PrefetchScalarGridSpec(
            num_scalar_prefetch=1,
            grid=(width // size,),
            in_specs=[pl.BlockSpec((cols // 2, rows), lambda i, info: (info[at], 0))] * count
            + [pl.BlockSpec((rows, size), lambda i, info: (0, i))] * count
            + ([] if got is None else [out]),
            out_specs=out,
        ),
        compiler_params=pltpu.CompilerParams(vmem_limit_bytes=40 << 20),
        cost_estimate=pl.CostEstimate(
            flops=count * rows * width * cols,
            bytes_accessed=4 * width * cols,
            transcendentals=0,
        ),
    )(info, *mixed, *gs, *([] if got is None else [got]))


def up_grad_kernel(count, chips, info_ref, *refs):
    lefts, rights, rest = refs[:count], refs[count : 2 * count], refs[2 * count :]
    gots, outs = rest[:-chips], rest[-chips:]
    total = sum(
        lax.dot_general(one[...], two[...], contract_first, preferred_element_type=f32)
        for one, two in zip(lefts, rights, strict=True)
    )
    for i in range(chips):

        @pl.when(pl.program_id(1) == i)
        def _(i=i):
            if gots:
                outs[i][...] = (
                    total.astype(bf16).astype(f32) + gots[i][...].astype(f32)
                ).astype(bf16)
            else:
                outs[i][...] = total.astype(bf16)


def up_grad(table, xs, both, gots=()):
    count, chips = len(xs), table.shape[0]
    rows, width = xs[0].shape
    cols = both[0].shape[1] // 2
    block = width // lax.axis_size("fsdp")
    if cols % 128 or block % 128:
        whole = sum(dot_first(one, two) for one, two in zip(xs, both, strict=True))
        outs = [
            lax.dynamic_slice_in_dim(whole, table[i] * block, block, 0).astype(bf16)
            for i in range(chips)
        ]
        return [added(one, two) for one, two in zip(outs, gots)] if gots else outs
    outs = [
        pl.BlockSpec(
            (block, cols), lambda h, b, table, i=i: (0, jnp.where(b >= i, h, jnp.maximum(h - 1, 0)))
        )
        for i in range(chips)
    ]
    return pl.pallas_call(
        functools.partial(up_grad_kernel, count, chips),
        out_shape=[jax.ShapeDtypeStruct((block, 2 * cols), bf16)] * chips,
        grid_spec=pltpu.PrefetchScalarGridSpec(
            num_scalar_prefetch=1,
            grid=(2, chips),
            in_specs=[pl.BlockSpec((rows, block), lambda h, b, table: (0, table[b]))] * count
            + [pl.BlockSpec((rows, cols), lambda h, b, table: (0, h))] * count
            + (outs if gots else []),
            out_specs=outs,
        ),
        compiler_params=pltpu.CompilerParams(vmem_limit_bytes=48 << 20),
        cost_estimate=pl.CostEstimate(
            flops=4 * count * rows * chips * block * cols,
            bytes_accessed=4 * chips * block * cols * 2,
            transcendentals=0,
        ),
    )(table, *xs, *both, *gots)


def angle_tables(positions):
    half_dim = HD // 2
    inverse = 10000.0 ** (-jnp.arange(half_dim, dtype=f32) * 2.0 / HD)
    angles = positions.astype(f32)[:, None] * inverse[None, :]
    return jnp.cos(angles), jnp.sin(angles)


def norm_factor(values):
    return lax.rsqrt(jnp.mean(values * values, axis=-1, keepdims=True) + epsilon)


def norm_back(incoming, inputs, factor, gain):
    weighted = incoming * gain
    gain_grad = jnp.sum(incoming * (inputs * factor), axis=0)
    input_grad = weighted * factor - inputs * (factor * factor * factor) * jnp.mean(
        weighted * inputs, axis=-1, keepdims=True
    )
    return (gain_grad, input_grad)


def dot(one, two):
    return jnp.dot(one, two, preferred_element_type=f32)


def dot_last(one, two):
    return lax.dot_general(one, two, contract_last, preferred_element_type=f32)


def dot_first(one, two):
    return lax.dot_general(one, two, contract_first, preferred_element_type=f32)


def on_device(
    hidden_in, norm_attn, qkv_weight, out_weight, norm_ffn, gate_up_weight, down_weight, cotangent
):
    n = lax.axis_size("fsdp")
    me = lax.axis_index("fsdp")
    chips, chip, core = n // 2, me // 2, me % 2
    order = piece_order()
    evens = order[:chips]
    near, rest = evens[1:3], evens[3:]
    width = hidden_in.shape[2]
    rows = hidden_in.shape[0] * hidden_in.shape[1]
    q_width = HEADS * HD
    kv_width = KVH * HD
    share = FF // n
    chip_share = 2 * share
    block = width // n
    half = block // 2
    seq_at = lax.axis_index("seq")
    rank = {k: i for i, k in enumerate(order)}
    to_table = (me ^ jnp.array(order, jnp.int32)).astype(jnp.int32)
    at_table = jnp.array([rank[k] for k in range(n)], jnp.int32)[
        me ^ jnp.arange(n, dtype=jnp.int32)
    ]
    odd_table, even_table = to_table[chips:], to_table[:chips]
    assisted = lax.axis_size("seq") % 2 == 0
    part_at = seq_at % 2 if assisted else jnp.zeros_like(seq_at)

    live = {}

    def fence(**more):
        live.update(more)
        new = lax.optimization_barrier(live)
        live.clear()
        live.update(new)

    def two_hops(pieces):
        if len(rest) != 1:
            return {k: send(pieces[0], k) for k in rest}
        a, b = near
        size = pieces[0].shape[0] // 2
        lower, upper = send(pieces[b][:size], a), send(pieces[a][size:], b)
        return {rest[0]: (lower, upper)}

    def whole_piece(x):
        return jnp.concatenate(x, 0) if isinstance(x, tuple) else x

    full_qkv = lax.all_gather(qkv_weight, "fsdp", axis=0, tiled=True)
    fence(
        gains=gather_small(jnp.stack([norm_attn, norm_ffn])),
        hidden=hidden_in.reshape(rows, width),
        grad=cotangent.reshape(rows, width),
        gate_up=gate_up_weight,
        down=down_weight,
        out=out_weight,
    )

    def my_columns(k, at):
        cols = chip ^ (k // 2)
        spots = jnp.stack([cols, cols + chips]).astype(jnp.int32)
        if at is None:
            return pick(live["gate_up"], spots, chip_share)
        if chip_share % 128:
            part = pick(live["gate_up"], spots, chip_share)
            return lax.dynamic_slice_in_dim(part, at * half, half, 0)
        return pick(live["gate_up"], spots, chip_share, rows_at=(at, half))

    def fetched(k):
        return send(my_columns(k, part_at), k)

    def other_half(k, first):
        return neighbour(first) if assisted else send(my_columns(k, 1 - part_at), k)

    firsts = {k: fetched(k) for k in near}
    fence(firsts=firsts, own=my_columns(0, None), d_other=send(live["down"], 1))
    firsts = live.pop("firsts")
    seconds = {k: other_half(k, x) for k, x in firsts.items()}
    inputs = live["hidden"].astype(f32)
    factor_one = norm_factor(inputs)
    gains = live["gains"].astype(f32)
    normed_one = (inputs * factor_one * gains[:1]).astype(bf16)
    firsts |= {k: fetched(k) for k in rest}
    fence(
        firsts=firsts,
        seconds=seconds,
        qkv=full_qkv,
        normed_one=normed_one,
        normed_one_x=pick(normed_one, to_table, block),
    )
    del live["gate_up"]

    joined = dot(live["normed_one"], live["qkv"])
    positions = seq_at * rows + jnp.arange(rows, dtype=jnp.int32)
    cosine, sine = angle_tables(positions)
    cos_wide, sin_wide = jnp.tile(cosine, (1, 2 * KVH)), jnp.tile(sine, (1, 2 * KVH))
    cos_t, sin_t = cosine.T, sine.T
    keys_values = jnp.concatenate(
        [
            turn(joined[:, q_width : q_width + kv_width], cos_wide, sin_wide, 1),
            joined[:, q_width + kv_width :].astype(bf16),
        ],
        1,
    )
    all_kv = lax.all_gather(keys_values, "seq", axis=0, tiled=True)
    outs = {0: live.pop("out")}
    outs |= {k: send(outs[0], k) for k in near}
    fence(joined=joined, kv=all_kv, outs=outs)

    firsts, seconds, outs = live.pop("firsts"), live.pop("seconds"), live.pop("outs")
    seconds |= {k: other_half(k, firsts[k]) for k in rest}
    outs |= two_hops(outs)
    grads = {0: live["grad"]}
    grads |= {k: send(grads[0], k) for k in near}
    info = jnp.concatenate([(seq_at * rows).reshape(1), at_table]).astype(jnp.int32)
    attended, lse = attend(info, live["joined"], live["kv"], cos_t, sin_t)
    fence(firsts=firsts, seconds=seconds, outs=outs, grads=grads, attended=attended, lse=lse)

    outs, grads = live.pop("outs"), live.pop("grads")
    out_even = jnp.concatenate([whole_piece(outs[k]) for k in evens], 0)
    out_odd = send(out_even, 1)
    grads |= two_hops(grads)
    middle = dot(live["attended"][:, : q_width // 2], out_even)
    middle = live["hidden"].astype(f32) + (
        middle + dot(live["attended"][:, q_width // 2 :], out_odd)
    )
    factor_two = norm_factor(middle)
    gain_two = live["gains"][1:].astype(f32)
    normed_two = (middle * factor_two * gain_two).astype(bf16)
    w_own = [live.pop("own")]
    firsts, seconds = live.pop("firsts"), live.pop("seconds")
    for k in evens[1:]:
        w_own += [firsts[k], seconds[k]]
    w_own = jnp.concatenate(w_own, 0)
    w_other = send(w_own, 1)
    fence(
        w_own=w_own,
        w_other=w_other,
        out_even=out_even,
        out_odd=out_odd,
        grads=grads,
        middle=middle,
        tokens={0: normed_two},
    )

    ffn_info = jnp.stack([me, part_at, core, 1 - core]).astype(jnp.int32)

    def ffn_of(group):
        names = ("mixed", "both", "back", "parts")
        weights = [live[k] for k in ("w_own", "w_other", "down", "d_other")]
        results = ffn(
            ffn_info,
            [live["tokens"][k] for k in group],
            [whole_piece(live["grads"][k]) for k in group],
            *weights,
        )
        for name, new in zip(names, results, strict=True):
            live[name] = live.get(name, {}) | dict(zip(group, new, strict=True))

    new = {k: send(live["tokens"][0], k) for k in near}
    ffn_of([0])
    live["tokens"] |= new
    fence()
    new = {k: send(live["tokens"][0], k) for k in rest}
    ffn_of(near)
    live["tokens"] |= new
    fence()
    new = {k: send(live["back"][k], k) for k in near}
    if rest:
        ffn_of(rest)
    fence(returned=new)

    live["returned"] |= {k: send(live["back"][k], k) for k in rest}

    def each(name):
        return [whole_piece(live[name][k]) for k in evens]

    theirs = down_grad(ffn_info, 3, each("mixed"), each("grads"))
    gots = up_grad(after(odd_table, theirs), each("tokens"), each("both"))
    got = send(theirs, 1)
    grad_down = down_grad(after(ffn_info, gots[0]), 2, each("mixed"), each("grads"), got)
    fence(gots=list(gots), zd=grad_down[: share // 2], ze=grad_down[share // 2 :])

    line_step(live, new="d")
    gots = [send(x, 1) for x in live.pop("gots")]
    grad_normed_two = live["back"][0].astype(f32)
    for k in evens[1:]:
        grad_normed_two = grad_normed_two + live["returned"][k].astype(f32)
    middle = live["middle"]
    factor_two = norm_factor(middle)
    gain_two = live["gains"][1:].astype(f32)
    grad_gain_two, grad_norm_two = norm_back(grad_normed_two, middle, factor_two, gain_two)
    grad_middle = live["grad"].astype(f32) + grad_norm_two
    grad_branch = grad_middle.astype(bf16)
    grad_attended = jnp.concatenate(
        [dot_last(grad_branch, live[k]).astype(bf16) for k in ("out_even", "out_odd")], 1
    )
    parts = up_grad(even_table, each("tokens"), each("both"), gots)
    for k in ("tokens", "grads", "both", "mixed", "back", "returned", "w_own", "w_other", "d_other"):
        del live[k]
    del live["out_even"], live["out_odd"], live["down"], live["grad"]
    fence(
        ups=dict(zip(evens, parts, strict=True)),
        grad_gain_two=grad_gain_two,
        grad_middle=grad_middle,
        grad_branch=grad_branch,
        grad_attended=grad_attended,
    )

    names = [str(k) for k in evens]

    def crossed(whole):
        return send(whole[whole.shape[0] // 2 :], 1)

    def blocks(whole, got):
        return {
            k: added(whole[i * block : (i + 1) * block], got[i * block : (i + 1) * block])
            for i, k in enumerate(evens)
        }

    def far_sends(parts):
        if len(rest) != 1:
            return [send(parts[k], k) for k in rest]
        far = parts[rest[0]]
        size = far.shape[0] // 2
        return [send(far[:size], near[0]), send(far[size:], near[1])]

    def near_sends(parts, got):
        if len(rest) != 1:
            return [send(parts[k], k) for k in near]
        size = parts[0].shape[0] // 2
        lower, upper = got
        one, two = parts[near[0]], parts[near[1]]
        one = jnp.concatenate([one[:size], added(one[size:], upper)], 0)
        two = jnp.concatenate([added(two[:size], lower), two[size:]], 0)
        return [send(one, near[0]), send(two, near[1])]

    def total_of(parts, *got):
        total = parts[0].astype(f32)
        for x in sum([g for g in got if g[0].shape == parts[0].shape], []):
            total = total + x.astype(f32)
        return total

    line_step(live, new="e", cross="d")
    sent = {k: send(live["ups"][k], k) for k in near}
    grad_queries, kv_parts = attend_back(
        info, live["joined"], live["kv"], cos_t, sin_t, live["grad_attended"], live["lse"]
    )
    fence(sent=sent, grad_queries=grad_queries, kv_parts=kv_parts)
    for k in ("grad_attended", "joined", "kv", "lse"):
        del live[k]

    ups = live.pop("ups")
    live["z0"] = ups[0]
    for k, x in live.pop("sent").items():
        live[f"z{k}"] = x
    line_step(live, new=names[0], cross="e", out="d")
    sent = {k: send(ups[k], k) for k in rest}
    length = live["kv_parts"].shape[1]
    kv_parts = live.pop("kv_parts").reshape(KVH, length, 2, HD).transpose(1, 2, 0, 3)
    kv_sums = lax.psum_scatter(
        kv_parts.reshape(length, 2 * kv_width), "seq", scatter_dimension=0, tiled=True
    )
    grad_out = dot_first(live.pop("attended"), live.pop("grad_branch")).astype(bf16)
    fence(sent=sent, kv_sums=kv_sums, grad_out=grad_out, got_out=crossed(grad_out))

    for k, x in live.pop("sent").items():
        live[f"z{k}"] = x
    line_step(live, new=names[1], cross=names[0], out="e")
    parts_out = blocks(live.pop("grad_out"), live.pop("got_out"))
    kv_sums = live.pop("kv_sums")
    grad_joined = jnp.concatenate(
        [
            live.pop("grad_queries"),
            turn(kv_sums[:, :kv_width], cos_wide, sin_wide, -1),
            kv_sums[:, kv_width:],
        ],
        1,
    )
    grad_qkv = dot_first(live.pop("normed_one_x"), grad_joined).astype(bf16)
    fence(
        parts_out=parts_out,
        far_out=far_sends(parts_out),
        grad_joined=grad_joined,
        grad_qkv=grad_qkv,
        got_qkv=crossed(grad_qkv),
    )

    gate_up_sums = blank((block, 2 * FF), f32)
    outer = is_outer()

    def summed(k):
        return jnp.where(outer, live.pop("o" + k), live.pop("t" + k)).astype(f32)

    def placed_in(buffer, k):
        cols = chip ^ (k // 2)
        spots = jnp.stack([cols, cols + chips])
        return place(buffer, (live.pop(f"o{k}"), live.pop(f"t{k}")), outer, spots, chip_share)

    line_step(live, new=names[2] if chips > 2 else None, cross=names[1], out=names[0])
    parts_qkv = blocks(live.pop("grad_qkv"), live.pop("got_qkv"))
    fence(
        near_out=near_sends(live["parts_out"], live["far_out"]),
        parts_qkv=parts_qkv,
        down_sums=jnp.concatenate([summed("d"), summed("e")], 0),
    )

    line_step(live, new=names[3] if chips > 3 else None, cross=names[2], out=names[1])
    for k in evens[4:]:
        line_step(live, new=str(k))
    gate_up_sums = placed_in(gate_up_sums, 0)
    zout = total_of(live.pop("parts_out"), live.pop("far_out"), live.pop("near_out"))
    inputs = live["hidden"].astype(f32)
    factor_one = norm_factor(inputs)
    grad_normed_one = dot_last(live.pop("grad_joined"), live.pop("qkv"))
    grad_gain_one, grad_norm_one = norm_back(
        grad_normed_one, inputs, factor_one, live["gains"][:1].astype(f32)
    )
    grad_input = (live["grad_middle"] + grad_norm_one).astype(bf16)
    fence(
        far_qkv=far_sends(live["parts_qkv"]),
        zout=zout.astype(bf16),
        grad_input=grad_input,
        grad_gains=jnp.stack([grad_gain_one, live.pop("grad_gain_two")]),
        sums=gate_up_sums,
    )

    line_step(live, new="out", cross=names[3], out=names[2])
    gate_up_sums = placed_in(live.pop("sums"), evens[1])
    fence(near_qkv=near_sends(live["parts_qkv"], live["far_qkv"]), sums=gate_up_sums)

    total = total_of(live.pop("parts_qkv"), live.pop("far_qkv"), live.pop("near_qkv")).astype(bf16)
    live["zq"], live["zr"] = total[:half], total[half:]
    line_step(live, new="q", cross="out", out=names[3])
    gate_up_sums = placed_in(live.pop("sums"), evens[2])
    fence(far=far_sends(live["parts"]), sums=gate_up_sums)

    line_step(live, new="r", cross="q", out="out")
    gate_up_sums = live.pop("sums")
    for k in evens[3:]:
        gate_up_sums = placed_in(gate_up_sums, k)
    fence(near=near_sends(live["parts"], live["far"]), sums=gate_up_sums)

    line_step(live, cross="r", out="q")
    out_sums = summed("out")
    grad_gains = small_sum(live.pop("grad_gains"))
    out = total_of(live.pop("parts"), live.pop("far"), live.pop("near"))
    out = (live["middle"] + out).astype(bf16)
    fence(grad_gains=grad_gains, out_final=out, out_sums=out_sums)

    line_step(live, out="r")
    qkv_sums = jnp.concatenate([summed("q"), summed("r")], 0)
    grad_gains = lax.dynamic_slice_in_dim(live["grad_gains"], me * block, block, 1)
    return (
        live["out_final"].reshape(hidden_in.shape),
        live["grad_input"].reshape(hidden_in.shape),
        grad_gains[0],
        qkv_sums,
        live["out_sums"],
        grad_gains[1],
        live["sums"],
        live["down_sums"],
    )


def solution(mesh):
    placed = (
        P("fsdp", "seq", None),
        P("fsdp"),
        P("fsdp", None),
        P("fsdp", None),
        P("fsdp"),
        P("fsdp", None),
        P("fsdp", None),
        P("fsdp", "seq", None),
    )
    return jax.shard_map(
        on_device,
        mesh=mesh,
        in_specs=placed,
        out_specs=(
            P("fsdp", "seq", None),
            P("fsdp", "seq", None),
            P("fsdp"),
            P("fsdp", None),
            P("fsdp", None),
            P("fsdp"),
            P("fsdp", None),
            P("fsdp", None),
        ),
        check_vma=False,
    )
```

time: 1240 us -> 798 us (0.64)
  waiting for transfers between devices: 589 us -> 244 us
  Pallas kernels: 72.4 us -> 220 us
  local copies, waits for them, and re-layouts: 143 us -> 55.2 us
  matrix products: 107 us -> 25.9 us
  blocking collectives: 65 us -> 0 us
    ppermute x42 -> x33, waiting for transfers between devices: 331 us -> 108 us  [the longest x7 49.5 us: line_step(): live['i' + new] = lax.ppermute(x, 'seq', inward)]
    pallas_call x2 -> x19, Pallas kernels: 58.7 us -> 216 us  [the longest x3 76.6 us: ffn(): pl.pallas_call(functools.partial(ffn_kernel, n, count), out_shape=shapes,...]
    ppermute x66 -> x45, waiting for transfers between devices: 220 us -> 124 us  [send(): return lax.ppermute(x, 'fsdp', [(i, i ^ k) for i in range(n)])]
    all_gather x1 -> x0, blocking collectives: 41.3 us -> none  [on_device(): lax.all_gather(jnp.stack([norm_attn, norm_ffn]), 'fsdp', axis=1, tiled=True)]
    unnamed x209 -> x239, local copies, waits for them, and re-layouts: 66.2 us -> 30.9 us
    dot_general x5 -> x3, matrix products: 37.6 us -> 8.36 us  [dot(): return jnp.dot(one, two, preferred_element_type=f32)]
    dot_general x4 -> x3, matrix products: 38.4 us -> 11 us  [dot_last(): return lax.dot_general(one, two, contract_last, preferred_element_type=f32)]
    unnamed x4 -> x3, waiting for transfers between devices: 26 us -> 0.71 us
  transfers between devices with their start and end apart: 111 -> 81, of which waited for: 41 -> 36; matrix products, arithmetic and copies ran while one was open for 22% -> 15% of each run, Pallas kernels for 6% -> 27%
where the time goes in v2:
time: 798 us; the launch traced here: 791 us
  waiting for transfers between devices  244 us (31%)
  Pallas kernels  220 us (28%)
  starting transfers between devices  131 us (16%)
  other arithmetic  98.4 us (12%)
  local copies, waits for them, and re-layouts  55.2 us (7%)
  matrix products  25.9 us (3%)
  between operations  16 us (2%)
    ppermute x45, waiting for transfers between devices, send(): return lax.ppermute(x, 'fsdp', [(i, i ^ k) for i in range(n)])  124 us
    pallas_call x3, Pallas kernels, ffn(): pl.pallas_call(functools.partial(ffn_kernel, n, count), out_shape=shapes,...  76.6 us
    ppermute x7, waiting for transfers between devices, line_step(): live['i' + new] = lax.ppermute(x, 'seq', inward)  49.5 us
    ppermute x45, starting transfers between devices, send(): return lax.ppermute(x, 'fsdp', [(i, i ^ k) for i in range(n)])  46.2 us
    convert_element_type x24, other arithmetic, added(): return (one.astype(f32) + two.astype(f32)).astype(bf16)  45.2 us
    ppermute x7, starting transfers between devices, line_step(): live['i' + new] = lax.ppermute(x, 'seq', inward)  40.6 us
    pallas_call x1, Pallas kernels, attend_back(): pl.pallas_call(functools.partial(attend_back_kernel, heads, per_kv), out_...  35.8 us
    ppermute x7, waiting for transfers between devices, line_step(): live['o' + out] = lax.ppermute(total, 'seq', outward)  34.8 us
  transfers between devices with their start and end apart: 81, of which 36 were waited for; matrix products, arithmetic and copies ran while one was open for 15% of the time, Pallas kernels for 27%

profile of v2, /device:TPU:0, one launch (start us, length us, event | category | flops | bytes accessed | tf_op | source)
XLA Modules:
  0.0 790.9 jit_solution(8053113201622199565)
XLA Ops:
  36.0 16.9 %collective-permute-done.4 = bf16[128,2816]{1,0:T(8,128)(2,1)S(1)} collective-permute-done((bf16[128,2816]{1,0:T(8,128)(2,1)}, bf16[128,2816]{1,0:T(8,128)(2,1)S(1)}, u32[]{:S(2)}, u32[]{:S(2)}) %collective-permute-start.4) | collective-permute-done | bytes 720928 | tf_op jit(solution)/shard_map/ppermute | solution.py:26
  67.2 24.3 %collective-permute-done.6 = bf16[128,2816]{1,0:T(8,128)(2,1)} collective-permute-done((bf16[128,2816]{1,0:T(8,128)(2,1)}, bf16[128,2816]{1,0:T(8,128)(2,1)}, u32[]{:S(2)}, u32[]{:S(2)}) %collective-permute-start.6) | collective-permute-done | bytes 720928 | tf_op jit(solution)/shard_map/ppermute | solution.py:26
  91.5 10.1 %all-gather.3.cloned.1.call-done = bf16[2048,2560]{1,0:T(8,128)(2,1)} async-done(((bf16[256,2560]{1,0:T(8,128)(2,1)}), bf16[2048,2560]{1,0:T(8,128)(2,1)}) %all-gather.3.cloned.1.call-update) | async-done | bytes 10485776 | tf_op jit(solution)/shard_map/all_gather | solution.py:703
  115.9 22.8 %collective-permute-done.9 = bf16[256,2048]{1,0:T(8,128)(2,1)S(1)} collective-permute-done((bf16[256,2048]{1,0:T(8,128)(2,1)}, bf16[256,2048]{1,0:T(8,128)(2,1)S(1)}, u32[]{:S(2)}, u32[]{:S(2)}) %collective-permute-start.9) | collective-permute-done | bytes 1048608 | tf_op jit(solution)/shard_map/ppermute | solution.py:26
  150.0 30.1 %shard_map.167 = (bf16[256,2048]{1,0:T(8,128)(2,1)S(1)}, f32[8,4,256]{2,1,0:T(4,128)S(1)}) custom-call(s32[9]{0:T(128)S(1)} %pad_add_fusion.info_ref, f32[256,2560]{1,0:T(8,128)S(1)} %copy-done.16, bf16[1024,512]{1,0:T(8,128)(2,1)S(1)} %copy-done.24, bf16[1024,512]{1,0:T(8,128)(2,1)S(1)} %copy-done.24, f32[32,256]{1,0:T(8,128)S(1)} %get-tuple-element.983.cos_ref, ...), custom_call_target="tpu_custom_call" | custom-call | flops 8589934592 | bytes 3145728 | tf_op jit(solution)/shard_map/pallas_call | solution.py:273
  208.6 21.5 %shard_map.168 = (bf16[1408,256]{1,0:T(8,128)(2,1)}, bf16[256,2816]{1,0:T(8,128)(2,1)}, bf16[256,2048]{1,0:T(8,128)(2,1)}, bf16[256,2048]{1,0:T(8,128)(2,1)}) custom-call(s32[4]{0:T(128)} %pad_add_fusion.3.info_ref, bf16[256,2048]{1,0:T(8,128)(2,1)} %copy-done.8, bf16[256,2048]{1,0:T(8,128)(2,1)} %bitcast.47, bf16[1024,2816]{1,0:T(8,128)(2,1)} %copy-done.91, ...), custom_call_target="tpu_custom_call" | custom-call | flops 8858370048 | bytes 17301504 | tf_op jit(solution)/shard_map/pallas_call | solution.py:474
  232.6 33.4 %shard_map.169 = (bf16[1408,256]{1,0:T(8,128)(2,1)}, bf16[1408,256]{1,0:T(8,128)(2,1)}, bf16[256,2816]{1,0:T(8,128)(2,1)}, bf16[256,2816]{1,0:T(8,128)(2,1)}, bf...) custom-call(s32[4]{0:T(128)} %pad_add_fusion.3.info_ref, ...), custom_call_target="tpu_custom_call" | custom-call | flops 17716740096 | bytes 17301504 | tf_op jit(solution)/shard_map/pallas_call | solution.py:474
  269.1 21.7 %shard_map.170 = (bf16[1408,256]{1,0:T(8,128)(2,1)}, bf16[256,2816]{1,0:T(8,128)(2,1)}, bf16[256,2048]{1,0:T(8,128)(2,1)}, bf16[256,2048]{1,0:T(8,128)(2,1)}) custom-call(s32[4]{0:T(128)} %pad_add_fusion.3.info_ref, bf16[256,2048]{1,0:T(8,128)(2,1)} %copy-done.32, bf16[256,2048]{1,0:T(8,128)(2,1)} %pad_maximum_fusion.3.refs_1_, ...), custom_call_target="tpu_custom_call" | custom-call | flops 8858370048 | bytes 17301504 | tf_op jit(solution)/shard_map/pallas_call | solution.py:474
  303.2 14.4 %shard_map.172 = (bf16[256,2816]{1,0:T(8,128)(2,1)S(1)}, bf16[256,2816]{1,0:T(8,128)(2,1)}, bf16[256,2816]{1,0:T(8,128)(2,1)}, bf16[256,2816]{1,0:T(8,128)(2,1)}) custom-call(s32[4]{0:T(128)S(1)} %get-tuple-element.677.info_ref, bf16[256,2048]{1,0:T(8,128)(2,1)S(1)} %copy-done.9, bf16[256,2048]{1,0:T(8,128)(2,1)S(1)} %copy-done.27, ...), custom_call_target="tpu_custom_call" | custom-call | flops 5905580032 | bytes 11534336 | tf_op jit(solution)/shard_map/pallas_call | solution.py:605
  345.8 16.6 %shard_map.174 = (bf16[256,2816]{1,0:T(8,128)(2,1)S(1)}, bf16[256,2816]{1,0:T(8,128)(2,1)}, bf16[256,2816]{1,0:T(8,128)(2,1)}, bf16[256,2816]{1,0:T(8,128)(2,1)}) custom-call(s32[4]{0:T(128)S(1)} %get-tuple-element.990.info_ref, bf16[256,2048]{1,0:T(8,128)(2,1)S(1)} %copy-done.9, bf16[256,2048]{1,0:T(8,128)(2,1)S(1)} %copy-done.28, ...), custom_call_target="tpu_custom_call" | custom-call | flops 5905580032 | bytes 11534336 | tf_op jit(solution)/shard_map/pallas_call | solution.py:605
  373.8 35.8 %shard_map.175 = (bf16[256,2048]{1,0:T(8,128)(2,1)S(1)}, bf16[4,1024,128]{2,1,0:T(8,128)(2,1)S(1)}) custom-call(s32[9]{0:T(128)S(1)} %pad_add_fusion.info_ref, f32[256,2560]{1,0:T(8,128)} %copy-done.15, bf16[1024,512]{1,0:T(8,128)(2,1)S(1)} %copy-done.25, bf16[1024,512]{1,0:T(8,128)(2,1)S(1)} %copy-done.25, bf16[256,2048]{1,0:T(8,128)(2,1)S(1)} %pad_maximum_fusion.4.g_ref, ...), custom_call_target="tpu_custom_call" | custom-call | flops 21474836480 | bytes 4194304 | tf_op jit(solution)/shard_map/pallas_call | solution.py:350
  434.4 35.3 %collective-permute-done.37 = bf16[256,2816]{1,0:T(8,128)(2,1)} collective-permute-done((bf16[256,2816]{1,0:T(8,128)(2,1)S(1)}, bf16[256,2816]{1,0:T(8,128)(2,1)}, u32[]{:S(2)}, u32[]{:S(2)}) %collective-permute-start.37) | collective-permute-done | bytes 1441824 | tf_op jit(solution)/shard_map/ppermute | solution.py:97
  469.7 11.1 %collective-permute-done.38 = bf16[352,2048]{1,0:T(8,128)(2,1)S(1)} collective-permute-done((bf16[352,2048]{1,0:T(8,128)(2,1)S(1)}, bf16[352,2048]{1,0:T(8,128)(2,1)S(1)}, u32[]{:S(2)}, u32[]{:S(2)}) %collective-permute-start.38) | collective-permute-done | bytes 1441824 | tf_op jit(solution)/shard_map/ppermute | solution.py:99
  516.2 12.8 %collective-permute-done.41 = bf16[128,2048]{1,0:T(8,128)(2,1)S(1)} collective-permute-done((bf16[128,2048]{1,0:T(8,128)(2,1)S(1)}, bf16[128,2048]{1,0:T(8,128)(2,1)S(1)}, u32[]{:S(2)}, u32[]{:S(2)}) %collective-permute-start.41) | collective-permute-done | bytes 524320 | tf_op jit(solution)/shard_map/ppermute | solution.py:26
  532.1 10.5 %collective-permute-done.42 = bf16[128,2048]{1,0:T(8,128)(2,1)} collective-permute-done((bf16[128,2048]{1,0:T(8,128)(2,1)}, bf16[128,2048]{1,0:T(8,128)(2,1)}, u32[]{:S(2)}, u32[]{:S(2)}) %collective-permute-start.42) | collective-permute-done | bytes 524320 | tf_op jit(solution)/shard_map/ppermute | solution.py:26
  567.1 8.3 %collective-permute-done.48 = bf16[256,2048]{1,0:T(8,128)(2,1)S(1)} collective-permute-done((bf16[256,2048]{1,0:T(8,128)(2,1)S(1)}, bf16[256,2048]{1,0:T(8,128)(2,1)S(1)}, u32[]{:S(2)}, u32[]{:S(2)}) %collective-permute-start.48) | collective-permute-done | bytes 1048608 | tf_op jit(solution)/shard_map/ppermute | solution.py:26
  588.6 7.6 collective-permute-start.53
  599.4 8.4 %fusion.10 = (f32[256]{0:T(256)S(1)}, f32[2048]{0:T(1024)S(1)}, f32[256,2048]{1,0:T(8,128)}) fusion(bf16[256,2048]{1,0:T(8,128)(2,1)S(1)} %bitcast.60, f32[2048]{0:T(1024)S(1)} %bitcast.70, f32[256]{0:T(256)S(1)} %get-tuple-element.987, bf16[256,2560]{1,0:T(8,128)(2,1)S(1)} %pad_maximum_fusion, bf16[2048,2560]{1,0:T(8,128)(2,1)} %all-gather.3.cloned.1.call-done), kind=kOutput, calls=%fused_computation.38 | convolution fusion | flops 2688022272 | bytes 14960640 | tf_op jit(solution)/shard_map/dot_general | solution.py:650
  616.5 8.7 %collective-permute-done.53.got_ref = bf16[256,2816]{1,0:T(8,128)(2,1)} collective-permute-done((bf16[256,2816]{1,0:T(8,128)(2,1)}, bf16[256,2816]{1,0:T(8,128)(2,1)}, u32[]{:S(2)}, u32[]{:S(2)}) %collective-permute-start.53) | collective-permute-done | bytes 1441824 | tf_op jit(solution)/shard_map/ppermute | solution.py:93
  640.5 9.6 %collective-permute-start.55 = (bf16[256,2048]{1,0:T(8,128)(2,1)}, bf16[256,2048]{1,0:T(8,128)(2,1)}, u32[]{:S(2)}, u32[]{:S(2)}) collective-permute-start(bf16[256,2048]{1,0:T(8,128)(2,1)} %add_convert_fusion.20), channel_id=1, source_target_pairs={{0,1},{3,2},{4,5},{7,6},{8,9},{11,10},{12,13},{15,14},{16,17},{19,... | collective-permute-start | bytes 3145736 | tf_op jit(solution)/shard_map/ppermute | solution.py:97
  654.4 12.9 %collective-permute-done.55 = bf16[256,2048]{1,0:T(8,128)(2,1)} collective-permute-done((bf16[256,2048]{1,0:T(8,128)(2,1)}, bf16[256,2048]{1,0:T(8,128)(2,1)}, u32[]{:S(2)}, u32[]{:S(2)}) %collective-permute-start.55) | collective-permute-done | bytes 1048608 | tf_op jit(solution)/shard_map/ppermute | solution.py:97
  677.3 11.4 %collective-permute-start.62 = (bf16[128,2560]{1,0:T(8,128)(2,1)S(1)}, bf16[128,2560]{1,0:T(8,128)(2,1)}, u32[]{:S(2)}, u32[]{:S(2)}) collective-permute-start(bf16[128,2560]{1,0:T(8,128)(2,1)S(1)} %get-tuple-element.920), channel_id=1, source_target_pairs={{0,1},{3,2},{4,5},{7,6},{8,9},{11,10},{12,13},{15,14},{16,17},{19,... | collective-permute-start | bytes 1966088 | tf_op jit(solution)/shard_map/ppermute | solution.py:97
  752.7 6.4 collective-permute-done.73
  767.5 14.6 %collective-permute-done.77 = bf16[128,2560]{1,0:T(8,128)(2,1)S(1)} collective-permute-done((bf16[128,2560]{1,0:T(8,128)(2,1)S(1)}, bf16[128,2560]{1,0:T(8,128)(2,1)S(1)}, u32[]{:S(2)}, u32[]{:S(2)}) %collective-permute-start.77) | collective-permute-done | bytes 655392 | tf_op jit(solution)/shard_map/ppermute | solution.py:99
  (536 shorter events, 369.6 us)
Async XLA Ops:
  7.2 94.4 %all-gather.3.cloned.1.call-start = ((), (), s32[]{:S(2)}) async-start(), calls=%async_computation.1 | async-start | bytes 11796480 | tf_op jit(solution)/shard_map/all_gather | solution.py:703
  7.9 133.2 %all-gather.5.cloned.1.call-start = ((), (), s32[]{:S(2)}) async-start(), calls=%async_computation.2 | async-start | bytes 1310720 | tf_op jit(solution)/shard_map/all_gather | solution.py:759
  56.2 35.3 %collective-permute-start.6 = (bf16[128,2816]{1,0:T(8,128)(2,1)}, bf16[128,2816]{1,0:T(8,128)(2,1)}, u32[]{:S(2)}, u32[]{:S(2)}) collective-permute-start(bf16[128,2816]{1,0:T(8,128)(2,1)} %shard_map.164), channel_id=1, source_target_pairs={{0,24},{4,28},{8,16},{12,20},{16,8},{20,12},{24,0},{28,4},{1,25},{... | collective-permute-start | bytes 2162696 | tf_op jit(solution)/shard_map/ppermute | solution.py:26
  113.1 368.9 %reduce-scatter.2.cloned.1.call-start = ((), (), s32[]{:S(2)}) async-start(), calls=%async_computation.3 | async-start | bytes 1310720 | tf_op jit(solution)/shard_map/reduce_scatter | solution.py:915
  141.2 39.0 %collective-permute-start.11 = (bf16[256,2048]{1,0:T(8,128)(2,1)S(1)}, bf16[256,2048]{1,0:T(8,128)(2,1)S(1)}, u32[]{:S(2)}, u32[]{:S(2)}) collective-permute-start(bf16[256,2048]{1,0:T(8,128)(2,1)S(1)} %bitcast.48), channel_id=1, source_target_pairs={{0,8},{4,12},{8,0},{12,4},{16,24},{20,28},{24,16},{28,20},{1,9},{5... | collective-permute-start | bytes 3145736 | tf_op jit(solution)/shard_map/ppermute | solution.py:26
  142.6 37.6 %collective-permute-start.12 = (bf16[256,2048]{1,0:T(8,128)(2,1)S(1)}, bf16[256,2048]{1,0:T(8,128)(2,1)S(1)}, u32[]{:S(2)}, u32[]{:S(2)}) collective-permute-start(bf16[256,2048]{1,0:T(8,128)(2,1)S(1)} %bitcast.49), channel_id=1, source_target_pairs={{0,16},{4,20},{8,24},{12,28},{16,0},{20,4},{24,8},{28,12},{1,17},{... | collective-permute-start | bytes 3145736 | tf_op jit(solution)/shard_map/ppermute | solution.py:26
  231.0 35.0 %collective-permute-start.22 = (bf16[256,2048]{1,0:T(8,128)(2,1)}, bf16[256,2048]{1,0:T(8,128)(2,1)S(1)}, u32[]{:S(2)}, u32[]{:S(2)}) collective-permute-start(bf16[256,2048]{1,0:T(8,128)(2,1)} %copy-done.8), channel_id=1, source_target_pairs={{0,24},{4,28},{8,16},{12,20},{16,8},{20,12},{24,0},{28,4},{1,25},{... | collective-permute-start | bytes 3145736 | tf_op jit(solution)/shard_map/ppermute | solution.py:26
  363.7 45.9 %collective-permute-start.32 = (bf16[352,2048]{1,0:T(8,128)(2,1)S(1)}, bf16[352,2048]{1,0:T(8,128)(2,1)S(1)}, u32[]{:S(2)}, u32[]{:S(2)}) collective-permute-start(bf16[352,2048]{1,0:T(8,128)(2,1)S(1)} %get-tuple-element.785), channel_id=1, source_target_pairs={{0,1},{3,2},{4,5},{7,6},{8,9},{11,10},{12,13},{15,14},{16,17},{19,... | collective-permute-start | bytes 4325384 | tf_op jit(solution)/shard_map/ppermute | solution.py:97
  368.4 41.2 %collective-permute-start.33 = (bf16[256,2816]{1,0:T(8,128)(2,1)}, bf16[256,2816]{1,0:T(8,128)(2,1)}, u32[]{:S(2)}, u32[]{:S(2)}) collective-permute-start(bf16[256,2816]{1,0:T(8,128)(2,1)} %get-tuple-element.763), channel_id=1, source_target_pairs={{0,8},{4,12},{8,0},{12,4},{16,24},{20,28},{24,16},{28,20},{1,9},{5... | collective-permute-start | bytes 4325384 | tf_op jit(solution)/shard_map/ppermute | solution.py:26
  369.7 40.0 %collective-permute-start.34 = (bf16[256,2816]{1,0:T(8,128)(2,1)}, bf16[256,2816]{1,0:T(8,128)(2,1)S(1)}, u32[]{:S(2)}, u32[]{:S(2)}) collective-permute-start(bf16[256,2816]{1,0:T(8,128)(2,1)} %get-tuple-element.764), channel_id=1, source_target_pairs={{0,16},{4,20},{8,24},{12,28},{16,0},{20,4},{24,8},{28,12},{1,17},{... | collective-permute-start | bytes 4325384 | tf_op jit(solution)/shard_map/ppermute | solution.py:26
  372.7 37.0 %collective-permute-start.35 = (bf16[352,2048]{1,0:T(8,128)(2,1)S(1)}, bf16[352,2048]{1,0:T(8,128)(2,1)S(1)}, u32[]{:S(2)}, u32[]{:S(2)}) collective-permute-start(bf16[352,2048]{1,0:T(8,128)(2,1)S(1)} %add_convert_fusion.11), channel_id=1, source_target_pairs={{1,2},{2,1},{5,6},{6,5},{9,10},{10,9},{13,14},{14,13},{17,18},{18,... | collective-permute-start | bytes 4325384 | tf_op jit(solution)/shard_map/ppermute | solution.py:102
  417.9 64.1 %collective-permute-start.36 = (bf16[1024,2048]{1,0:T(8,128)(2,1)}, bf16[1024,2048]{1,0:T(8,128)(2,1)}, u32[]{:S(2)}, u32[]{:S(2)}) collective-permute-start(bf16[1024,2048]{1,0:T(8,128)(2,1)} %slice.240), channel_id=1, source_target_pairs={{0,4},{4,0},{8,12},{12,8},{16,20},{20,16},{24,28},{28,24},{1,5},{5... | collective-permute-start | bytes 12582920 | tf_op jit(solution)/shard_map/ppermute | solution.py:26
  417.9 51.8 %collective-permute-start.37 = (bf16[256,2816]{1,0:T(8,128)(2,1)S(1)}, bf16[256,2816]{1,0:T(8,128)(2,1)}, u32[]{:S(2)}, u32[]{:S(2)}) collective-permute-start(bf16[256,2816]{1,0:T(8,128)(2,1)S(1)} %get-tuple-element.805), channel_id=1, source_target_pairs={{0,1},{3,2},{4,5},{7,6},{8,9},{11,10},{12,13},{15,14},{16,17},{19,... | collective-permute-start | bytes 4325384 | tf_op jit(solution)/shard_map/ppermute | solution.py:97
  428.9 51.9 %collective-permute-start.38 = (bf16[352,2048]{1,0:T(8,128)(2,1)S(1)}, bf16[352,2048]{1,0:T(8,128)(2,1)S(1)}, u32[]{:S(2)}, u32[]{:S(2)}) collective-permute-start(bf16[352,2048]{1,0:T(8,128)(2,1)S(1)} %add_convert_fusion.10), channel_id=1, source_target_pairs={{1,0},{2,3},{5,4},{6,7},{9,8},{10,11},{13,12},{14,15},{17,16},{18,... | collective-permute-start | bytes 4325384 | tf_op jit(solution)/shard_map/ppermute | solution.py:99
  430.5 51.4 %collective-permute-start.39 = (bf16[256,2816]{1,0:T(8,128)(2,1)S(1)}, bf16[256,2816]{1,0:T(8,128)(2,1)}, u32[]{:S(2)}, u32[]{:S(2)}) collective-permute-start(bf16[256,2816]{1,0:T(8,128)(2,1)S(1)} %copy-done.102), channel_id=1, source_target_pairs={{0,24},{4,28},{8,16},{12,20},{16,8},{20,12},{24,0},{28,4},{1,25},{... | collective-permute-start | bytes 4325384 | tf_op jit(solution)/shard_map/ppermute | solution.py:26
  432.6 49.4 %collective-permute-start.40 = (bf16[352,2048]{1,0:T(8,128)(2,1)S(1)}, bf16[352,2048]{1,0:T(8,128)(2,1)}, u32[]{:S(2)}, u32[]{:S(2)}) collective-permute-start(bf16[352,2048]{1,0:T(8,128)(2,1)S(1)} %add_convert_fusion.9), channel_id=1, source_target_pairs={{1,2},{2,1},{5,6},{6,5},{9,10},{10,9},{13,14},{14,13},{17,18},{18,... | collective-permute-start | bytes 4325384 | tf_op jit(solution)/shard_map/ppermute | solution.py:102
  495.3 47.3 %collective-permute-start.43 = (bf16[1024,2560]{1,0:T(8,128)(2,1)}, bf16[1024,2560]{1,0:T(8,128)(2,1)}, u32[]{:S(2)}, u32[]{:S(2)}) collective-permute-start(bf16[1024,2560]{1,0:T(8,128)(2,1)} %slice.243), channel_id=1, source_target_pairs={{0,4},{4,0},{8,12},{12,8},{16,20},{20,16},{24,28},{28,24},{1,5},{5... | collective-permute-start | bytes 15728648 | tf_op jit(solution)/shard_map/ppermute | solution.py:26
  495.3 47.3 %collective-permute-start.44 = (bf16[256,2816]{1,0:T(8,128)(2,1)}, bf16[256,2816]{1,0:T(8,128)(2,1)}, u32[]{:S(2)}, u32[]{:S(2)}) collective-permute-start(bf16[256,2816]{1,0:T(8,128)(2,1)} %collective-permute-done.33), channel_id=1, source_target_pairs={{0,1},{3,2},{4,5},{7,6},{8,9},{11,10},{12,13},{15,14},{16,17},{19,... | collective-permute-start | bytes 4325384 | tf_op jit(solution)/shard_map/ppermute | solution.py:97
  502.7 39.9 %collective-permute-start.45 = (bf16[352,2048]{1,0:T(8,128)(2,1)}, bf16[352,2048]{1,0:T(8,128)(2,1)}, u32[]{:S(2)}, u32[]{:S(2)}) collective-permute-start(bf16[352,2048]{1,0:T(8,128)(2,1)} %add_convert_fusion.8), channel_id=1, source_target_pairs={{1,0},{2,3},{5,4},{6,7},{9,8},{10,11},{13,12},{14,15},{17,16},{18,... | collective-permute-start | bytes 4325384 | tf_op jit(solution)/shard_map/ppermute | solution.py:99
  507.1 35.5 %collective-permute-start.46 = (bf16[256,2816]{1,0:T(8,128)(2,1)}, bf16[256,2816]{1,0:T(8,128)(2,1)}, u32[]{:S(2)}, u32[]{:S(2)}) collective-permute-start(bf16[256,2816]{1,0:T(8,128)(2,1)} %add_convert_fusion.7), channel_id=1, source_target_pairs={{1,2},{2,1},{5,6},{6,5},{9,10},{10,9},{13,14},{14,13},{17,18},{18,... | collective-permute-start | bytes 4325384 | tf_op jit(solution)/shard_map/ppermute | solution.py:102
  546.2 34.7 %collective-permute-start.47 = (bf16[256,2816]{1,0:T(8,128)(2,1)S(1)}, bf16[256,2816]{1,0:T(8,128)(2,1)S(1)}, u32[]{:S(2)}, u32[]{:S(2)}) collective-permute-start(bf16[256,2816]{1,0:T(8,128)(2,1)S(1)} %get-tuple-element.954), channel_id=1, source_target_pairs={{0,1},{3,2},{1,0},{2,3},{4,5},{7,6},{5,4},{6,7},{8,9},{11,10},{9,8... | collective-permute-start | bytes 4325384 | tf_op jit(solution)/shard_map/ppermute | solution.py:93
  588.6 36.6 %collective-permute-start.53 = (bf16[256,2816]{1,0:T(8,128)(2,1)}, bf16[256,2816]{1,0:T(8,128)(2,1)}, u32[]{:S(2)}, u32[]{:S(2)}) collective-permute-start(bf16[256,2816]{1,0:T(8,128)(2,1)} %get-tuple-element.952), channel_id=1, source_target_pairs={{0,1},{3,2},{1,0},{2,3},{4,5},{7,6},{5,4},{6,7},{8,9},{11,10},{9,8... | collective-permute-start | bytes 4325384 | tf_op jit(solution)/shard_map/ppermute | solution.py:93
  627.8 39.5 %collective-permute-start.56 = (bf16[256,2560]{1,0:T(8,128)(2,1)}, bf16[256,2560]{1,0:T(8,128)(2,1)}, u32[]{:S(2)}, u32[]{:S(2)}) collective-permute-start(bf16[256,2560]{1,0:T(8,128)(2,1)} %pad_maximum_fusion.1), channel_id=1, source_target_pairs={{0,8},{4,12},{8,0},{12,4},{16,24},{20,28},{24,16},{28,20},{1,9},{5... | collective-permute-start | bytes 3932168 | tf_op jit(solution)/shard_map/ppermute | solution.py:26
  669.0 35.4 %collective-permute-start.63 = (bf16[256,2816]{1,0:T(8,128)(2,1)S(1)}, bf16[256,2816]{1,0:T(8,128)(2,1)}, u32[]{:S(2)}, u32[]{:S(2)}) collective-permute-start(bf16[256,2816]{1,0:T(8,128)(2,1)S(1)} %add_convert_fusion.total_ref), channel_id=1, source_target_pairs={{1,0},{2,3},{5,4},{6,7},{9,8},{10,11},{13,12},{14,15},{17,16},{18,... | collective-permute-start | bytes 4325384 | tf_op jit(solution)/shard_map/ppermute | solution.py:99
  (171 other events, 2325.9 us)
Sparse Core Ops, SparseCore 0:
  9.9 91.6 all-gather.2
  113.2 27.9 all-gather.4
  426.5 41.7 reduce-scatter.1

commit v3 on v2

--- a/solution.py
+++ b/solution.py
@@ -84,22 +84,21 @@
             live["o" + new] = live["t" + new] = line_sum(live["z" + new])
         return
     inward, outward, across = [(0, 1), (3, 2)], [(1, 0), (2, 3)], [(1, 2), (2, 1)]
-    x = total = None
-    if out is not None:
-        total = live["t" + out] = added(live["p" + out], live["x" + out])
-    if new is not None:
-        x = live["z" + new]
-    if x is not None and total is not None and x.shape == total.shape:
-        got = lax.ppermute(jnp.where(is_outer(), x, total), "seq", inward + outward)
-        live["i" + new] = live["o" + out] = got
-    else:
-        if x is not None:
-            live["i" + new] = lax.ppermute(x, "seq", inward)
-        if total is not None:
-            live["o" + out] = lax.ppermute(total, "seq", outward)
+    x = None if new is None else live["z" + new]
+    part = None
     if cross is not None:
         part = live["p" + cross] = added(live["z" + cross], live["i" + cross])
         live["x" + cross] = lax.ppermute(part, "seq", across)
+        if x is not None:
+            x = after(x, part)
+    if x is not None:
+        live["i" + new] = lax.ppermute(x, "seq", inward)
+    if out is not None:
+        old = live["p" + out]
+        if part is not None:
+            old = after(old, part)
+        total = live["t" + out] = added(old, live["x" + out])
+        live["o" + out] = lax.ppermute(total, "seq", outward)
 
 
 def is_outer():
@@ -107,14 +106,12 @@
     return (me == 0) | (me == n - 1)
 
 
-def small_sum(x):
-    for axis in ("fsdp", "seq"):
-        n = lax.axis_size(axis)
-        if n & (n - 1):
-            x = lax.psum(x, axis)
-            continue
-        for k in (1 << i for i in range(n.bit_length() - 1)):
-            x = x + lax.ppermute(x, axis, [(i, i ^ k) for i in range(n)])
+def small_sum(x, axis):
+    n = lax.axis_size(axis)
+    if n & (n - 1):
+        return lax.psum(x, axis)
+    for k in (1 << i for i in range(n.bit_length() - 1)):
+        x = x + lax.ppermute(x, axis, [(i, i ^ k) for i in range(n)])
     return x
 
 
@@ -338,7 +335,7 @@
 
     @pl.when(step % steps == steps - 1)
     def _():
-        dkv_ref[0] = jnp.concatenate([dk * scale, dv], 1).astype(bf16)
+        dkv_ref[...] = jnp.concatenate([dk * scale, dv], 1).astype(bf16)
 
 
 def attend_back(info, joined, all_kv, cos_t, sin_t, grads, lse):
@@ -351,7 +348,7 @@
         functools.partial(attend_back_kernel, heads, per_kv),
         out_shape=(
             jax.ShapeDtypeStruct((rows, HEADS * HD), bf16),
-            jax.ShapeDtypeStruct((KVH, length, 2 * HD), bf16),
+            jax.ShapeDtypeStruct((length, 2 * KVH * HD), bf16),
         ),
         grid_spec=pltpu.PrefetchScalarGridSpec(
             num_scalar_prefetch=1,
@@ -359,7 +356,7 @@
             in_specs=[spec[k] for k in names],
             out_specs=(
                 spec["plain"],
-                pl.BlockSpec((1, length, 2 * HD), lambda i, info: (i * heads // per_kv, 0, 0)),
+                pl.BlockSpec((length, 2 * HD), lambda i, info: (0, i * heads // per_kv)),
             ),
             scratch_shapes=[
                 pltpu.VMEM((length, rows), f32),
@@ -380,10 +377,15 @@
     return [(c, min(size, total - c)) for c in range(0, total, size)]
 
 
+def part_pieces(n):
+    evens = list(range(0, n, 2))
+    return evens[:3], evens[3:], [k | 1 for k in evens[:3]], [k | 1 for k in evens[3:]]
+
+
 def ffn_kernel(n, count, info_ref, *refs):
     x_refs, g_refs, refs = refs[:count], refs[count : 2 * count], refs[2 * count :]
-    w_own, w_other, d_own, d_other = refs[:4]
-    outs, (x, g, w, d, both, mid, sems) = refs[4 : 4 + 4 * count], refs[4 + 4 * count :]
+    parts, (d_own, d_other), refs = refs[:4], refs[4:6], refs[6:]
+    outs, (x, g, w, d, both, mid, sems) = refs[: 4 * count], refs[4 * count :]
     mixed_refs, both_refs = outs[:count], outs[count : 2 * count]
     back_refs, out_refs = outs[2 * count : 3 * count], outs[3 * count :]
     me, part = info_ref[0], info_ref[1]
@@ -392,15 +394,14 @@
     share = cols // 2
     block = width // n
     half = block // 2
-    evens = range(0, n, 2)
 
     copies = []
-    for source, flip in ((w_own, 0), (w_other, 1)):
-        for i, k in enumerate(evens):
-            owner = (me ^ (k | flip)) * block
+    for source, ks in zip(parts, part_pieces(n), strict=True):
+        for i, k in enumerate(ks):
+            owner = (me ^ k) * block
             for j in range(2):
-                at = owner if k == 0 else owner + (part if j == 0 else 1 - part) * half
-                if k == 0:
+                at = owner if k < 2 else owner + (part if j == 0 else 1 - part) * half
+                if k < 2:
                     at = at + j * half
                 copies.append(
                     pltpu.make_async_copy(
@@ -458,13 +459,13 @@
             out_refs[i][:, pl.ds(at, 256)] = out[i * rows : (i + 1) * rows]
 
 
-def ffn(info, xs, gs, w_own, w_other, d_own, d_other):
+def ffn(info, xs, gs, parts, d_own, d_other):
     n = lax.axis_size("fsdp")
     count = len(xs)
     rows, width = xs[0].shape
     cols = 2 * d_own.shape[0]
     if cols % 128:
-        return ffn_plain(info, xs, gs, w_own, w_other, d_own, d_other)
+        return ffn_plain(info, xs, gs, parts, d_own, d_other)
     shapes = (
         [jax.ShapeDtypeStruct((cols, rows), bf16)] * count
         + [jax.ShapeDtypeStruct((rows, 2 * cols), bf16)] * count
@@ -474,7 +475,7 @@
     outs = pl.pallas_call(
         functools.partial(ffn_kernel, n, count),
         out_shape=shapes,
-        in_specs=[pl.BlockSpec(memory_space=pltpu.SMEM)] + [vmem] * (2 * count) + [hbm] * 4,
+        in_specs=[pl.BlockSpec(memory_space=pltpu.SMEM)] + [vmem] * (2 * count) + [hbm] * 6,
         out_specs=[vmem] * (4 * count),
         scratch_shapes=[
             pltpu.VMEM((count * rows, width), bf16),
@@ -491,23 +492,23 @@
             bytes_accessed=6 * width * cols,
             transcendentals=count * rows * cols,
         ),
-    )(info, *xs, *gs, w_own, w_other, d_own, d_other)
+    )(info, *xs, *gs, *parts, d_own, d_other)
     return [outs[i * count : (i + 1) * count] for i in range(4)]
 
 
-def ffn_plain(info, xs, gs, w_own, w_other, d_own, d_other):
+def ffn_plain(info, xs, gs, parts, d_own, d_other):
     n = lax.axis_size("fsdp")
     me, part = info[0], info[1]
     width, share = xs[0].shape[1], d_own.shape[0]
     block, cols = width // n, 2 * share
     half = block // 2
     w = jnp.zeros((width, 2 * cols), bf16)
-    for source, flip in ((w_own, 0), (w_other, 1)):
-        for i, k in enumerate(range(0, n, 2)):
+    for source, ks in zip(parts, part_pieces(n), strict=True):
+        for i, k in enumerate(ks):
             for j in range(2):
-                at = j if k == 0 else (part if j == 0 else 1 - part)
+                at = j if k < 2 else (part if j == 0 else 1 - part)
                 rows = source[i * block + j * half : i * block + (j + 1) * half]
-                w = lax.dynamic_update_slice_in_dim(w, rows, (me ^ (k | flip)) * block + at * half, 0)
+                w = lax.dynamic_update_slice_in_dim(w, rows, (me ^ k) * block + at * half, 0)
     d = jnp.where(
         me % 2 == 0, jnp.concatenate([d_own, d_other], 0), jnp.concatenate([d_other, d_own], 0)
     )
@@ -565,26 +566,24 @@
     )(info, *mixed, *gs, *([] if got is None else [got]))
 
 
-def up_grad_kernel(count, chips, info_ref, *refs):
+def up_grad_kernel(count, split, info_ref, *refs):
     lefts, rights, rest = refs[:count], refs[count : 2 * count], refs[2 * count :]
-    gots, outs = rest[:-chips], rest[-chips:]
     total = sum(
         lax.dot_general(one[...], two[...], contract_first, preferred_element_type=f32)
         for one, two in zip(lefts, rights, strict=True)
-    )
-    for i in range(chips):
+    ).astype(bf16)
+    if not split:
+        rest[0][...] = total
+        return
+    total = (total.astype(f32) + rest[0][...].astype(f32)).astype(bf16)
+    for i, out in enumerate(rest[1:]):
 
         @pl.when(pl.program_id(1) == i)
-        def _(i=i):
-            if gots:
-                outs[i][...] = (
-                    total.astype(bf16).astype(f32) + gots[i][...].astype(f32)
-                ).astype(bf16)
-            else:
-                outs[i][...] = total.astype(bf16)
-
-
-def up_grad(table, xs, both, gots=()):
+        def _(out=out):
+            out[...] = total
+
+
+def up_grad(table, xs, both, got=None):
     count, chips = len(xs), table.shape[0]
     rows, width = xs[0].shape
     cols = both[0].shape[1] // 2
@@ -595,23 +594,30 @@
             lax.dynamic_slice_in_dim(whole, table[i] * block, block, 0).astype(bf16)
             for i in range(chips)
         ]
-        return [added(one, two) for one, two in zip(outs, gots)] if gots else outs
+        if got is None:
+            return jnp.concatenate(outs, 0)
+        return [added(x, got[i * block : (i + 1) * block]) for i, x in enumerate(outs)]
+    one = pl.BlockSpec((block, cols), lambda h, b, table: (b, h))
     outs = [
         pl.BlockSpec(
             (block, cols), lambda h, b, table, i=i: (0, jnp.where(b >= i, h, jnp.maximum(h - 1, 0)))
         )
         for i in range(chips)
     ]
+    split = got is not None
+    shape = jax.ShapeDtypeStruct((block, 2 * cols), bf16)
     return pl.pallas_call(
-        functools.partial(up_grad_kernel, count, chips),
-        out_shape=[jax.ShapeDtypeStruct((block, 2 * cols), bf16)] * chips,
+        functools.partial(up_grad_kernel, count, split),
+        out_shape=[shape] * chips
+        if split
+        else jax.ShapeDtypeStruct((chips * block, 2 * cols), bf16),
         grid_spec=pltpu.PrefetchScalarGridSpec(
             num_scalar_prefetch=1,
             grid=(2, chips),
             in_specs=[pl.BlockSpec((rows, block), lambda h, b, table: (0, table[b]))] * count
             + [pl.BlockSpec((rows, cols), lambda h, b, table: (0, h))] * count
-            + (outs if gots else []),
-            out_specs=outs,
+            + ([one] if split else []),
+            out_specs=outs if split else one,
         ),
         compiler_params=pltpu.CompilerParams(vmem_limit_bytes=48 << 20),
         cost_estimate=pl.CostEstimate(
@@ -619,7 +625,7 @@
             bytes_accessed=4 * chips * block * cols * 2,
             transcendentals=0,
         ),
-    )(table, *xs, *both, *gots)
+    )(table, *xs, *both, *([got] if split else []))
 
 
 def angle_tables(positions):
@@ -700,16 +706,6 @@
     def whole_piece(x):
         return jnp.concatenate(x, 0) if isinstance(x, tuple) else x
 
-    full_qkv = lax.all_gather(qkv_weight, "fsdp", axis=0, tiled=True)
-    fence(
-        gains=gather_small(jnp.stack([norm_attn, norm_ffn])),
-        hidden=hidden_in.reshape(rows, width),
-        grad=cotangent.reshape(rows, width),
-        gate_up=gate_up_weight,
-        down=down_weight,
-        out=out_weight,
-    )
-
     def my_columns(k, at):
         cols = chip ^ (k // 2)
         spots = jnp.stack([cols, cols + chips]).astype(jnp.int32)
@@ -720,60 +716,69 @@
             return lax.dynamic_slice_in_dim(part, at * half, half, 0)
         return pick(live["gate_up"], spots, chip_share, rows_at=(at, half))
 
-    def fetched(k):
-        return send(my_columns(k, part_at), k)
-
     def other_half(k, first):
-        return neighbour(first) if assisted else send(my_columns(k, 1 - part_at), k)
-
-    firsts = {k: fetched(k) for k in near}
-    fence(firsts=firsts, own=my_columns(0, None), d_other=send(live["down"], 1))
-    firsts = live.pop("firsts")
-    seconds = {k: other_half(k, x) for k, x in firsts.items()}
+        return neighbour(first) if assisted else send(live["others"][k], k)
+
+    full_qkv = lax.all_gather(qkv_weight, "fsdp", axis=0, tiled=True)
+    fence(
+        gains=gather_small(jnp.stack([norm_attn, norm_ffn])),
+        hidden=hidden_in.reshape(rows, width),
+        grad=cotangent.reshape(rows, width),
+        gate_up=gate_up_weight,
+        down=down_weight,
+        out=out_weight,
+    )
+
+    firsts = {k: send(my_columns(k, part_at), k) for k in near}
+    fence(
+        firsts=firsts,
+        others={} if assisted else {k: my_columns(k, 1 - part_at) for k in evens[1:]},
+        own=my_columns(0, None),
+        d_other=send(live["down"], 1),
+    )
     inputs = live["hidden"].astype(f32)
     factor_one = norm_factor(inputs)
     gains = live["gains"].astype(f32)
     normed_one = (inputs * factor_one * gains[:1]).astype(bf16)
-    firsts |= {k: fetched(k) for k in rest}
     fence(
-        firsts=firsts,
-        seconds=seconds,
+        seconds={k: other_half(k, live["firsts"][k]) for k in near},
+        mine={k: my_columns(k, part_at) for k in rest},
         qkv=full_qkv,
         normed_one=normed_one,
         normed_one_x=pick(normed_one, to_table, block),
     )
     del live["gate_up"]
 
-    joined = dot(live["normed_one"], live["qkv"])
+    normed_one = live.pop("normed_one")
+    joined = dot(normed_one, live["qkv"][:, q_width:])
     positions = seq_at * rows + jnp.arange(rows, dtype=jnp.int32)
     cosine, sine = angle_tables(positions)
     cos_wide, sin_wide = jnp.tile(cosine, (1, 2 * KVH)), jnp.tile(sine, (1, 2 * KVH))
     cos_t, sin_t = cosine.T, sine.T
     keys_values = jnp.concatenate(
-        [
-            turn(joined[:, q_width : q_width + kv_width], cos_wide, sin_wide, 1),
-            joined[:, q_width + kv_width :].astype(bf16),
-        ],
-        1,
+        [turn(joined[:, :kv_width], cos_wide, sin_wide, 1), joined[:, kv_width:].astype(bf16)], 1
     )
     all_kv = lax.all_gather(keys_values, "seq", axis=0, tiled=True)
+    joined = dot(normed_one, live["qkv"][:, :q_width])
     outs = {0: live.pop("out")}
     outs |= {k: send(outs[0], k) for k in near}
-    fence(joined=joined, kv=all_kv, outs=outs)
-
-    firsts, seconds, outs = live.pop("firsts"), live.pop("seconds"), live.pop("outs")
-    seconds |= {k: other_half(k, firsts[k]) for k in rest}
+    firsts, seconds = live.pop("firsts"), live.pop("seconds")
+    w_own = jnp.concatenate(sum([[firsts[k], seconds[k]] for k in near], [live.pop("own")]), 0)
+    fence(w_own=w_own, joined=joined, kv=all_kv, outs=outs)
+
+    outs = live.pop("outs")
     outs |= two_hops(outs)
+    firsts = {k: send(x, k) for k, x in live.pop("mine").items()}
+    info = jnp.concatenate([(seq_at * rows).reshape(1), at_table]).astype(jnp.int32)
+    attended, lse = attend(info, live["joined"], live["kv"], cos_t, sin_t)
+    fence(firsts=firsts, outs=outs, attended=attended, lse=lse, w_other=send(live["w_own"], 1))
+
+    outs, firsts = live.pop("outs"), live.pop("firsts")
+    out_even = jnp.concatenate([whole_piece(outs[k]) for k in evens], 0)
+    out_odd = send(out_even, 1)
     grads = {0: live["grad"]}
     grads |= {k: send(grads[0], k) for k in near}
-    info = jnp.concatenate([(seq_at * rows).reshape(1), at_table]).astype(jnp.int32)
-    attended, lse = attend(info, live["joined"], live["kv"], cos_t, sin_t)
-    fence(firsts=firsts, seconds=seconds, outs=outs, grads=grads, attended=attended, lse=lse)
-
-    outs, grads = live.pop("outs"), live.pop("grads")
-    out_even = jnp.concatenate([whole_piece(outs[k]) for k in evens], 0)
-    out_odd = send(out_even, 1)
-    grads |= two_hops(grads)
+    seconds = {k: other_half(k, firsts[k]) for k in rest}
     middle = dot(live["attended"][:, : q_width // 2], out_even)
     middle = live["hidden"].astype(f32) + (
         middle + dot(live["attended"][:, q_width // 2 :], out_odd)
@@ -781,15 +786,9 @@
     factor_two = norm_factor(middle)
     gain_two = live["gains"][1:].astype(f32)
     normed_two = (middle * factor_two * gain_two).astype(bf16)
-    w_own = [live.pop("own")]
-    firsts, seconds = live.pop("firsts"), live.pop("seconds")
-    for k in evens[1:]:
-        w_own += [firsts[k], seconds[k]]
-    w_own = jnp.concatenate(w_own, 0)
-    w_other = send(w_own, 1)
     fence(
-        w_own=w_own,
-        w_other=w_other,
+        firsts=firsts,
+        seconds=seconds,
         out_even=out_even,
         out_odd=out_odd,
         grads=grads,
@@ -801,23 +800,30 @@
 
     def ffn_of(group):
         names = ("mixed", "both", "back", "parts")
-        weights = [live[k] for k in ("w_own", "w_other", "down", "d_other")]
+        weights = [live[k] for k in ("w_own", "w_rest", "w_other", "w_rest_other")]
         results = ffn(
             ffn_info,
-            [live["tokens"][k] for k in group],
+            [whole_piece(live["tokens"][k]) for k in group],
             [whole_piece(live["grads"][k]) for k in group],
-            *weights,
+            weights,
+            live["down"],
+            live["d_other"],
         )
         for name, new in zip(names, results, strict=True):
             live[name] = live.get(name, {}) | dict(zip(group, new, strict=True))
 
     new = {k: send(live["tokens"][0], k) for k in near}
+    firsts, seconds = live.pop("firsts"), live.pop("seconds")
+    w_rest = sum([[firsts[k], seconds[k]] for k in rest], [])
+    live["w_rest"] = jnp.concatenate(w_rest or [live["w_own"]], 0)
+    live["w_rest_other"] = send(live["w_rest"], 1)
     ffn_of([0])
     live["tokens"] |= new
     fence()
-    new = {k: send(live["tokens"][0], k) for k in rest}
+    far_tokens, far_grads = two_hops(live["tokens"]), two_hops(live["grads"])
     ffn_of(near)
-    live["tokens"] |= new
+    live["tokens"] |= far_tokens
+    live["grads"] |= far_grads
     fence()
     new = {k: send(live["back"][k], k) for k in near}
     if rest:
@@ -832,11 +838,11 @@
     theirs = down_grad(ffn_info, 3, each("mixed"), each("grads"))
     gots = up_grad(after(odd_table, theirs), each("tokens"), each("both"))
     got = send(theirs, 1)
-    grad_down = down_grad(after(ffn_info, gots[0]), 2, each("mixed"), each("grads"), got)
-    fence(gots=list(gots), zd=grad_down[: share // 2], ze=grad_down[share // 2 :])
+    grad_down = down_grad(after(ffn_info, gots), 2, each("mixed"), each("grads"), got)
+    fence(gots=gots, zd=grad_down[: share // 2], ze=grad_down[share // 2 :])
 
     line_step(live, new="d")
-    gots = [send(x, 1) for x in live.pop("gots")]
+    gots = send(live.pop("gots"), 1)
     grad_normed_two = live["back"][0].astype(f32)
     for k in evens[1:]:
         grad_normed_two = grad_normed_two + live["returned"][k].astype(f32)
@@ -850,7 +856,9 @@
         [dot_last(grad_branch, live[k]).astype(bf16) for k in ("out_even", "out_odd")], 1
     )
     parts = up_grad(even_table, each("tokens"), each("both"), gots)
-    for k in ("tokens", "grads", "both", "mixed", "back", "returned", "w_own", "w_other", "d_other"):
+    for k in ("tokens", "grads", "both", "mixed", "back", "returned", "d_other"):
+        del live[k]
+    for k in ("w_own", "w_rest", "w_other", "w_rest_other"):
         del live[k]
     del live["out_even"], live["out_odd"], live["down"], live["grad"]
     fence(
@@ -862,9 +870,6 @@
     )
 
     names = [str(k) for k in evens]
-
-    def crossed(whole):
-        return send(whole[whole.shape[0] // 2 :], 1)
 
     def blocks(whole, got):
         return {
@@ -910,19 +915,8 @@
         live[f"z{k}"] = x
     line_step(live, new=names[0], cross="e", out="d")
     sent = {k: send(ups[k], k) for k in rest}
-    length = live["kv_parts"].shape[1]
-    kv_parts = live.pop("kv_parts").reshape(KVH, length, 2, HD).transpose(1, 2, 0, 3)
-    kv_sums = lax.psum_scatter(
-        kv_parts.reshape(length, 2 * kv_width), "seq", scatter_dimension=0, tiled=True
-    )
-    grad_out = dot_first(live.pop("attended"), live.pop("grad_branch")).astype(bf16)
-    fence(sent=sent, kv_sums=kv_sums, grad_out=grad_out, got_out=crossed(grad_out))
-
-    for k, x in live.pop("sent").items():
-        live[f"z{k}"] = x
-    line_step(live, new=names[1], cross=names[0], out="e")
-    parts_out = blocks(live.pop("grad_out"), live.pop("got_out"))
-    kv_sums = live.pop("kv_sums")
+    kv_sums = lax.psum_scatter(live.pop("kv_parts"), "seq", scatter_dimension=0, tiled=True)
+    kv_sums = kv_sums.reshape(rows, KVH, 2, HD).transpose(0, 2, 1, 3).reshape(rows, 2 * kv_width)
     grad_joined = jnp.concatenate(
         [
             live.pop("grad_queries"),
@@ -931,14 +925,24 @@
         ],
         1,
     )
-    grad_qkv = dot_first(live.pop("normed_one_x"), grad_joined).astype(bf16)
+    normed_one_x = live.pop("normed_one_x")
+    theirs = dot_first(normed_one_x[:, width // 2 :], grad_joined).astype(bf16)
+    attended = pick(live.pop("attended"), at_table, block)
+    grad_out = dot_first(attended, live.pop("grad_branch")).astype(bf16)
     fence(
-        parts_out=parts_out,
-        far_out=far_sends(parts_out),
+        sent=sent,
+        grad_out=grad_out,
         grad_joined=grad_joined,
-        grad_qkv=grad_qkv,
-        got_qkv=crossed(grad_qkv),
-    )
+        normed_one_x=normed_one_x,
+        theirs=theirs,
+    )
+
+    for k, x in live.pop("sent").items():
+        live[f"z{k}"] = x
+    line_step(live, new=names[1], cross=names[0], out="e")
+    out_total = lax.psum_scatter(live.pop("grad_out"), "fsdp", scatter_dimension=0, tiled=True)
+    mine = dot_first(live.pop("normed_one_x")[:, : width // 2], live["grad_joined"])
+    fence(got_qkv=send(live.pop("theirs"), 1), mine=mine.astype(bf16))
 
     gate_up_sums = blank((block, 2 * FF), f32)
     outer = is_outer()
@@ -952,18 +956,14 @@
         return place(buffer, (live.pop(f"o{k}"), live.pop(f"t{k}")), outer, spots, chip_share)
 
     line_step(live, new=names[2] if chips > 2 else None, cross=names[1], out=names[0])
-    parts_qkv = blocks(live.pop("grad_qkv"), live.pop("got_qkv"))
-    fence(
-        near_out=near_sends(live["parts_out"], live["far_out"]),
-        parts_qkv=parts_qkv,
-        down_sums=jnp.concatenate([summed("d"), summed("e")], 0),
-    )
+    parts_qkv = blocks(live.pop("mine"), live.pop("got_qkv"))
+    down_sums = jnp.concatenate([summed("d"), summed("e")], 0)
+    fence(parts_qkv=parts_qkv, far_qkv=far_sends(parts_qkv), down_sums=down_sums)
 
     line_step(live, new=names[3] if chips > 3 else None, cross=names[2], out=names[1])
     for k in evens[4:]:
         line_step(live, new=str(k))
     gate_up_sums = placed_in(gate_up_sums, 0)
-    zout = total_of(live.pop("parts_out"), live.pop("far_out"), live.pop("near_out"))
     inputs = live["hidden"].astype(f32)
     factor_one = norm_factor(inputs)
     grad_normed_one = dot_last(live.pop("grad_joined"), live.pop("qkv"))
@@ -972,39 +972,38 @@
     )
     grad_input = (live["grad_middle"] + grad_norm_one).astype(bf16)
     fence(
-        far_qkv=far_sends(live["parts_qkv"]),
-        zout=zout.astype(bf16),
+        near_qkv=near_sends(live["parts_qkv"], live["far_qkv"]),
+        zout=out_total,
+        sums=gate_up_sums,
         grad_input=grad_input,
         grad_gains=jnp.stack([grad_gain_one, live.pop("grad_gain_two")]),
-        sums=gate_up_sums,
     )
 
     line_step(live, new="out", cross=names[3], out=names[2])
     gate_up_sums = placed_in(live.pop("sums"), evens[1])
-    fence(near_qkv=near_sends(live["parts_qkv"], live["far_qkv"]), sums=gate_up_sums)
-
     total = total_of(live.pop("parts_qkv"), live.pop("far_qkv"), live.pop("near_qkv")).astype(bf16)
-    live["zq"], live["zr"] = total[:half], total[half:]
+    fence(far=far_sends(live["parts"]), sums=gate_up_sums, zq=total[:half], zr=total[half:])
+
     line_step(live, new="q", cross="out", out=names[3])
     gate_up_sums = placed_in(live.pop("sums"), evens[2])
-    fence(far=far_sends(live["parts"]), sums=gate_up_sums)
+    fence(near=near_sends(live["parts"], live["far"]), sums=gate_up_sums)
 
     line_step(live, new="r", cross="q", out="out")
     gate_up_sums = live.pop("sums")
     for k in evens[3:]:
         gate_up_sums = placed_in(gate_up_sums, k)
-    fence(near=near_sends(live["parts"], live["far"]), sums=gate_up_sums)
-
-    line_step(live, cross="r", out="q")
-    out_sums = summed("out")
-    grad_gains = small_sum(live.pop("grad_gains"))
+    grad_gains = small_sum(live.pop("grad_gains"), "fsdp")
     out = total_of(live.pop("parts"), live.pop("far"), live.pop("near"))
     out = (live["middle"] + out).astype(bf16)
-    fence(grad_gains=grad_gains, out_final=out, out_sums=out_sums)
+    fence(sums=gate_up_sums, grad_gains=grad_gains, out_final=out)
+
+    line_step(live, cross="r", out="q")
+    fence(out_sums=summed("out"))
 
     line_step(live, out="r")
+    grad_gains = small_sum(live.pop("grad_gains"), "seq")
     qkv_sums = jnp.concatenate([summed("q"), summed("r")], 0)
-    grad_gains = lax.dynamic_slice_in_dim(live["grad_gains"], me * block, block, 1)
+    grad_gains = lax.dynamic_slice_in_dim(grad_gains, me * block, block, 1)
     return (
         live["out_final"].reshape(hidden_in.shape),
         live["grad_input"].reshape(hidden_in.shape),

time: 798 us -> 771 us (0.966)
  waiting for transfers between devices: 244 us -> 217 us
  local copies, waits for them, and re-layouts: 55.2 us -> 44.5 us
  other arithmetic: 98.4 us -> 89.3 us
  starting transfers between devices: 131 us -> 140 us
    ppermute x45 -> x39, waiting for transfers between devices: 124 us -> 65.1 us  [send(): return lax.ppermute(x, 'fsdp', [(i, i ^ k) for i in range(n)])]
    ppermute x7 -> x9, waiting for transfers between devices: 34.8 us -> 88 us  [line_step(): live['o' + out] = lax.ppermute(total, 'seq', outward)]
    ppermute x7 -> x9, waiting for transfers between devices: 49.5 us -> 17.4 us  [line_step(): live['i' + new] = lax.ppermute(x, 'seq', inward)]
    ppermute x3, waiting for transfers between devices: 0.01 us -> 28.2 us  [neighbour(): return lax.ppermute(x, 'seq', [(i, i ^ 1) for i in range(n)])]
    ppermute x7 -> x9, starting transfers between devices: 40.6 us -> 60.3 us  [line_step(): live['i' + new] = lax.ppermute(x, 'seq', inward)]
    ppermute x2 -> x0, waiting for transfers between devices: 12.8 us -> none  [line_step(): got = lax.ppermute(jnp.where(is_outer(), x, total), 'seq', inward + outward)]
    ppermute x2 -> x0, starting transfers between devices: 11.4 us -> none  [line_step(): got = lax.ppermute(jnp.where(is_outer(), x, total), 'seq', inward + outward)]
    all_gather x1, waiting for transfers between devices: 10.1 us -> 0.01 us  [on_device(): full_qkv = lax.all_gather(qkv_weight, 'fsdp', axis=0, tiled=True)]
  transfers between devices with their start and end apart: 81 -> 78, of which waited for: 36 -> 41; matrix products, arithmetic and copies ran while one was open for 15% -> 16% of each run, Pallas kernels for 27% -> 29%
where the time goes in v3:
time: 771 us; the launch traced here: 763 us
  Pallas kernels  223 us (29%)
  waiting for transfers between devices  217 us (28%)
  starting transfers between devices  140 us (18%)
  other arithmetic  89.3 us (12%)
  local copies, waits for them, and re-layouts  44.5 us (6%)
  matrix products  33 us (4%)
  between operations  15.5 us (2%)
    ppermute x9, waiting for transfers between devices, line_step(): live['o' + out] = lax.ppermute(total, 'seq', outward)  88 us
    pallas_call x3, Pallas kernels, ffn(): pl.pallas_call(functools.partial(ffn_kernel, n, count), out_shape=shapes,...  76.5 us
    ppermute x39, waiting for transfers between devices, send(): return lax.ppermute(x, 'fsdp', [(i, i ^ k) for i in range(n)])  65.1 us
    ppermute x9, starting transfers between devices, line_step(): live['i' + new] = lax.ppermute(x, 'seq', inward)  60.3 us
    convert_element_type x23, other arithmetic, added(): return (one.astype(f32) + two.astype(f32)).astype(bf16)  41.9 us
    ppermute x39, starting transfers between devices, send(): return lax.ppermute(x, 'fsdp', [(i, i ^ k) for i in range(n)])  41.5 us
    pallas_call x1, Pallas kernels, attend_back(): pl.pallas_call(functools.partial(attend_back_kernel, heads, per_kv), out_...  36.5 us
    pallas_call x1, Pallas kernels, attend(): pl.pallas_call(functools.partial(attend_kernel, heads, HEADS // KVH), out...  30.2 us
  transfers between devices with their start and end apart: 78, of which 41 were waited for; matrix products, arithmetic and copies ran while one was open for 16% of the time, Pallas kernels for 29%

profile of v3, /device:TPU:0, one launch (start us, length us, event | category | flops | bytes accessed | tf_op | source)
XLA Modules:
  0.0 762.8 jit_solution(18035688102116859956)
XLA Ops:
  35.5 17.5 %collective-permute-done.4 = bf16[128,2816]{1,0:T(8,128)(2,1)} collective-permute-done((bf16[128,2816]{1,0:T(8,128)(2,1)}, bf16[128,2816]{1,0:T(8,128)(2,1)}, u32[]{:S(2)}, u32[]{:S(2)}) %collective-permute-start.4) | collective-permute-done | bytes 720928 | tf_op jit(solution)/shard_map/ppermute | solution.py:26
  65.8 7.1 collective-permute-done.6
  72.9 14.2 %collective-permute-done.7 = bf16[128,2816]{1,0:T(8,128)(2,1)S(1)} collective-permute-done((bf16[128,2816]{1,0:T(8,128)(2,1)}, bf16[128,2816]{1,0:T(8,128)(2,1)S(1)}, u32[]{:S(2)}, u32[]{:S(2)}) %collective-permute-start.7) | collective-permute-done | bytes 720928 | tf_op jit(solution)/shard_map/ppermute | solution.py:51
  116.3 8.6 %all-gather.5.cloned.1.call-done.k_ref.v_ref = bf16[1024,512]{1,0:T(8,128)(2,1)} async-done(((bf16[256,512]{1,0:T(8,128)(2,1)}), bf16[1024,512]{1,0:T(8,128)(2,1)}) %all-gather.5.cloned.1.call-update) | async-done | bytes 1048592 | tf_op jit(solution)/shard_map/all_gather | solution.py:761
  132.1 30.2 %shard_map.167 = (bf16[256,2048]{1,0:T(8,128)(2,1)S(1)}, f32[8,4,256]{2,1,0:T(4,128)S(1)}) custom-call(s32[9]{0:T(128)S(1)} %get-tuple-element.953.info_ref, f32[256,2048]{1,0:T(8,128)S(1)} %fusion.q_ref, bf16[1024,512]{1,0:T(8,128)(2,1)S(1)} %copy-done.17, bf16[1024,512]{1,0:T(8,128)(2,1)S(1)} %copy-done.17, f32[32,256]{1,0:T(8,128)S(1)} %get-tuple-element.945.cos_ref, ...), custom_call_target="tpu_custom_call" | custom-call | flops 8589934592 | bytes 3145728 | tf_op jit(solution)/shard_map/pallas_call | solution.py:270
  179.7 6.9 collective-permute-done.17
  197.8 21.5 %shard_map.168 = (bf16[1408,256]{1,0:T(8,128)(2,1)}, bf16[256,2816]{1,0:T(8,128)(2,1)}, bf16[256,2048]{1,0:T(8,128)(2,1)}, bf16[256,2048]{1,0:T(8,128)(2,1)}) custom-call(s32[4]{0:T(128)} %pad_add_fusion.4.info_ref, bf16[256,2048]{1,0:T(8,128)(2,1)} %get-tuple-element.697.refs_0_, bf16[256,2048]{1,0:T(8,128)(2,1)} %bitcast.47, ...), custom_call_target="tpu_custom_call" | custom-call | flops 8858370048 | bytes 17301504 | tf_op jit(solution)/shard_map/pallas_call | solution.py:475
  225.9 33.2 %shard_map.169 = (bf16[1408,256]{1,0:T(8,128)(2,1)}, bf16[1408,256]{1,0:T(8,128)(2,1)}, bf16[256,2816]{1,0:T(8,128)(2,1)}, bf16[256,2816]{1,0:T(8,128)(2,1)}, bf...) custom-call(s32[4]{0:T(128)} %pad_add_fusion.4.info_ref, ...), custom_call_target="tpu_custom_call" | custom-call | flops 17716740096 | bytes 17301504 | tf_op jit(solution)/shard_map/pallas_call | solution.py:475
  263.6 21.8 %shard_map.170 = (bf16[1408,256]{1,0:T(8,128)(2,1)}, bf16[256,2816]{1,0:T(8,128)(2,1)}, bf16[256,2048]{1,0:T(8,128)(2,1)}, bf16[256,2048]{1,0:T(8,128)(2,1)}) custom-call(s32[4]{0:T(128)} %pad_add_fusion.4.info_ref, bf16[256,2048]{1,0:T(8,128)(2,1)} %get-tuple-element.959.refs_0_, bf16[256,2048]{1,0:T(8,128)(2,1)} %get-tuple-element.960.refs_1_, ...), custom_call_target="tpu_custom_call" | custom-call | flops 8858370048 | bytes 17301504 | tf_op jit(solution)/shard_map/pallas_call | solution.py:475
  296.1 12.8 %shard_map.172 = bf16[1024,2816]{1,0:T(8,128)(2,1)} custom-call(s32[4]{0:T(128)S(1)} %get-tuple-element.653.info_ref, bf16[256,2048]{1,0:T(8,128)(2,1)} %get-tuple-element.697.refs_0_, bf16[256,2048]{1,0:T(8,128)(2,1)} %collective-permute-done.19.refs_0_.refs_1_, bf16[256,2048]{1,0:T(8,128)(2,1)S(1)} %copy-done.13, ...), custom_call_target="tpu_custom_call" | custom-call | flops 5905580032 | bytes 11534336 | tf_op jit(solution)/shard_map/pallas_call | solution.py:609
  314.3 7.5 collective-permute-done.27
  339.7 15.1 %shard_map.174 = (bf16[256,2816]{1,0:T(8,128)(2,1)S(1)}, bf16[256,2816]{1,0:T(8,128)(2,1)}, bf16[256,2816]{1,0:T(8,128)(2,1)}, bf16[256,2816]{1,0:T(8,128)(2,1)}) custom-call(s32[4]{0:T(128)S(1)} %get-tuple-element.954.info_ref, bf16[256,2048]{1,0:T(8,128)(2,1)} %get-tuple-element.697.refs_0_, bf16[256,2048]{1,0:T(8,128)(2,1)} %collective-permute-done.19.refs_0_.refs_1_, ...), custom_call_target="tpu_custom_call" | custom-call | flops 5905580032 | bytes 11534336 | tf_op jit(solution)/shard_map/pallas_call | solution.py:609
  366.0 36.5 %shard_map.175 = (bf16[256,2048]{1,0:T(8,128)(2,1)S(1)}, bf16[1024,512]{1,0:T(8,128)(2,1)}) custom-call(s32[9]{0:T(128)S(1)} %get-tuple-element.953.info_ref, f32[256,2048]{1,0:T(8,128)} %copy-done.19, bf16[1024,512]{1,0:T(8,128)(2,1)S(1)} %copy-done.18, bf16[1024,512]{1,0:T(8,128)(2,1)S(1)} %copy-done.18, bf16[256,2048]{1,0:T(8,128)(2,1)S(1)} %pad_maximum_fusion.6.g_ref, ...), custom_call_target="tpu_custom_call" | custom-call | flops 21474836480 | bytes 4194304 | tf_op jit(solution)/shard_map/pallas_call | solution.py:347
  427.6 7.1 convolution_convert_fusion
  450.8 8.7 %collective-permute-done.36 = bf16[352,2048]{1,0:T(8,128)(2,1)} collective-permute-done((bf16[352,2048]{1,0:T(8,128)(2,1)}, bf16[352,2048]{1,0:T(8,128)(2,1)}, u32[]{:S(2)}, u32[]{:S(2)}) %collective-permute-start.36) | collective-permute-done | bytes 1441824 | tf_op jit(solution)/shard_map/ppermute | solution.py:101
  477.8 21.8 %collective-permute-done.41 = bf16[352,2048]{1,0:T(8,128)(2,1)} collective-permute-done((bf16[352,2048]{1,0:T(8,128)(2,1)S(1)}, bf16[352,2048]{1,0:T(8,128)(2,1)}, u32[]{:S(2)}, u32[]{:S(2)}) %collective-permute-start.41) | collective-permute-done | bytes 1441824 | tf_op jit(solution)/shard_map/ppermute | solution.py:101
  508.2 9.0 %collective-permute-start.45 = (bf16[256,2816]{1,0:T(8,128)(2,1)}, bf16[256,2816]{1,0:T(8,128)(2,1)S(1)}, u32[]{:S(2)}, u32[]{:S(2)}) collective-permute-start(bf16[256,2816]{1,0:T(8,128)(2,1)} %collective-permute-done.33), channel_id=1, source_target_pairs={{0,1},{3,2},{4,5},{7,6},{8,9},{11,10},{12,13},{15,14},{16,17},{19,... | collective-permute-start | bytes 4325384 | tf_op jit(solution)/shard_map/ppermute | solution.py:95
  530.5 11.6 %collective-permute-done.44 = bf16[128,2560]{1,0:T(8,128)(2,1)S(1)} collective-permute-done((bf16[128,2560]{1,0:T(8,128)(2,1)S(1)}, bf16[128,2560]{1,0:T(8,128)(2,1)S(1)}, u32[]{:S(2)}, u32[]{:S(2)}) %collective-permute-start.44) | collective-permute-done | bytes 655392 | tf_op jit(solution)/shard_map/ppermute | solution.py:26
  560.4 7.0 collective-permute-start.48
  580.1 12.8 %collective-permute-done.51.got_ref = bf16[256,2816]{1,0:T(8,128)(2,1)} collective-permute-done((bf16[256,2816]{1,0:T(8,128)(2,1)}, bf16[256,2816]{1,0:T(8,128)(2,1)}, u32[]{:S(2)}, u32[]{:S(2)}) %collective-permute-start.51) | collective-permute-done | bytes 1441824 | tf_op jit(solution)/shard_map/ppermute | solution.py:101
  627.2 15.4 %collective-permute-done.56.got_ref = bf16[256,2816]{1,0:T(8,128)(2,1)} collective-permute-done((bf16[256,2816]{1,0:T(8,128)(2,1)S(1)}, bf16[256,2816]{1,0:T(8,128)(2,1)}, u32[]{:S(2)}, u32[]{:S(2)}) %collective-permute-start.56) | collective-permute-done | bytes 1441824 | tf_op jit(solution)/shard_map/ppermute | solution.py:101
  688.2 8.2 %collective-permute-start.66 = (bf16[128,2560]{1,0:T(8,128)(2,1)S(1)}, bf16[128,2560]{1,0:T(8,128)(2,1)}, u32[]{:S(2)}, u32[]{:S(2)}) collective-permute-start(bf16[128,2560]{1,0:T(8,128)(2,1)S(1)} %get-tuple-element.903), channel_id=1, source_target_pairs={{0,1},{3,2},{4,5},{7,6},{8,9},{11,10},{12,13},{15,14},{16,17},{19,... | collective-permute-start | bytes 1966088 | tf_op jit(solution)/shard_map/ppermute | solution.py:95
  718.6 13.5 %collective-permute-done.69 = bf16[128,2560]{1,0:T(8,128)(2,1)S(1)} collective-permute-done((bf16[128,2560]{1,0:T(8,128)(2,1)S(1)}, bf16[128,2560]{1,0:T(8,128)(2,1)S(1)}, u32[]{:S(2)}, u32[]{:S(2)}) %collective-permute-start.69) | collective-permute-done | bytes 655392 | tf_op jit(solution)/shard_map/ppermute | solution.py:101
  744.6 9.6 %collective-permute-done.73 = bf16[128,2560]{1,0:T(8,128)(2,1)S(1)} collective-permute-done((bf16[128,2560]{1,0:T(8,128)(2,1)S(1)}, bf16[128,2560]{1,0:T(8,128)(2,1)S(1)}, u32[]{:S(2)}, u32[]{:S(2)}) %collective-permute-start.73) | collective-permute-done | bytes 655392 | tf_op jit(solution)/shard_map/ppermute | solution.py:101
  (455 shorter events, 389.7 us)
Async XLA Ops:
  7.2 79.9 %all-gather.3.cloned.1.call-start = ((), (), s32[]{:S(2)}) async-start(), calls=%async_computation.2 | async-start | bytes 11796480 | tf_op jit(solution)/shard_map/all_gather | solution.py:722
  7.9 116.9 %all-gather.5.cloned.1.call-start = ((), (), s32[]{:S(2)}) async-start(), calls=%async_computation.3 | async-start | bytes 1310720 | tf_op jit(solution)/shard_map/all_gather | solution.py:761
  96.7 344.0 %reduce-scatter.3.cloned.1.call-start = ((), (), s32[]{:S(2)}) async-start(), calls=%async_computation.4 | async-start | bytes 1310720 | tf_op jit(solution)/shard_map/reduce_scatter | solution.py:918
  124.8 37.6 %collective-permute-start.13 = (bf16[768,2816]{1,0:T(8,128)(2,1)}, bf16[768,2816]{1,0:T(8,128)(2,1)}, u32[]{:S(2)}, u32[]{:S(2)}) collective-permute-start(bf16[768,2816]{1,0:T(8,128)(2,1)} %constant_dynamic-update-slice_fusion.refs_2_.refs_4_), channel_id=1, source_target_pairs={{0,4},{4,0},{8,12},{12,8},{16,20},{20,16},{24,28},{28,24},{1,5},{5... | collective-permute-start | bytes 12976136 | tf_op jit(solution)/shard_map/ppermute | solution.py:26
  221.7 37.3 %collective-permute-start.21 = (bf16[128,2048]{1,0:T(8,128)(2,1)S(1)}, bf16[128,2048]{1,0:T(8,128)(2,1)S(1)}, u32[]{:S(2)}, u32[]{:S(2)}) collective-permute-start(bf16[128,2048]{1,0:T(8,128)(2,1)S(1)} %slice.156), channel_id=1, source_target_pairs={{0,8},{4,12},{8,0},{12,4},{16,24},{20,28},{24,16},{28,20},{1,9},{5... | collective-permute-start | bytes 1572872 | tf_op jit(solution)/shard_map/ppermute | solution.py:26
  223.3 35.8 %collective-permute-start.22 = (bf16[128,2048]{1,0:T(8,128)(2,1)S(1)}, bf16[128,2048]{1,0:T(8,128)(2,1)S(1)}, u32[]{:S(2)}, u32[]{:S(2)}) collective-permute-start(bf16[128,2048]{1,0:T(8,128)(2,1)S(1)} %slice.157), channel_id=1, source_target_pairs={{0,16},{4,20},{8,24},{12,28},{16,0},{20,4},{24,8},{28,12},{1,17},{... | collective-permute-start | bytes 1572872 | tf_op jit(solution)/shard_map/ppermute | solution.py:26
  321.8 34.8 %collective-permute-start.29 = (bf16[352,2048]{1,0:T(8,128)(2,1)S(1)}, bf16[352,2048]{1,0:T(8,128)(2,1)S(1)}, u32[]{:S(2)}, u32[]{:S(2)}) collective-permute-start(bf16[352,2048]{1,0:T(8,128)(2,1)S(1)} %get-tuple-element.725), channel_id=1, source_target_pairs={{0,1},{3,2},{4,5},{7,6},{8,9},{11,10},{12,13},{15,14},{16,17},{19,... | collective-permute-start | bytes 4325384 | tf_op jit(solution)/shard_map/ppermute | solution.py:95
  357.2 45.3 %collective-permute-start.34 = (bf16[352,2048]{1,0:T(8,128)(2,1)S(1)}, bf16[352,2048]{1,0:T(8,128)(2,1)S(1)}, u32[]{:S(2)}, u32[]{:S(2)}) collective-permute-start(bf16[352,2048]{1,0:T(8,128)(2,1)S(1)} %add_convert_fusion.11), channel_id=1, source_target_pairs={{1,2},{2,1},{5,6},{6,5},{9,10},{10,9},{13,14},{14,13},{17,18},{18,... | collective-permute-start | bytes 4325384 | tf_op jit(solution)/shard_map/ppermute | solution.py:91
  358.1 44.4 %collective-permute-start.31 = (bf16[352,2048]{1,0:T(8,128)(2,1)S(1)}, bf16[352,2048]{1,0:T(8,128)(2,1)S(1)}, u32[]{:S(2)}, u32[]{:S(2)}) collective-permute-start(bf16[352,2048]{1,0:T(8,128)(2,1)S(1)} %get-tuple-element.748), channel_id=1, source_target_pairs={{0,1},{3,2},{4,5},{7,6},{8,9},{11,10},{12,13},{15,14},{16,17},{19,... | collective-permute-start | bytes 4325384 | tf_op jit(solution)/shard_map/ppermute | solution.py:95
  364.7 39.0 %collective-permute-start.32 = (bf16[256,2816]{1,0:T(8,128)(2,1)}, bf16[256,2816]{1,0:T(8,128)(2,1)}, u32[]{:S(2)}, u32[]{:S(2)}) collective-permute-start(bf16[256,2816]{1,0:T(8,128)(2,1)} %get-tuple-element.735), channel_id=1, source_target_pairs={{0,8},{4,12},{8,0},{12,4},{16,24},{20,28},{24,16},{28,20},{1,9},{5... | collective-permute-start | bytes 4325384 | tf_op jit(solution)/shard_map/ppermute | solution.py:26
  365.3 38.7 %collective-permute-start.33 = (bf16[256,2816]{1,0:T(8,128)(2,1)S(1)}, bf16[256,2816]{1,0:T(8,128)(2,1)}, u32[]{:S(2)}, u32[]{:S(2)}) collective-permute-start(bf16[256,2816]{1,0:T(8,128)(2,1)S(1)} %copy-done.72), channel_id=1, source_target_pairs={{0,16},{4,20},{8,24},{12,28},{16,0},{20,4},{24,8},{28,12},{1,17},{... | collective-permute-start | bytes 4325384 | tf_op jit(solution)/shard_map/ppermute | solution.py:26
  404.1 191.1 %reduce-scatter.5.cloned.1.call-start = ((), (), s32[]{:S(2)}) async-start(), calls=%async_computation.5 | async-start | bytes 9437184 | tf_op jit(solution)/shard_map/reduce_scatter | solution.py:943
  408.0 51.5 %collective-permute-start.38 = (bf16[352,2048]{1,0:T(8,128)(2,1)}, bf16[352,2048]{1,0:T(8,128)(2,1)}, u32[]{:S(2)}, u32[]{:S(2)}) collective-permute-start(bf16[352,2048]{1,0:T(8,128)(2,1)} %add_convert_fusion.10), channel_id=1, source_target_pairs={{1,2},{2,1},{5,6},{6,5},{9,10},{10,9},{13,14},{14,13},{17,18},{18,... | collective-permute-start | bytes 4325384 | tf_op jit(solution)/shard_map/ppermute | solution.py:91
  411.4 48.1 %collective-permute-start.36 = (bf16[352,2048]{1,0:T(8,128)(2,1)}, bf16[352,2048]{1,0:T(8,128)(2,1)}, u32[]{:S(2)}, u32[]{:S(2)}) collective-permute-start(bf16[352,2048]{1,0:T(8,128)(2,1)} %add_convert_fusion.9), channel_id=1, source_target_pairs={{1,0},{2,3},{5,4},{6,7},{9,8},{10,11},{13,12},{14,15},{17,16},{18,... | collective-permute-start | bytes 4325384 | tf_op jit(solution)/shard_map/ppermute | solution.py:101
  412.7 46.8 %collective-permute-start.35 = (bf16[256,2816]{1,0:T(8,128)(2,1)S(1)}, bf16[256,2816]{1,0:T(8,128)(2,1)}, u32[]{:S(2)}, u32[]{:S(2)}) collective-permute-start(bf16[256,2816]{1,0:T(8,128)(2,1)S(1)} %get-tuple-element.772), channel_id=1, source_target_pairs={{0,1},{3,2},{4,5},{7,6},{8,9},{11,10},{12,13},{15,14},{16,17},{19,... | collective-permute-start | bytes 4325384 | tf_op jit(solution)/shard_map/ppermute | solution.py:95
  419.4 40.1 %collective-permute-start.37 = (bf16[256,2816]{1,0:T(8,128)(2,1)}, bf16[256,2816]{1,0:T(8,128)(2,1)}, u32[]{:S(2)}, u32[]{:S(2)}) collective-permute-start(bf16[256,2816]{1,0:T(8,128)(2,1)} %get-tuple-element.761), channel_id=1, source_target_pairs={{0,24},{4,28},{8,16},{12,20},{16,8},{20,12},{24,0},{28,4},{1,25},{... | collective-permute-start | bytes 4325384 | tf_op jit(solution)/shard_map/ppermute | solution.py:26
  459.5 42.6 %collective-permute-start.39 = (bf16[1024,2560]{1,0:T(8,128)(2,1)}, bf16[1024,2560]{1,0:T(8,128)(2,1)}, u32[]{:S(2)}, u32[]{:S(2)}) collective-permute-start(bf16[1024,2560]{1,0:T(8,128)(2,1)} %convolution_convert_fusion.2), channel_id=1, source_target_pairs={{0,4},{4,0},{8,12},{12,8},{16,20},{20,16},{24,28},{28,24},{1,5},{5... | collective-permute-start | bytes 15728648 | tf_op jit(solution)/shard_map/ppermute | solution.py:26
  463.7 36.0 %collective-permute-start.41 = (bf16[352,2048]{1,0:T(8,128)(2,1)S(1)}, bf16[352,2048]{1,0:T(8,128)(2,1)}, u32[]{:S(2)}, u32[]{:S(2)}) collective-permute-start(bf16[352,2048]{1,0:T(8,128)(2,1)S(1)} %add_convert_fusion.7), channel_id=1, source_target_pairs={{1,0},{2,3},{5,4},{6,7},{9,8},{10,11},{13,12},{14,15},{17,16},{18,... | collective-permute-start | bytes 4325384 | tf_op jit(solution)/shard_map/ppermute | solution.py:101
  465.0 37.2 %collective-permute-start.40 = (bf16[256,2816]{1,0:T(8,128)(2,1)}, bf16[256,2816]{1,0:T(8,128)(2,1)}, u32[]{:S(2)}, u32[]{:S(2)}) collective-permute-start(bf16[256,2816]{1,0:T(8,128)(2,1)} %collective-permute-done.32), channel_id=1, source_target_pairs={{0,1},{3,2},{4,5},{7,6},{8,9},{11,10},{12,13},{15,14},{16,17},{19,... | collective-permute-start | bytes 4325384 | tf_op jit(solution)/shard_map/ppermute | solution.py:95
  504.3 42.7 %collective-permute-start.47 = (bf16[256,2816]{1,0:T(8,128)(2,1)S(1)}, bf16[256,2816]{1,0:T(8,128)(2,1)S(1)}, u32[]{:S(2)}, u32[]{:S(2)}) collective-permute-start(bf16[256,2816]{1,0:T(8,128)(2,1)S(1)} %add_convert_fusion.6), channel_id=1, source_target_pairs={{1,2},{2,1},{5,6},{6,5},{9,10},{10,9},{13,14},{14,13},{17,18},{18,... | collective-permute-start | bytes 4325384 | tf_op jit(solution)/shard_map/ppermute | solution.py:91
  506.9 38.5 %collective-permute-start.46 = (bf16[256,2816]{1,0:T(8,128)(2,1)S(1)}, bf16[256,2816]{1,0:T(8,128)(2,1)S(1)}, u32[]{:S(2)}, u32[]{:S(2)}) collective-permute-start(bf16[256,2816]{1,0:T(8,128)(2,1)S(1)} %add_convert_fusion.5.total_ref), channel_id=1, source_target_pairs={{1,0},{2,3},{5,4},{6,7},{9,8},{10,11},{13,12},{14,15},{17,16},{18,... | collective-permute-start | bytes 4325384 | tf_op jit(solution)/shard_map/ppermute | solution.py:101
  508.2 38.7 %collective-permute-start.45 = (bf16[256,2816]{1,0:T(8,128)(2,1)}, bf16[256,2816]{1,0:T(8,128)(2,1)S(1)}, u32[]{:S(2)}, u32[]{:S(2)}) collective-permute-start(bf16[256,2816]{1,0:T(8,128)(2,1)} %collective-permute-done.33), channel_id=1, source_target_pairs={{0,1},{3,2},{4,5},{7,6},{8,9},{11,10},{12,13},{15,14},{16,17},{19,... | collective-permute-start | bytes 4325384 | tf_op jit(solution)/shard_map/ppermute | solution.py:95
  555.8 39.4 %collective-permute-start.52 = (bf16[256,2816]{1,0:T(8,128)(2,1)}, bf16[256,2816]{1,0:T(8,128)(2,1)}, u32[]{:S(2)}, u32[]{:S(2)}) collective-permute-start(bf16[256,2816]{1,0:T(8,128)(2,1)} %add_convert_fusion.4), channel_id=1, source_target_pairs={{1,2},{2,1},{5,6},{6,5},{9,10},{10,9},{13,14},{14,13},{17,18},{18,... | collective-permute-start | bytes 4325384 | tf_op jit(solution)/shard_map/ppermute | solution.py:91
  600.8 41.9 %collective-permute-start.57 = (bf16[256,2816]{1,0:T(8,128)(2,1)S(1)}, bf16[256,2816]{1,0:T(8,128)(2,1)}, u32[]{:S(2)}, u32[]{:S(2)}) collective-permute-start(bf16[256,2816]{1,0:T(8,128)(2,1)S(1)} %add_convert_fusion.2), channel_id=1, source_target_pairs={{1,2},{2,1},{5,6},{6,5},{9,10},{10,9},{13,14},{14,13},{17,18},{18,... | collective-permute-start | bytes 4325384 | tf_op jit(solution)/shard_map/ppermute | solution.py:91
  (131 other events, 2151.7 us)
Sparse Core Ops, SparseCore 0:
  9.9 74.4 all-gather.2
  96.8 27.9 all-gather.4
  404.2 36.4 reduce-scatter.2
  473.7 76.8 reduce-scatter.4

commit v4 on v3

--- a/solution.py
+++ b/solution.py
@@ -89,15 +89,12 @@
     if cross is not None:
         part = live["p" + cross] = added(live["z" + cross], live["i" + cross])
         live["x" + cross] = lax.ppermute(part, "seq", across)
-        if x is not None:
-            x = after(x, part)
+        others = {k: v for k, v in live.items() if not k.endswith(cross)}
+        live.update(lax.optimization_barrier((others, part))[0])
     if x is not None:
         live["i" + new] = lax.ppermute(x, "seq", inward)
     if out is not None:
-        old = live["p" + out]
-        if part is not None:
-            old = after(old, part)
-        total = live["t" + out] = added(old, live["x" + out])
+        total = live["t" + out] = added(live["p" + out], live["x" + out])
         live["o" + out] = lax.ppermute(total, "seq", outward)
 
 
@@ -235,17 +232,36 @@
     values_t = kv_head(v_ref, kv).astype(f32).T.astype(bf16)
     q_t = q_ref[...].T
     cos, sin = cos_ref[...], sin_ref[...]
-    outs = []
-    for h in range(heads):
-        q_h = turned_t(q_t[h * HD : (h + 1) * HD], cos, sin).astype(bf16)
-        scores = jnp.dot(keys, q_h, preferred_element_type=f32) + bias_ref[...]
-        top = jnp.max(scores, axis=0, keepdims=True)
-        weights = jnp.exp2((scores - top) * scale2)
-        total = jnp.sum(weights, axis=0, keepdims=True)
-        probs = (weights * (1.0 / total)).astype(bf16)
-        outs.append(jnp.dot(values_t, probs, preferred_element_type=f32))
-        lse_ref[0, h : h + 1, :] = top * scale2 + jnp.log2(total)
-    o_ref[...] = jnp.concatenate(outs, 0).T.astype(bf16)
+    q_all = [
+        turned_t(q_t[h * HD : (h + 1) * HD], cos, sin).astype(bf16) for h in range(heads)
+    ]
+
+    key_size = jnp.max(jnp.sum(jnp.square(keys.astype(f32)), axis=1))
+    query_size = jnp.max(
+        sum(
+            jnp.sum(jnp.square(q.astype(f32)), axis=0, keepdims=True) for q in q_all
+        )
+    )
+    small = key_size * query_size * scale2**2 < 50.0**2
+
+    def run(shift):
+        outs = []
+        for h in range(heads):
+            scores = jnp.dot(keys, q_all[h], preferred_element_type=f32) + bias_ref[...]
+            if shift:
+                top = jnp.max(scores, axis=0, keepdims=True)
+                weights = jnp.exp2((scores - top) * scale2)
+            else:
+                weights = jnp.exp2(scores * scale2)
+            total = jnp.sum(weights, axis=0, keepdims=True)
+            out = jnp.dot(values_t, weights.astype(bf16), preferred_element_type=f32)
+            outs.append(out * (1.0 / total))
+            lse = jnp.log2(total)
+            lse_ref[0, h : h + 1, :] = lse + top * scale2 if shift else lse
+        o_ref[...] = jnp.concatenate(outs, 0).T.astype(bf16)
+
+    pl.when(small)(lambda: run(False))
+    pl.when(jnp.logical_not(small))(lambda: run(True))
 
 
 def attend_specs(n, rows, length):
@@ -290,7 +306,7 @@
 
 
 def attend_back_kernel(
-    heads, per_kv, info_ref, q_ref, k_ref, v_ref, g_ref, cos_ref, sin_ref, lse_ref,
+    heads, per_kv, info_ref, q_ref, k_ref, v_ref, g_ref, o_ref, cos_ref, sin_ref, lse_ref,
     dq_ref, dkv_ref, bias_ref, dk_ref, dv_ref,
 ):
     length, rows = k_ref.shape[0], q_ref.shape[0]
@@ -312,7 +328,9 @@
     keys, values = kv_head(k_ref, kv), kv_head(v_ref, kv)
     keys_t = keys.astype(f32).T.astype(bf16)
     q_t = q_ref[...].T
-    g_t = g_ref[...].astype(f32).T.astype(bf16)
+    g_t = g_ref[...].astype(f32).T
+    deltas = g_t * o_ref[...].astype(f32).T
+    g_t = g_t.astype(bf16)
     cos, sin = cos_ref[...], sin_ref[...]
     outs = []
     dk, dv = dk_ref[...], dv_ref[...]
@@ -322,7 +340,7 @@
         scores = jnp.dot(keys, q_h, preferred_element_type=f32) + bias_ref[...]
         weights = jnp.exp2(scores * scale2 - lse_ref[0, h : h + 1, :])
         grad_p = jnp.dot(values, g_h, preferred_element_type=f32)
-        delta = jnp.sum(grad_p * weights, axis=0, keepdims=True)
+        delta = jnp.sum(deltas[h * HD : (h + 1) * HD], axis=0, keepdims=True)
         grad_s = (weights * (grad_p - delta)).astype(bf16)
         grad_q = jnp.dot(keys_t, grad_s, preferred_element_type=f32) * scale
         outs.append(turned_t(grad_q.astype(bf16).astype(f32), cos, -sin))
@@ -338,12 +356,12 @@
         dkv_ref[...] = jnp.concatenate([dk * scale, dv], 1).astype(bf16)
 
 
-def attend_back(info, joined, all_kv, cos_t, sin_t, grads, lse):
+def attend_back(info, joined, all_kv, cos_t, sin_t, grads, outs, lse):
     n = lax.axis_size("fsdp")
     rows, length = joined.shape[0], all_kv.shape[0]
     heads, per_kv = HEADS // n, HEADS // KVH
     spec = attend_specs(n, rows, length)
-    names = ("plain", "keys", "values", "ordered", "table", "table", "lse")
+    names = ("plain", "keys", "values", "ordered", "ordered", "table", "table", "lse")
     return pl.pallas_call(
         functools.partial(attend_back_kernel, heads, per_kv),
         out_shape=(
@@ -370,7 +388,7 @@
             bytes_accessed=8 * rows * HEADS * HD,
             transcendentals=HEADS * rows * length,
         ),
-    )(info, joined, all_kv, all_kv, grads, cos_t, sin_t, lse)
+    )(info, joined, all_kv, all_kv, grads, outs, cos_t, sin_t, lse)
 
 
 def column_chunks(total, size=256):
@@ -764,21 +782,31 @@
     outs |= {k: send(outs[0], k) for k in near}
     firsts, seconds = live.pop("firsts"), live.pop("seconds")
     w_own = jnp.concatenate(sum([[firsts[k], seconds[k]] for k in near], [live.pop("own")]), 0)
-    fence(w_own=w_own, joined=joined, kv=all_kv, outs=outs)
+    firsts = {k: send(x, k) for k, x in live.pop("mine").items()}
+    fence(w_own=w_own, joined=joined, kv=all_kv, outs=outs, firsts=firsts)
 
     outs = live.pop("outs")
     outs |= two_hops(outs)
-    firsts = {k: send(x, k) for k, x in live.pop("mine").items()}
+    firsts = live.pop("firsts")
+    seconds = {k: other_half(k, firsts[k]) for k in rest}
     info = jnp.concatenate([(seq_at * rows).reshape(1), at_table]).astype(jnp.int32)
     attended, lse = attend(info, live["joined"], live["kv"], cos_t, sin_t)
-    fence(firsts=firsts, outs=outs, attended=attended, lse=lse, w_other=send(live["w_own"], 1))
-
-    outs, firsts = live.pop("outs"), live.pop("firsts")
+    fence(
+        firsts=firsts,
+        seconds=seconds,
+        outs=outs,
+        attended=attended,
+        lse=lse,
+        w_other=send(live["w_own"], 1),
+    )
+
+    outs, firsts, seconds = live.pop("outs"), live.pop("firsts"), live.pop("seconds")
     out_even = jnp.concatenate([whole_piece(outs[k]) for k in evens], 0)
     out_odd = send(out_even, 1)
     grads = {0: live["grad"]}
     grads |= {k: send(grads[0], k) for k in near}
-    seconds = {k: other_half(k, firsts[k]) for k in rest}
+    w_rest = sum([[firsts[k], seconds[k]] for k in rest], [])
+    w_rest = jnp.concatenate(w_rest or [live["w_own"]], 0)
     middle = dot(live["attended"][:, : q_width // 2], out_even)
     middle = live["hidden"].astype(f32) + (
         middle + dot(live["attended"][:, q_width // 2 :], out_odd)
@@ -787,8 +815,8 @@
     gain_two = live["gains"][1:].astype(f32)
     normed_two = (middle * factor_two * gain_two).astype(bf16)
     fence(
-        firsts=firsts,
-        seconds=seconds,
+        w_rest=w_rest,
+        w_rest_other=send(w_rest, 1),
         out_even=out_even,
         out_odd=out_odd,
         grads=grads,
@@ -813,10 +841,6 @@
             live[name] = live.get(name, {}) | dict(zip(group, new, strict=True))
 
     new = {k: send(live["tokens"][0], k) for k in near}
-    firsts, seconds = live.pop("firsts"), live.pop("seconds")
-    w_rest = sum([[firsts[k], seconds[k]] for k in rest], [])
-    live["w_rest"] = jnp.concatenate(w_rest or [live["w_own"]], 0)
-    live["w_rest_other"] = send(live["w_rest"], 1)
     ffn_of([0])
     live["tokens"] |= new
     fence()
@@ -903,7 +927,14 @@
     line_step(live, new="e", cross="d")
     sent = {k: send(live["ups"][k], k) for k in near}
     grad_queries, kv_parts = attend_back(
-        info, live["joined"], live["kv"], cos_t, sin_t, live["grad_attended"], live["lse"]
+        info,
+        live["joined"],
+        live["kv"],
+        cos_t,
+        sin_t,
+        live["grad_attended"],
+        live["attended"],
+        live["lse"],
     )
     fence(sent=sent, grad_queries=grad_queries, kv_parts=kv_parts)
     for k in ("grad_attended", "joined", "kv", "lse"):

time: 771 us -> 771 us (level)
  waiting for transfers between devices: 217 us -> 233 us
  starting transfers between devices: 140 us -> 127 us
    ppermute x39, waiting for transfers between devices: 65.1 us -> 95.9 us  [send(): return lax.ppermute(x, 'fsdp', [(i, i ^ k) for i in range(n)])]
    reduce_scatter x1, waiting for transfers between devices: 5.93 us -> 16.9 us  [on_device(): lax.psum_scatter(live.pop('kv_parts'), 'seq', scatter_dimension=0, tiled=...]
    ppermute x9, starting transfers between devices: 60.3 us -> 51.6 us  [line_step(): live['i' + new] = lax.ppermute(x, 'seq', inward)]
    all_gather x1, waiting for transfers between devices: 8.56 us -> 0.01 us  [on_device(): all_kv = lax.all_gather(keys_values, 'seq', axis=0, tiled=True)]
    unnamed x166 -> x184, local copies, waits for them, and re-layouts: 26.8 us -> 30.3 us
  transfers between devices with their start and end apart: 78 -> 78, of which waited for: 41 -> 35; matrix products, arithmetic and copies ran while one was open for 16% -> 16% of each run, Pallas kernels for 29% -> 28%
where the time goes in v4:
time: 771 us; the launch traced here: 763 us
  waiting for transfers between devices  233 us (30%)
  Pallas kernels  216 us (28%)
  starting transfers between devices  127 us (16%)
  other arithmetic  89.4 us (12%)
  local copies, waits for them, and re-layouts  48.3 us (6%)
  matrix products  32.8 us (4%)
  between operations  15.9 us (2%)
    ppermute x39, waiting for transfers between devices, send(): return lax.ppermute(x, 'fsdp', [(i, i ^ k) for i in range(n)])  95.9 us
    ppermute x9, waiting for transfers between devices, line_step(): live['o' + out] = lax.ppermute(total, 'seq', outward)  82.7 us
    pallas_call x3, Pallas kernels, ffn(): pl.pallas_call(functools.partial(ffn_kernel, n, count), out_shape=shapes,...  76.2 us
    ppermute x9, starting transfers between devices, line_step(): live['i' + new] = lax.ppermute(x, 'seq', inward)  51.6 us
    convert_element_type x23, other arithmetic, added(): return (one.astype(f32) + two.astype(f32)).astype(bf16)  41.6 us
    ppermute x39, starting transfers between devices, send(): return lax.ppermute(x, 'fsdp', [(i, i ^ k) for i in range(n)])  39.3 us
    pallas_call x1, Pallas kernels, attend(): pl.pallas_call(functools.partial(attend_kernel, heads, HEADS // KVH), out...  30.8 us
    unnamed x184, local copies, waits for them, and re-layouts  30.3 us
  transfers between devices with their start and end apart: 78, of which 35 were waited for; matrix products, arithmetic and copies ran while one was open for 16% of the time, Pallas kernels for 28%

profile of v4, /device:TPU:0, one launch (start us, length us, event | category | flops | bytes accessed | tf_op | source)
XLA Modules:
  0.0 762.9 jit_solution(4556510112542607179)
XLA Ops:
  35.5 17.5 %collective-permute-done.4 = bf16[128,2816]{1,0:T(8,128)(2,1)} collective-permute-done((bf16[128,2816]{1,0:T(8,128)(2,1)}, bf16[128,2816]{1,0:T(8,128)(2,1)}, u32[]{:S(2)}, u32[]{:S(2)}) %collective-permute-start.4) | collective-permute-done | bytes 720928 | tf_op jit(solution)/shard_map/ppermute | solution.py:26
  65.7 7.2 collective-permute-done.6
  72.9 14.2 %collective-permute-done.7 = bf16[128,2816]{1,0:T(8,128)(2,1)S(1)} collective-permute-done((bf16[128,2816]{1,0:T(8,128)(2,1)}, bf16[128,2816]{1,0:T(8,128)(2,1)S(1)}, u32[]{:S(2)}, u32[]{:S(2)}) %collective-permute-start.7) | collective-permute-done | bytes 720928 | tf_op jit(solution)/shard_map/ppermute | solution.py:51
  112.3 19.7 %collective-permute-done.8 = bf16[128,2816]{1,0:T(8,128)(2,1)} collective-permute-done((bf16[128,2816]{1,0:T(8,128)(2,1)}, bf16[128,2816]{1,0:T(8,128)(2,1)}, u32[]{:S(2)}, u32[]{:S(2)}) %collective-permute-start.8) | collective-permute-done | bytes 720928 | tf_op jit(solution)/shard_map/ppermute | solution.py:26
  139.5 30.8 %shard_map.167 = (bf16[256,2048]{1,0:T(8,128)(2,1)S(1)}, f32[8,4,256]{2,1,0:T(4,128)S(1)}) custom-call(s32[9]{0:T(128)S(1)} %get-tuple-element.1243.info_ref, f32[256,2048]{1,0:T(8,128)S(1)} %fusion.q_ref, bf16[1024,512]{1,0:T(8,128)(2,1)S(1)} %copy-done.20, bf16[1024,512]{1,0:T(8,128)(2,1)S(1)} %copy-done.20, f32[32,256]{1,0:T(8,128)S(1)} %get-tuple-element.1235.cos_ref, ...), custom_call_target="tpu_custom_call" | custom-call | flops 8589934592 | bytes 3145728 | tf_op jit(solution)/shard_map/pallas_call | solution.py:286
  187.7 11.5 %collective-permute-done.16.refs_3_.refs_6_ = bf16[256,2048]{1,0:T(8,128)(2,1)S(1)} collective-permute-done((bf16[256,2048]{1,0:T(8,128)(2,1)S(1)}, bf16[256,2048]{1,0:T(8,128)(2,1)S(1)}, u32[]{:S(2)}, u32[]{:S(2)}) %collective-permute-start.16) | collective-permute-done | bytes 1048608 | tf_op jit(solution)/shard_map/ppermute | solution.py:26
  203.9 21.5 %shard_map.168 = (bf16[1408,256]{1,0:T(8,128)(2,1)}, bf16[256,2816]{1,0:T(8,128)(2,1)}, bf16[256,2048]{1,0:T(8,128)(2,1)}, bf16[256,2048]{1,0:T(8,128)(2,1)}) custom-call(s32[4]{0:T(128)} %pad_add_fusion.4.info_ref, bf16[256,2048]{1,0:T(8,128)(2,1)} %get-tuple-element.843.refs_0_, bf16[256,2048]{1,0:T(8,128)(2,1)} %bitcast.47, ...), custom_call_target="tpu_custom_call" | custom-call | flops 8858370048 | bytes 17301504 | tf_op jit(solution)/shard_map/pallas_call | solution.py:493
  232.0 33.0 %shard_map.169 = (bf16[1408,256]{1,0:T(8,128)(2,1)}, bf16[1408,256]{1,0:T(8,128)(2,1)}, bf16[256,2816]{1,0:T(8,128)(2,1)}, bf16[256,2816]{1,0:T(8,128)(2,1)}, bf...) custom-call(s32[4]{0:T(128)} %pad_add_fusion.4.info_ref, ...), custom_call_target="tpu_custom_call" | custom-call | flops 17716740096 | bytes 17301504 | tf_op jit(solution)/shard_map/pallas_call | solution.py:493
  268.7 21.7 %shard_map.170 = (bf16[1408,256]{1,0:T(8,128)(2,1)}, bf16[256,2816]{1,0:T(8,128)(2,1)}, bf16[256,2048]{1,0:T(8,128)(2,1)}, bf16[256,2048]{1,0:T(8,128)(2,1)}) custom-call(s32[4]{0:T(128)} %pad_add_fusion.4.info_ref, bf16[256,2048]{1,0:T(8,128)(2,1)} %get-tuple-element.1249.refs_0_, bf16[256,2048]{1,0:T(8,128)(2,1)} %get-tuple-element.1250.refs_1_, ...), custom_call_target="tpu_custom_call" | custom-call | flops 8858370048 | bytes 17301504 | tf_op jit(solution)/shard_map/pallas_call | solution.py:493
  301.6 12.8 %shard_map.172 = bf16[1024,2816]{1,0:T(8,128)(2,1)} custom-call(s32[4]{0:T(128)S(1)} %get-tuple-element.799.info_ref, bf16[256,2048]{1,0:T(8,128)(2,1)} %get-tuple-element.843.refs_0_, bf16[256,2048]{1,0:T(8,128)(2,1)} %collective-permute-done.19.refs_0_.refs_1_, bf16[256,2048]{1,0:T(8,128)(2,1)S(1)} %copy-done.14, ...), custom_call_target="tpu_custom_call" | custom-call | flops 5905580032 | bytes 11534336 | tf_op jit(solution)/shard_map/pallas_call | solution.py:627
  343.8 15.1 %shard_map.174 = (bf16[256,2816]{1,0:T(8,128)(2,1)S(1)}, bf16[256,2816]{1,0:T(8,128)(2,1)}, bf16[256,2816]{1,0:T(8,128)(2,1)}, bf16[256,2816]{1,0:T(8,128)(2,1)}) custom-call(s32[4]{0:T(128)S(1)} %get-tuple-element.1244.info_ref, bf16[256,2048]{1,0:T(8,128)(2,1)} %get-tuple-element.843.refs_0_, bf16[256,2048]{1,0:T(8,128)(2,1)} %collective-permute-done.19.refs_0_.refs_1_, ...), custom_call_target="tpu_custom_call" | custom-call | flops 5905580032 | bytes 11534336 | tf_op jit(solution)/shard_map/pallas_call | solution.py:627
  362.3 8.3 %collective-permute-start.31 = (bf16[352,2048]{1,0:T(8,128)(2,1)S(1)}, bf16[352,2048]{1,0:T(8,128)(2,1)S(1)}, u32[]{:S(2)}, u32[]{:S(2)}) collective-permute-start(bf16[352,2048]{1,0:T(8,128)(2,1)S(1)} %get-tuple-element.923), channel_id=1, source_target_pairs={{0,1},{3,2},{4,5},{7,6},{8,9},{11,10},{12,13},{15,14},{16,17},{19,... | collective-permute-start | bytes 4325384 | tf_op jit(solution)/shard_map/ppermute | solution.py:95
  372.6 29.6 %shard_map.175 = (bf16[256,2048]{1,0:T(8,128)(2,1)S(1)}, bf16[1024,512]{1,0:T(8,128)(2,1)}) custom-call(s32[9]{0:T(128)S(1)} %get-tuple-element.1243.info_ref, f32[256,2048]{1,0:T(8,128)} %copy-done.22, bf16[1024,512]{1,0:T(8,128)(2,1)S(1)} %copy-done.21, bf16[1024,512]{1,0:T(8,128)(2,1)S(1)} %copy-done.21, bf16[256,2048]{1,0:T(8,128)(2,1)S(1)} %pad_maximum_fusion.6.g_ref, ...), custom_call_target="tpu_custom_call" | custom-call | flops 21474836480 | bytes 4194304 | tf_op jit(solution)/shard_map/pallas_call | solution.py:365
  434.5 16.9 %reduce-scatter.3.cloned.1.call-done = bf16[256,512]{1,0:T(8,128)(2,1)} async-done(((bf16[1024,512]{1,0:T(8,128)(2,1)}), bf16[256,512]{1,0:T(8,128)(2,1)}) %reduce-scatter.3.cloned.1.call-update) | async-done | bytes 262160 | tf_op jit(solution)/shard_map/reduce_scatter | solution.py:949
  473.2 7.4 collective-permute-start.40
  485.0 21.1 %collective-permute-done.41 = bf16[352,2048]{1,0:T(8,128)(2,1)} collective-permute-done((bf16[352,2048]{1,0:T(8,128)(2,1)S(1)}, bf16[352,2048]{1,0:T(8,128)(2,1)}, u32[]{:S(2)}, u32[]{:S(2)}) %collective-permute-start.41) | collective-permute-done | bytes 1441824 | tf_op jit(solution)/shard_map/ppermute | solution.py:98
  513.8 7.2 collective-permute-start.45
  537.3 11.8 %collective-permute-done.44 = bf16[128,2560]{1,0:T(8,128)(2,1)S(1)} collective-permute-done((bf16[128,2560]{1,0:T(8,128)(2,1)S(1)}, bf16[128,2560]{1,0:T(8,128)(2,1)S(1)}, u32[]{:S(2)}, u32[]{:S(2)}) %collective-permute-start.44) | collective-permute-done | bytes 655392 | tf_op jit(solution)/shard_map/ppermute | solution.py:26
  584.2 9.4 %collective-permute-done.50 = bf16[256,2560]{1,0:T(8,128)(2,1)} collective-permute-done((bf16[256,2560]{1,0:T(8,128)(2,1)}, bf16[256,2560]{1,0:T(8,128)(2,1)}, u32[]{:S(2)}, u32[]{:S(2)}) %collective-permute-start.50) | collective-permute-done | bytes 1310752 | tf_op jit(solution)/shard_map/ppermute | solution.py:26
  624.8 19.9 %collective-permute-done.56.got_ref = bf16[256,2816]{1,0:T(8,128)(2,1)} collective-permute-done((bf16[256,2816]{1,0:T(8,128)(2,1)S(1)}, bf16[256,2816]{1,0:T(8,128)(2,1)}, u32[]{:S(2)}, u32[]{:S(2)}) %collective-permute-start.56) | collective-permute-done | bytes 1441824 | tf_op jit(solution)/shard_map/ppermute | solution.py:98
  658.8 7.6 collective-permute-start.58
  687.8 9.1 %collective-permute-start.66 = (bf16[128,2560]{1,0:T(8,128)(2,1)S(1)}, bf16[128,2560]{1,0:T(8,128)(2,1)}, u32[]{:S(2)}, u32[]{:S(2)}) collective-permute-start(bf16[128,2560]{1,0:T(8,128)(2,1)S(1)} %get-tuple-element.1189), channel_id=1, source_target_pairs={{0,1},{3,2},{4,5},{7,6},{8,9},{11,10},{12,13},{15,14},{16,17},{19,... | collective-permute-start | bytes 1966088 | tf_op jit(solution)/shard_map/ppermute | solution.py:95
  718.4 13.5 %collective-permute-done.69 = bf16[128,2560]{1,0:T(8,128)(2,1)S(1)} collective-permute-done((bf16[128,2560]{1,0:T(8,128)(2,1)S(1)}, bf16[128,2560]{1,0:T(8,128)(2,1)S(1)}, u32[]{:S(2)}, u32[]{:S(2)}) %collective-permute-start.69) | collective-permute-done | bytes 655392 | tf_op jit(solution)/shard_map/ppermute | solution.py:98
  743.7 10.3 %collective-permute-done.73 = bf16[128,2560]{1,0:T(8,128)(2,1)S(1)} collective-permute-done((bf16[128,2560]{1,0:T(8,128)(2,1)S(1)}, bf16[128,2560]{1,0:T(8,128)(2,1)S(1)}, u32[]{:S(2)}, u32[]{:S(2)}) %collective-permute-start.73) | collective-permute-done | bytes 655392 | tf_op jit(solution)/shard_map/ppermute | solution.py:98
  (473 shorter events, 369.8 us)
Async XLA Ops:
  7.2 79.9 %all-gather.3.cloned.1.call-start = ((), (), s32[]{:S(2)}) async-start(), calls=%async_computation.2 | async-start | bytes 11796480 | tf_op jit(solution)/shard_map/all_gather | solution.py:740
  7.9 124.1 %all-gather.5.cloned.1.call-start = ((), (), s32[]{:S(2)}) async-start(), calls=%async_computation.3 | async-start | bytes 1310720 | tf_op jit(solution)/shard_map/all_gather | solution.py:779
  91.0 41.0 %collective-permute-start.10 = (bf16[256,2048]{1,0:T(8,128)(2,1)}, bf16[256,2048]{1,0:T(8,128)(2,1)}, u32[]{:S(2)}, u32[]{:S(2)}) collective-permute-start(bf16[256,2048]{1,0:T(8,128)(2,1)} %param.13), channel_id=1, source_target_pairs={{0,16},{4,20},{8,24},{12,28},{16,0},{20,4},{24,8},{28,12},{1,17},{... | collective-permute-start | bytes 3145736 | tf_op jit(solution)/shard_map/ppermute | solution.py:26
  92.1 40.0 %collective-permute-start.9 = (bf16[256,2048]{1,0:T(8,128)(2,1)}, bf16[256,2048]{1,0:T(8,128)(2,1)}, u32[]{:S(2)}, u32[]{:S(2)}) collective-permute-start(bf16[256,2048]{1,0:T(8,128)(2,1)} %param.13), channel_id=1, source_target_pairs={{0,8},{4,12},{8,0},{12,4},{16,24},{20,28},{24,16},{28,20},{1,9},{5... | collective-permute-start | bytes 3145736 | tf_op jit(solution)/shard_map/ppermute | solution.py:26
  96.7 354.7 %reduce-scatter.3.cloned.1.call-start = ((), (), s32[]{:S(2)}) async-start(), calls=%async_computation.4 | async-start | bytes 1310720 | tf_op jit(solution)/shard_map/reduce_scatter | solution.py:949
  96.7 35.3 %collective-permute-start.8 = (bf16[128,2816]{1,0:T(8,128)(2,1)}, bf16[128,2816]{1,0:T(8,128)(2,1)}, u32[]{:S(2)}, u32[]{:S(2)}) collective-permute-start(bf16[128,2816]{1,0:T(8,128)(2,1)} %shard_map.164), channel_id=1, source_target_pairs={{0,24},{4,28},{8,16},{12,20},{16,8},{20,12},{24,0},{28,4},{1,25},{... | collective-permute-start | bytes 2162696 | tf_op jit(solution)/shard_map/ppermute | solution.py:26
  132.1 38.3 %collective-permute-start.14 = (bf16[768,2816]{1,0:T(8,128)(2,1)}, bf16[768,2816]{1,0:T(8,128)(2,1)}, u32[]{:S(2)}, u32[]{:S(2)}) collective-permute-start(bf16[768,2816]{1,0:T(8,128)(2,1)} %constant_dynamic-update-slice_fusion.refs_2_.refs_4_), channel_id=1, source_target_pairs={{0,4},{4,0},{8,12},{12,8},{16,20},{20,16},{24,28},{28,24},{1,5},{5... | collective-permute-start | bytes 12976136 | tf_op jit(solution)/shard_map/ppermute | solution.py:26
  227.8 37.1 %collective-permute-start.21 = (bf16[128,2048]{1,0:T(8,128)(2,1)S(1)}, bf16[128,2048]{1,0:T(8,128)(2,1)S(1)}, u32[]{:S(2)}, u32[]{:S(2)}) collective-permute-start(bf16[128,2048]{1,0:T(8,128)(2,1)S(1)} %slice.156), channel_id=1, source_target_pairs={{0,8},{4,12},{8,0},{12,4},{16,24},{20,28},{24,16},{28,20},{1,9},{5... | collective-permute-start | bytes 1572872 | tf_op jit(solution)/shard_map/ppermute | solution.py:26
  229.0 35.9 %collective-permute-start.22 = (bf16[128,2048]{1,0:T(8,128)(2,1)S(1)}, bf16[128,2048]{1,0:T(8,128)(2,1)S(1)}, u32[]{:S(2)}, u32[]{:S(2)}) collective-permute-start(bf16[128,2048]{1,0:T(8,128)(2,1)S(1)} %slice.157), channel_id=1, source_target_pairs={{0,16},{4,20},{8,24},{12,28},{16,0},{20,4},{24,8},{28,12},{1,17},{... | collective-permute-start | bytes 1572872 | tf_op jit(solution)/shard_map/ppermute | solution.py:26
  361.4 43.0 %collective-permute-start.34 = (bf16[352,2048]{1,0:T(8,128)(2,1)S(1)}, bf16[352,2048]{1,0:T(8,128)(2,1)S(1)}, u32[]{:S(2)}, u32[]{:S(2)}) collective-permute-start(bf16[352,2048]{1,0:T(8,128)(2,1)S(1)} %add_convert_fusion.11), channel_id=1, source_target_pairs={{1,2},{2,1},{5,6},{6,5},{9,10},{10,9},{13,14},{14,13},{17,18},{18,... | collective-permute-start | bytes 4325384 | tf_op jit(solution)/shard_map/ppermute | solution.py:91
  362.3 42.1 %collective-permute-start.31 = (bf16[352,2048]{1,0:T(8,128)(2,1)S(1)}, bf16[352,2048]{1,0:T(8,128)(2,1)S(1)}, u32[]{:S(2)}, u32[]{:S(2)}) collective-permute-start(bf16[352,2048]{1,0:T(8,128)(2,1)S(1)} %get-tuple-element.923), channel_id=1, source_target_pairs={{0,1},{3,2},{4,5},{7,6},{8,9},{11,10},{12,13},{15,14},{16,17},{19,... | collective-permute-start | bytes 4325384 | tf_op jit(solution)/shard_map/ppermute | solution.py:95
  410.6 192.5 %reduce-scatter.5.cloned.1.call-start = ((), (), s32[]{:S(2)}) async-start(), calls=%async_computation.5 | async-start | bytes 9437184 | tf_op jit(solution)/shard_map/reduce_scatter | solution.py:974
  410.6 55.7 %collective-permute-start.38 = (bf16[352,2048]{1,0:T(8,128)(2,1)}, bf16[352,2048]{1,0:T(8,128)(2,1)}, u32[]{:S(2)}, u32[]{:S(2)}) collective-permute-start(bf16[352,2048]{1,0:T(8,128)(2,1)} %add_convert_fusion.10), channel_id=1, source_target_pairs={{1,2},{2,1},{5,6},{6,5},{9,10},{10,9},{13,14},{14,13},{17,18},{18,... | collective-permute-start | bytes 4325384 | tf_op jit(solution)/shard_map/ppermute | solution.py:91
  412.4 53.9 %collective-permute-start.35 = (bf16[256,2816]{1,0:T(8,128)(2,1)S(1)}, bf16[256,2816]{1,0:T(8,128)(2,1)}, u32[]{:S(2)}, u32[]{:S(2)}) collective-permute-start(bf16[256,2816]{1,0:T(8,128)(2,1)S(1)} %get-tuple-element.969), channel_id=1, source_target_pairs={{0,1},{3,2},{4,5},{7,6},{8,9},{11,10},{12,13},{15,14},{16,17},{19,... | collective-permute-start | bytes 4325384 | tf_op jit(solution)/shard_map/ppermute | solution.py:95
  419.1 47.2 %collective-permute-start.36 = (bf16[352,2048]{1,0:T(8,128)(2,1)}, bf16[352,2048]{1,0:T(8,128)(2,1)}, u32[]{:S(2)}, u32[]{:S(2)}) collective-permute-start(bf16[352,2048]{1,0:T(8,128)(2,1)} %add_convert_fusion.9), channel_id=1, source_target_pairs={{1,0},{2,3},{5,4},{6,7},{9,8},{10,11},{13,12},{14,15},{17,16},{18,... | collective-permute-start | bytes 4325384 | tf_op jit(solution)/shard_map/ppermute | solution.py:98
  420.4 45.9 %collective-permute-start.37 = (bf16[256,2816]{1,0:T(8,128)(2,1)}, bf16[256,2816]{1,0:T(8,128)(2,1)}, u32[]{:S(2)}, u32[]{:S(2)}) collective-permute-start(bf16[256,2816]{1,0:T(8,128)(2,1)} %get-tuple-element.943), channel_id=1, source_target_pairs={{0,24},{4,28},{8,16},{12,20},{16,8},{20,12},{24,0},{28,4},{1,25},{... | collective-permute-start | bytes 4325384 | tf_op jit(solution)/shard_map/ppermute | solution.py:26
  468.2 42.7 %collective-permute-start.39 = (bf16[1024,2560]{1,0:T(8,128)(2,1)}, bf16[1024,2560]{1,0:T(8,128)(2,1)}, u32[]{:S(2)}, u32[]{:S(2)}) collective-permute-start(bf16[1024,2560]{1,0:T(8,128)(2,1)} %convolution_convert_fusion.2), channel_id=1, source_target_pairs={{0,4},{4,0},{8,12},{12,8},{16,20},{20,16},{24,28},{28,24},{1,5},{5... | collective-permute-start | bytes 15728648 | tf_op jit(solution)/shard_map/ppermute | solution.py:26
  470.2 35.9 %collective-permute-start.41 = (bf16[352,2048]{1,0:T(8,128)(2,1)S(1)}, bf16[352,2048]{1,0:T(8,128)(2,1)}, u32[]{:S(2)}, u32[]{:S(2)}) collective-permute-start(bf16[352,2048]{1,0:T(8,128)(2,1)S(1)} %add_convert_fusion.7), channel_id=1, source_target_pairs={{1,0},{2,3},{5,4},{6,7},{9,8},{10,11},{13,12},{14,15},{17,16},{18,... | collective-permute-start | bytes 4325384 | tf_op jit(solution)/shard_map/ppermute | solution.py:98
  473.2 37.6 %collective-permute-start.40 = (bf16[256,2816]{1,0:T(8,128)(2,1)}, bf16[256,2816]{1,0:T(8,128)(2,1)}, u32[]{:S(2)}, u32[]{:S(2)}) collective-permute-start(bf16[256,2816]{1,0:T(8,128)(2,1)} %collective-permute-done.32), channel_id=1, source_target_pairs={{0,1},{3,2},{4,5},{7,6},{8,9},{11,10},{12,13},{15,14},{16,17},{19,... | collective-permute-start | bytes 4325384 | tf_op jit(solution)/shard_map/ppermute | solution.py:95
  513.0 43.8 %collective-permute-start.47 = (bf16[256,2816]{1,0:T(8,128)(2,1)S(1)}, bf16[256,2816]{1,0:T(8,128)(2,1)S(1)}, u32[]{:S(2)}, u32[]{:S(2)}) collective-permute-start(bf16[256,2816]{1,0:T(8,128)(2,1)S(1)} %add_convert_fusion.6), channel_id=1, source_target_pairs={{1,2},{2,1},{5,6},{6,5},{9,10},{10,9},{13,14},{14,13},{17,18},{18,... | collective-permute-start | bytes 4325384 | tf_op jit(solution)/shard_map/ppermute | solution.py:91
  513.8 43.1 %collective-permute-start.45 = (bf16[256,2816]{1,0:T(8,128)(2,1)S(1)}, bf16[256,2816]{1,0:T(8,128)(2,1)S(1)}, u32[]{:S(2)}, u32[]{:S(2)}) collective-permute-start(bf16[256,2816]{1,0:T(8,128)(2,1)S(1)} %copy-done.56), channel_id=1, source_target_pairs={{0,1},{3,2},{4,5},{7,6},{8,9},{11,10},{12,13},{15,14},{16,17},{19,... | collective-permute-start | bytes 4325384 | tf_op jit(solution)/shard_map/ppermute | solution.py:95
  558.4 44.7 %collective-permute-start.52 = (bf16[256,2816]{1,0:T(8,128)(2,1)}, bf16[256,2816]{1,0:T(8,128)(2,1)}, u32[]{:S(2)}, u32[]{:S(2)}) collective-permute-start(bf16[256,2816]{1,0:T(8,128)(2,1)} %add_convert_fusion.4), channel_id=1, source_target_pairs={{1,2},{2,1},{5,6},{6,5},{9,10},{10,9},{13,14},{14,13},{17,18},{18,... | collective-permute-start | bytes 4325384 | tf_op jit(solution)/shard_map/ppermute | solution.py:91
  560.3 42.8 %collective-permute-start.48 = (bf16[256,2816]{1,0:T(8,128)(2,1)}, bf16[256,2816]{1,0:T(8,128)(2,1)}, u32[]{:S(2)}, u32[]{:S(2)}) collective-permute-start(bf16[256,2816]{1,0:T(8,128)(2,1)} %collective-permute-done.37), channel_id=1, source_target_pairs={{0,1},{3,2},{4,5},{7,6},{8,9},{11,10},{12,13},{15,14},{16,17},{19,... | collective-permute-start | bytes 4325384 | tf_op jit(solution)/shard_map/ppermute | solution.py:95
  607.6 37.1 %collective-permute-start.57 = (bf16[256,2816]{1,0:T(8,128)(2,1)S(1)}, bf16[256,2816]{1,0:T(8,128)(2,1)}, u32[]{:S(2)}, u32[]{:S(2)}) collective-permute-start(bf16[256,2816]{1,0:T(8,128)(2,1)S(1)} %add_convert_fusion.2), channel_id=1, source_target_pairs={{1,2},{2,1},{5,6},{6,5},{9,10},{10,9},{13,14},{14,13},{17,18},{18,... | collective-permute-start | bytes 4325384 | tf_op jit(solution)/shard_map/ppermute | solution.py:91
  (140 other events, 2282.0 us)
Sparse Core Ops, SparseCore 0:
  9.9 74.4 all-gather.2
  96.8 27.9 all-gather.4
  410.7 40.6 reduce-scatter.2
  480.8 76.5 reduce-scatter.4

commit v5 on v4

--- a/solution.py
+++ b/solution.py
@@ -242,7 +242,7 @@
             jnp.sum(jnp.square(q.astype(f32)), axis=0, keepdims=True) for q in q_all
         )
     )
-    small = key_size * query_size * scale2**2 < 50.0**2
+    small = key_size * query_size * scale2**2 < 80.0**2
 
     def run(shift):
         outs = []
@@ -1013,13 +1013,13 @@
     line_step(live, new="out", cross=names[3], out=names[2])
     gate_up_sums = placed_in(live.pop("sums"), evens[1])
     total = total_of(live.pop("parts_qkv"), live.pop("far_qkv"), live.pop("near_qkv")).astype(bf16)
-    fence(far=far_sends(live["parts"]), sums=gate_up_sums, zq=total[:half], zr=total[half:])
+    fence(far=far_sends(live["parts"]), sums=gate_up_sums, zq=total)
 
     line_step(live, new="q", cross="out", out=names[3])
     gate_up_sums = placed_in(live.pop("sums"), evens[2])
     fence(near=near_sends(live["parts"], live["far"]), sums=gate_up_sums)
 
-    line_step(live, new="r", cross="q", out="out")
+    line_step(live, cross="q", out="out")
     gate_up_sums = live.pop("sums")
     for k in evens[3:]:
         gate_up_sums = placed_in(gate_up_sums, k)
@@ -1028,19 +1028,17 @@
     out = (live["middle"] + out).astype(bf16)
     fence(sums=gate_up_sums, grad_gains=grad_gains, out_final=out)
 
-    line_step(live, cross="r", out="q")
-    fence(out_sums=summed("out"))
-
-    line_step(live, out="r")
+    line_step(live, out="q")
+    out_sums = summed("out")
     grad_gains = small_sum(live.pop("grad_gains"), "seq")
-    qkv_sums = jnp.concatenate([summed("q"), summed("r")], 0)
+    qkv_sums = summed("q")
     grad_gains = lax.dynamic_slice_in_dim(grad_gains, me * block, block, 1)
     return (
         live["out_final"].reshape(hidden_in.shape),
         live["grad_input"].reshape(hidden_in.shape),
         grad_gains[0],
         qkv_sums,
-        live["out_sums"],
+        out_sums,
         grad_gains[1],
         live["sums"],
         live["down_sums"],

time: 771 us -> 751 us (0.974)
  starting transfers between devices: 127 us -> 119 us
    ppermute x9 -> x8, waiting for transfers between devices: 82.7 us -> 45.3 us  [line_step(): live['o' + out] = lax.ppermute(total, 'seq', outward)]
    ppermute x5, waiting for transfers between devices: 4.01 us -> 28.1 us  [small_sum(): x = x + lax.ppermute(x, axis, [(i, i ^ k) for i in range(n)])]
    ppermute x39, waiting for transfers between devices: 95.9 us -> 110 us  [send(): return lax.ppermute(x, 'fsdp', [(i, i ^ k) for i in range(n)])]
    pallas_call x1, Pallas kernels: 30.8 us -> 23 us  [attend(): pl.pallas_call(functools.partial(attend_kernel, heads, HEADS // KVH), out...]
    convert_element_type x23 -> x21, other arithmetic: 41.6 us -> 38.1 us  [added(): return (one.astype(f32) + two.astype(f32)).astype(bf16)]
    ppermute x9 -> x8, starting transfers between devices: 51.6 us -> 48.8 us  [line_step(): live['i' + new] = lax.ppermute(x, 'seq', inward)]
  transfers between devices with their start and end apart: 78 -> 75, of which waited for: 35 -> 38; matrix products, arithmetic and copies ran while one was open for 16% -> 17% of each run, Pallas kernels for 28% -> 27%
where the time goes in v5:
time: 751 us; the launch traced here: 744 us
  waiting for transfers between devices  234 us (31%)
  Pallas kernels  209 us (28%)
  starting transfers between devices  119 us (16%)
  other arithmetic  85.8 us (11%)
  local copies, waits for them, and re-layouts  46.9 us (6%)
  matrix products  32.7 us (4%)
  between operations  15.8 us (2%)
    ppermute x39, waiting for transfers between devices, send(): return lax.ppermute(x, 'fsdp', [(i, i ^ k) for i in range(n)])  110 us
    pallas_call x3, Pallas kernels, ffn(): pl.pallas_call(functools.partial(ffn_kernel, n, count), out_shape=shapes,...  76.2 us
    ppermute x8, starting transfers between devices, line_step(): live['i' + new] = lax.ppermute(x, 'seq', inward)  48.8 us
    ppermute x8, waiting for transfers between devices, line_step(): live['o' + out] = lax.ppermute(total, 'seq', outward)  45.3 us
    ppermute x39, starting transfers between devices, send(): return lax.ppermute(x, 'fsdp', [(i, i ^ k) for i in range(n)])  38.9 us
    convert_element_type x21, other arithmetic, added(): return (one.astype(f32) + two.astype(f32)).astype(bf16)  38.1 us
    unnamed x184, local copies, waits for them, and re-layouts  31.2 us
    pallas_call x1, Pallas kernels, attend_back(): pl.pallas_call(functools.partial(attend_back_kernel, heads, per_kv), out_...  29.6 us
  transfers between devices with their start and end apart: 75, of which 38 were waited for; matrix products, arithmetic and copies ran while one was open for 17% of the time, Pallas kernels for 27%

profile of v5, /device:TPU:0, one launch (start us, length us, event | category | flops | bytes accessed | tf_op | source)
XLA Modules:
  0.0 743.8 jit_solution(13786316206517704133)
XLA Ops:
  35.5 17.5 %collective-permute-done.4 = bf16[128,2816]{1,0:T(8,128)(2,1)} collective-permute-done((bf16[128,2816]{1,0:T(8,128)(2,1)}, bf16[128,2816]{1,0:T(8,128)(2,1)}, u32[]{:S(2)}, u32[]{:S(2)}) %collective-permute-start.4) | collective-permute-done | bytes 720928 | tf_op jit(solution)/shard_map/ppermute | solution.py:26
  65.7 7.1 collective-permute-done.6
  72.9 14.2 %collective-permute-done.7 = bf16[128,2816]{1,0:T(8,128)(2,1)S(1)} collective-permute-done((bf16[128,2816]{1,0:T(8,128)(2,1)}, bf16[128,2816]{1,0:T(8,128)(2,1)S(1)}, u32[]{:S(2)}, u32[]{:S(2)}) %collective-permute-start.7) | collective-permute-done | bytes 720928 | tf_op jit(solution)/shard_map/ppermute | solution.py:51
  112.3 19.7 %collective-permute-done.8 = bf16[128,2816]{1,0:T(8,128)(2,1)} collective-permute-done((bf16[128,2816]{1,0:T(8,128)(2,1)}, bf16[128,2816]{1,0:T(8,128)(2,1)}, u32[]{:S(2)}, u32[]{:S(2)}) %collective-permute-start.8) | collective-permute-done | bytes 720928 | tf_op jit(solution)/shard_map/ppermute | solution.py:26
  139.4 23.0 %shard_map.167 = (bf16[256,2048]{1,0:T(8,128)(2,1)S(1)}, f32[8,4,256]{2,1,0:T(4,128)S(1)}) custom-call(s32[9]{0:T(128)S(1)} %get-tuple-element.1183.info_ref, f32[256,2048]{1,0:T(8,128)S(1)} %fusion.q_ref, bf16[1024,512]{1,0:T(8,128)(2,1)S(1)} %copy-done.20, bf16[1024,512]{1,0:T(8,128)(2,1)S(1)} %copy-done.20, f32[32,256]{1,0:T(8,128)S(1)} %get-tuple-element.1175.cos_ref, ...), custom_call_target="tpu_custom_call" | custom-call | flops 8589934592 | bytes 3145728 | tf_op jit(solution)/shard_map/pallas_call | solution.py:286
  179.8 11.5 %collective-permute-done.16.refs_3_.refs_6_ = bf16[256,2048]{1,0:T(8,128)(2,1)S(1)} collective-permute-done((bf16[256,2048]{1,0:T(8,128)(2,1)S(1)}, bf16[256,2048]{1,0:T(8,128)(2,1)S(1)}, u32[]{:S(2)}, u32[]{:S(2)}) %collective-permute-start.16) | collective-permute-done | bytes 1048608 | tf_op jit(solution)/shard_map/ppermute | solution.py:26
  196.0 21.5 %shard_map.168 = (bf16[1408,256]{1,0:T(8,128)(2,1)}, bf16[256,2816]{1,0:T(8,128)(2,1)}, bf16[256,2048]{1,0:T(8,128)(2,1)}, bf16[256,2048]{1,0:T(8,128)(2,1)}) custom-call(s32[4]{0:T(128)} %pad_add_fusion.4.info_ref, bf16[256,2048]{1,0:T(8,128)(2,1)} %get-tuple-element.814.refs_0_, bf16[256,2048]{1,0:T(8,128)(2,1)} %bitcast.47, ...), custom_call_target="tpu_custom_call" | custom-call | flops 8858370048 | bytes 17301504 | tf_op jit(solution)/shard_map/pallas_call | solution.py:493
  224.1 33.0 %shard_map.169 = (bf16[1408,256]{1,0:T(8,128)(2,1)}, bf16[1408,256]{1,0:T(8,128)(2,1)}, bf16[256,2816]{1,0:T(8,128)(2,1)}, bf16[256,2816]{1,0:T(8,128)(2,1)}, bf...) custom-call(s32[4]{0:T(128)} %pad_add_fusion.4.info_ref, ...), custom_call_target="tpu_custom_call" | custom-call | flops 17716740096 | bytes 17301504 | tf_op jit(solution)/shard_map/pallas_call | solution.py:493
  260.8 21.7 %shard_map.170 = (bf16[1408,256]{1,0:T(8,128)(2,1)}, bf16[256,2816]{1,0:T(8,128)(2,1)}, bf16[256,2048]{1,0:T(8,128)(2,1)}, bf16[256,2048]{1,0:T(8,128)(2,1)}) custom-call(s32[4]{0:T(128)} %pad_add_fusion.4.info_ref, bf16[256,2048]{1,0:T(8,128)(2,1)} %get-tuple-element.1189.refs_0_, bf16[256,2048]{1,0:T(8,128)(2,1)} %get-tuple-element.1190.refs_1_, ...), custom_call_target="tpu_custom_call" | custom-call | flops 8858370048 | bytes 17301504 | tf_op jit(solution)/shard_map/pallas_call | solution.py:493
  293.8 12.8 %shard_map.172 = bf16[1024,2816]{1,0:T(8,128)(2,1)} custom-call(s32[4]{0:T(128)S(1)} %get-tuple-element.770.info_ref, bf16[256,2048]{1,0:T(8,128)(2,1)} %get-tuple-element.814.refs_0_, bf16[256,2048]{1,0:T(8,128)(2,1)} %collective-permute-done.19.refs_0_.refs_1_, bf16[256,2048]{1,0:T(8,128)(2,1)S(1)} %copy-done.14, ...), custom_call_target="tpu_custom_call" | custom-call | flops 5905580032 | bytes 11534336 | tf_op jit(solution)/shard_map/pallas_call | solution.py:627
  336.0 15.1 %shard_map.174 = (bf16[256,2816]{1,0:T(8,128)(2,1)S(1)}, bf16[256,2816]{1,0:T(8,128)(2,1)}, bf16[256,2816]{1,0:T(8,128)(2,1)}, bf16[256,2816]{1,0:T(8,128)(2,1)}) custom-call(s32[4]{0:T(128)S(1)} %get-tuple-element.1184.info_ref, bf16[256,2048]{1,0:T(8,128)(2,1)} %get-tuple-element.814.refs_0_, bf16[256,2048]{1,0:T(8,128)(2,1)} %collective-permute-done.19.refs_0_.refs_1_, ...), custom_call_target="tpu_custom_call" | custom-call | flops 5905580032 | bytes 11534336 | tf_op jit(solution)/shard_map/pallas_call | solution.py:627
  354.4 8.3 %collective-permute-start.31 = (bf16[352,2048]{1,0:T(8,128)(2,1)S(1)}, bf16[352,2048]{1,0:T(8,128)(2,1)S(1)}, u32[]{:S(2)}, u32[]{:S(2)}) collective-permute-start(bf16[352,2048]{1,0:T(8,128)(2,1)S(1)} %get-tuple-element.892), channel_id=1, source_target_pairs={{0,1},{3,2},{4,5},{7,6},{8,9},{11,10},{12,13},{15,14},{16,17},{19,... | collective-permute-start | bytes 4325384 | tf_op jit(solution)/shard_map/ppermute | solution.py:95
  364.8 29.6 %shard_map.175 = (bf16[256,2048]{1,0:T(8,128)(2,1)S(1)}, bf16[1024,512]{1,0:T(8,128)(2,1)}) custom-call(s32[9]{0:T(128)S(1)} %get-tuple-element.1183.info_ref, f32[256,2048]{1,0:T(8,128)} %copy-done.22, bf16[1024,512]{1,0:T(8,128)(2,1)S(1)} %copy-done.21, bf16[1024,512]{1,0:T(8,128)(2,1)S(1)} %copy-done.21, bf16[256,2048]{1,0:T(8,128)(2,1)S(1)} %pad_maximum_fusion.6.g_ref, ...), custom_call_target="tpu_custom_call" | custom-call | flops 21474836480 | bytes 4194304 | tf_op jit(solution)/shard_map/pallas_call | solution.py:365
  419.7 6.9 convolution_convert_fusion
  426.7 17.0 %reduce-scatter.3.cloned.1.call-done = bf16[256,512]{1,0:T(8,128)(2,1)} async-done(((bf16[1024,512]{1,0:T(8,128)(2,1)}), bf16[256,512]{1,0:T(8,128)(2,1)}) %reduce-scatter.3.cloned.1.call-update) | async-done | bytes 262160 | tf_op jit(solution)/shard_map/reduce_scatter | solution.py:949
  465.5 7.4 collective-permute-start.40
  476.6 21.7 %collective-permute-done.41 = bf16[352,2048]{1,0:T(8,128)(2,1)} collective-permute-done((bf16[352,2048]{1,0:T(8,128)(2,1)S(1)}, bf16[352,2048]{1,0:T(8,128)(2,1)}, u32[]{:S(2)}, u32[]{:S(2)}) %collective-permute-start.41) | collective-permute-done | bytes 1441824 | tf_op jit(solution)/shard_map/ppermute | solution.py:98
  506.0 7.2 collective-permute-start.45
  529.6 11.9 %collective-permute-done.44 = bf16[128,2560]{1,0:T(8,128)(2,1)S(1)} collective-permute-done((bf16[128,2560]{1,0:T(8,128)(2,1)S(1)}, bf16[128,2560]{1,0:T(8,128)(2,1)S(1)}, u32[]{:S(2)}, u32[]{:S(2)}) %collective-permute-start.44) | collective-permute-done | bytes 655392 | tf_op jit(solution)/shard_map/ppermute | solution.py:26
  576.3 9.4 %collective-permute-done.50 = bf16[256,2560]{1,0:T(8,128)(2,1)} collective-permute-done((bf16[256,2560]{1,0:T(8,128)(2,1)}, bf16[256,2560]{1,0:T(8,128)(2,1)}, u32[]{:S(2)}, u32[]{:S(2)}) %collective-permute-start.50) | collective-permute-done | bytes 1310752 | tf_op jit(solution)/shard_map/ppermute | solution.py:26
  603.3 8.4 %collective-permute-start.55 = (bf16[256,2048]{1,0:T(8,128)(2,1)}, bf16[256,2048]{1,0:T(8,128)(2,1)}, u32[]{:S(2)}, u32[]{:S(2)}) collective-permute-start(bf16[256,2048]{1,0:T(8,128)(2,1)} %reduce-scatter.5.cloned.1.call-done), channel_id=1, source_target_pairs={{0,1},{3,2},{4,5},{7,6},{8,9},{11,10},{12,13},{15,14},{16,17},{19,... | collective-permute-start | bytes 3145736 | tf_op jit(solution)/shard_map/ppermute | solution.py:95
  630.4 8.1 %collective-permute-start.58 = (bf16[256,2560]{1,0:T(8,128)(2,1)}, bf16[256,2560]{1,0:T(8,128)(2,1)}, u32[]{:S(2)}, u32[]{:S(2)}) collective-permute-start(bf16[256,2560]{1,0:T(8,128)(2,1)} %add_convert_fusion.14), channel_id=1, source_target_pairs={{0,1},{3,2},{4,5},{7,6},{8,9},{11,10},{12,13},{15,14},{16,17},{19,... | collective-permute-start | bytes 3932168 | tf_op jit(solution)/shard_map/ppermute | solution.py:95
  654.9 11.6 %collective-permute-done.60 = bf16[256,2048]{1,0:T(8,128)(2,1)} collective-permute-done((bf16[256,2048]{1,0:T(8,128)(2,1)}, bf16[256,2048]{1,0:T(8,128)(2,1)}, u32[]{:S(2)}, u32[]{:S(2)}) %collective-permute-start.60) | collective-permute-done | bytes 1048608 | tf_op jit(solution)/shard_map/ppermute | solution.py:26
  706.5 23.3 %collective-permute-done.68 = f32[2,2048]{1,0:T(2,128)S(1)} collective-permute-done((f32[2,2048]{1,0:T(2,128)S(1)}, f32[2,2048]{1,0:T(2,128)S(1)}, u32[]{:S(2)}, u32[]{:S(2)}) %collective-permute-start.68) | collective-permute-done | bytes 16416 | tf_op jit(solution)/shard_map/ppermute | solution.py:111
  (462 shorter events, 359.9 us)
Async XLA Ops:
  7.2 79.9 %all-gather.3.cloned.1.call-start = ((), (), s32[]{:S(2)}) async-start(), calls=%async_computation.2 | async-start | bytes 11796480 | tf_op jit(solution)/shard_map/all_gather | solution.py:740
  7.9 124.1 %all-gather.5.cloned.1.call-start = ((), (), s32[]{:S(2)}) async-start(), calls=%async_computation.3 | async-start | bytes 1310720 | tf_op jit(solution)/shard_map/all_gather | solution.py:779
  91.0 41.0 %collective-permute-start.10 = (bf16[256,2048]{1,0:T(8,128)(2,1)}, bf16[256,2048]{1,0:T(8,128)(2,1)}, u32[]{:S(2)}, u32[]{:S(2)}) collective-permute-start(bf16[256,2048]{1,0:T(8,128)(2,1)} %param.13), channel_id=1, source_target_pairs={{0,16},{4,20},{8,24},{12,28},{16,0},{20,4},{24,8},{28,12},{1,17},{... | collective-permute-start | bytes 3145736 | tf_op jit(solution)/shard_map/ppermute | solution.py:26
  92.1 40.0 %collective-permute-start.9 = (bf16[256,2048]{1,0:T(8,128)(2,1)}, bf16[256,2048]{1,0:T(8,128)(2,1)}, u32[]{:S(2)}, u32[]{:S(2)}) collective-permute-start(bf16[256,2048]{1,0:T(8,128)(2,1)} %param.13), channel_id=1, source_target_pairs={{0,8},{4,12},{8,0},{12,4},{16,24},{20,28},{24,16},{28,20},{1,9},{5... | collective-permute-start | bytes 3145736 | tf_op jit(solution)/shard_map/ppermute | solution.py:26
  96.7 347.0 %reduce-scatter.3.cloned.1.call-start = ((), (), s32[]{:S(2)}) async-start(), calls=%async_computation.4 | async-start | bytes 1310720 | tf_op jit(solution)/shard_map/reduce_scatter | solution.py:949
  96.7 35.3 %collective-permute-start.8 = (bf16[128,2816]{1,0:T(8,128)(2,1)}, bf16[128,2816]{1,0:T(8,128)(2,1)}, u32[]{:S(2)}, u32[]{:S(2)}) collective-permute-start(bf16[128,2816]{1,0:T(8,128)(2,1)} %shard_map.164), channel_id=1, source_target_pairs={{0,24},{4,28},{8,16},{12,20},{16,8},{20,12},{24,0},{28,4},{1,25},{... | collective-permute-start | bytes 2162696 | tf_op jit(solution)/shard_map/ppermute | solution.py:26
  220.0 37.1 %collective-permute-start.21 = (bf16[128,2048]{1,0:T(8,128)(2,1)S(1)}, bf16[128,2048]{1,0:T(8,128)(2,1)S(1)}, u32[]{:S(2)}, u32[]{:S(2)}) collective-permute-start(bf16[128,2048]{1,0:T(8,128)(2,1)S(1)} %slice.150), channel_id=1, source_target_pairs={{0,8},{4,12},{8,0},{12,4},{16,24},{20,28},{24,16},{28,20},{1,9},{5... | collective-permute-start | bytes 1572872 | tf_op jit(solution)/shard_map/ppermute | solution.py:26
  221.2 36.0 %collective-permute-start.22 = (bf16[128,2048]{1,0:T(8,128)(2,1)S(1)}, bf16[128,2048]{1,0:T(8,128)(2,1)S(1)}, u32[]{:S(2)}, u32[]{:S(2)}) collective-permute-start(bf16[128,2048]{1,0:T(8,128)(2,1)S(1)} %slice.151), channel_id=1, source_target_pairs={{0,16},{4,20},{8,24},{12,28},{16,0},{20,4},{24,8},{28,12},{1,17},{... | collective-permute-start | bytes 1572872 | tf_op jit(solution)/shard_map/ppermute | solution.py:26
  222.1 35.1 %collective-permute-start.23 = (bf16[128,2048]{1,0:T(8,128)(2,1)S(1)}, bf16[128,2048]{1,0:T(8,128)(2,1)S(1)}, u32[]{:S(2)}, u32[]{:S(2)}) collective-permute-start(bf16[128,2048]{1,0:T(8,128)(2,1)S(1)} %slice.152), channel_id=1, source_target_pairs={{0,8},{4,12},{8,0},{12,4},{16,24},{20,28},{24,16},{28,20},{1,9},{5... | collective-permute-start | bytes 1572872 | tf_op jit(solution)/shard_map/ppermute | solution.py:26
  353.5 43.0 %collective-permute-start.34 = (bf16[352,2048]{1,0:T(8,128)(2,1)S(1)}, bf16[352,2048]{1,0:T(8,128)(2,1)S(1)}, u32[]{:S(2)}, u32[]{:S(2)}) collective-permute-start(bf16[352,2048]{1,0:T(8,128)(2,1)S(1)} %add_convert_fusion.11), channel_id=1, source_target_pairs={{1,2},{2,1},{5,6},{6,5},{9,10},{10,9},{13,14},{14,13},{17,18},{18,... | collective-permute-start | bytes 4325384 | tf_op jit(solution)/shard_map/ppermute | solution.py:91
  354.4 42.1 %collective-permute-start.31 = (bf16[352,2048]{1,0:T(8,128)(2,1)S(1)}, bf16[352,2048]{1,0:T(8,128)(2,1)S(1)}, u32[]{:S(2)}, u32[]{:S(2)}) collective-permute-start(bf16[352,2048]{1,0:T(8,128)(2,1)S(1)} %get-tuple-element.892), channel_id=1, source_target_pairs={{0,1},{3,2},{4,5},{7,6},{8,9},{11,10},{12,13},{15,14},{16,17},{19,... | collective-permute-start | bytes 4325384 | tf_op jit(solution)/shard_map/ppermute | solution.py:95
  402.8 192.4 %reduce-scatter.5.cloned.1.call-start = ((), (), s32[]{:S(2)}) async-start(), calls=%async_computation.5 | async-start | bytes 9437184 | tf_op jit(solution)/shard_map/reduce_scatter | solution.py:974
  402.8 55.7 %collective-permute-start.38 = (bf16[352,2048]{1,0:T(8,128)(2,1)}, bf16[352,2048]{1,0:T(8,128)(2,1)}, u32[]{:S(2)}, u32[]{:S(2)}) collective-permute-start(bf16[352,2048]{1,0:T(8,128)(2,1)} %add_convert_fusion.10), channel_id=1, source_target_pairs={{1,2},{2,1},{5,6},{6,5},{9,10},{10,9},{13,14},{14,13},{17,18},{18,... | collective-permute-start | bytes 4325384 | tf_op jit(solution)/shard_map/ppermute | solution.py:91
  404.6 53.9 %collective-permute-start.35 = (bf16[256,2816]{1,0:T(8,128)(2,1)S(1)}, bf16[256,2816]{1,0:T(8,128)(2,1)}, u32[]{:S(2)}, u32[]{:S(2)}) collective-permute-start(bf16[256,2816]{1,0:T(8,128)(2,1)S(1)} %get-tuple-element.936), channel_id=1, source_target_pairs={{0,1},{3,2},{4,5},{7,6},{8,9},{11,10},{12,13},{15,14},{16,17},{19,... | collective-permute-start | bytes 4325384 | tf_op jit(solution)/shard_map/ppermute | solution.py:95
  411.3 47.2 %collective-permute-start.36 = (bf16[352,2048]{1,0:T(8,128)(2,1)}, bf16[352,2048]{1,0:T(8,128)(2,1)}, u32[]{:S(2)}, u32[]{:S(2)}) collective-permute-start(bf16[352,2048]{1,0:T(8,128)(2,1)} %add_convert_fusion.9), channel_id=1, source_target_pairs={{1,0},{2,3},{5,4},{6,7},{9,8},{10,11},{13,12},{14,15},{17,16},{18,... | collective-permute-start | bytes 4325384 | tf_op jit(solution)/shard_map/ppermute | solution.py:98
  412.6 45.9 %collective-permute-start.37 = (bf16[256,2816]{1,0:T(8,128)(2,1)}, bf16[256,2816]{1,0:T(8,128)(2,1)}, u32[]{:S(2)}, u32[]{:S(2)}) collective-permute-start(bf16[256,2816]{1,0:T(8,128)(2,1)} %get-tuple-element.911), channel_id=1, source_target_pairs={{0,24},{4,28},{8,16},{12,20},{16,8},{20,12},{24,0},{28,4},{1,25},{... | collective-permute-start | bytes 4325384 | tf_op jit(solution)/shard_map/ppermute | solution.py:26
  460.4 42.7 %collective-permute-start.39 = (bf16[1024,2560]{1,0:T(8,128)(2,1)}, bf16[1024,2560]{1,0:T(8,128)(2,1)}, u32[]{:S(2)}, u32[]{:S(2)}) collective-permute-start(bf16[1024,2560]{1,0:T(8,128)(2,1)} %convolution_convert_fusion.2), channel_id=1, source_target_pairs={{0,4},{4,0},{8,12},{12,8},{16,20},{20,16},{24,28},{28,24},{1,5},{5... | collective-permute-start | bytes 15728648 | tf_op jit(solution)/shard_map/ppermute | solution.py:26
  462.4 35.9 %collective-permute-start.41 = (bf16[352,2048]{1,0:T(8,128)(2,1)S(1)}, bf16[352,2048]{1,0:T(8,128)(2,1)}, u32[]{:S(2)}, u32[]{:S(2)}) collective-permute-start(bf16[352,2048]{1,0:T(8,128)(2,1)S(1)} %add_convert_fusion.7), channel_id=1, source_target_pairs={{1,0},{2,3},{5,4},{6,7},{9,8},{10,11},{13,12},{14,15},{17,16},{18,... | collective-permute-start | bytes 4325384 | tf_op jit(solution)/shard_map/ppermute | solution.py:98
  465.5 37.6 %collective-permute-start.40 = (bf16[256,2816]{1,0:T(8,128)(2,1)}, bf16[256,2816]{1,0:T(8,128)(2,1)}, u32[]{:S(2)}, u32[]{:S(2)}) collective-permute-start(bf16[256,2816]{1,0:T(8,128)(2,1)} %collective-permute-done.32), channel_id=1, source_target_pairs={{0,1},{3,2},{4,5},{7,6},{8,9},{11,10},{12,13},{15,14},{16,17},{19,... | collective-permute-start | bytes 4325384 | tf_op jit(solution)/shard_map/ppermute | solution.py:95
  505.3 43.8 %collective-permute-start.47 = (bf16[256,2816]{1,0:T(8,128)(2,1)S(1)}, bf16[256,2816]{1,0:T(8,128)(2,1)S(1)}, u32[]{:S(2)}, u32[]{:S(2)}) collective-permute-start(bf16[256,2816]{1,0:T(8,128)(2,1)S(1)} %add_convert_fusion.6), channel_id=1, source_target_pairs={{1,2},{2,1},{5,6},{6,5},{9,10},{10,9},{13,14},{14,13},{17,18},{18,... | collective-permute-start | bytes 4325384 | tf_op jit(solution)/shard_map/ppermute | solution.py:91
  506.0 43.0 %collective-permute-start.45 = (bf16[256,2816]{1,0:T(8,128)(2,1)S(1)}, bf16[256,2816]{1,0:T(8,128)(2,1)S(1)}, u32[]{:S(2)}, u32[]{:S(2)}) collective-permute-start(bf16[256,2816]{1,0:T(8,128)(2,1)S(1)} %copy-done.56), channel_id=1, source_target_pairs={{0,1},{3,2},{4,5},{7,6},{8,9},{11,10},{12,13},{15,14},{16,17},{19,... | collective-permute-start | bytes 4325384 | tf_op jit(solution)/shard_map/ppermute | solution.py:95
  550.6 44.6 %collective-permute-start.52 = (bf16[256,2816]{1,0:T(8,128)(2,1)}, bf16[256,2816]{1,0:T(8,128)(2,1)}, u32[]{:S(2)}, u32[]{:S(2)}) collective-permute-start(bf16[256,2816]{1,0:T(8,128)(2,1)} %add_convert_fusion.4), channel_id=1, source_target_pairs={{1,2},{2,1},{5,6},{6,5},{9,10},{10,9},{13,14},{14,13},{17,18},{18,... | collective-permute-start | bytes 4325384 | tf_op jit(solution)/shard_map/ppermute | solution.py:91
  552.5 42.7 %collective-permute-start.48 = (bf16[256,2816]{1,0:T(8,128)(2,1)}, bf16[256,2816]{1,0:T(8,128)(2,1)}, u32[]{:S(2)}, u32[]{:S(2)}) collective-permute-start(bf16[256,2816]{1,0:T(8,128)(2,1)} %collective-permute-done.37), channel_id=1, source_target_pairs={{0,1},{3,2},{4,5},{7,6},{8,9},{11,10},{12,13},{15,14},{16,17},{19,... | collective-permute-start | bytes 4325384 | tf_op jit(solution)/shard_map/ppermute | solution.py:95
  630.4 38.6 %collective-permute-start.58 = (bf16[256,2560]{1,0:T(8,128)(2,1)}, bf16[256,2560]{1,0:T(8,128)(2,1)}, u32[]{:S(2)}, u32[]{:S(2)}) collective-permute-start(bf16[256,2560]{1,0:T(8,128)(2,1)} %add_convert_fusion.14), channel_id=1, source_target_pairs={{0,1},{3,2},{4,5},{7,6},{8,9},{11,10},{12,13},{15,14},{16,17},{19,... | collective-permute-start | bytes 3932168 | tf_op jit(solution)/shard_map/ppermute | solution.py:95
  (137 other events, 2172.7 us)
Sparse Core Ops, SparseCore 0:
  9.9 74.4 all-gather.2
  96.8 27.9 all-gather.4
  402.9 40.6 reduce-scatter.2
  473.1 76.4 reduce-scatter.4

commit v6 on v5

--- a/solution.py
+++ b/solution.py
@@ -1010,16 +1010,17 @@
         grad_gains=jnp.stack([grad_gain_one, live.pop("grad_gain_two")]),
     )
 
-    line_step(live, new="out", cross=names[3], out=names[2])
+    total = total_of(live.pop("parts_qkv"), live.pop("far_qkv"), live.pop("near_qkv"))
+    live["zq"] = total.astype(bf16)
+    line_step(live, new="q", cross=names[3], out=names[2])
     gate_up_sums = placed_in(live.pop("sums"), evens[1])
-    total = total_of(live.pop("parts_qkv"), live.pop("far_qkv"), live.pop("near_qkv")).astype(bf16)
-    fence(far=far_sends(live["parts"]), sums=gate_up_sums, zq=total)
-
-    line_step(live, new="q", cross="out", out=names[3])
+    fence(far=far_sends(live["parts"]), sums=gate_up_sums)
+
+    line_step(live, new="out", cross="q", out=names[3])
     gate_up_sums = placed_in(live.pop("sums"), evens[2])
     fence(near=near_sends(live["parts"], live["far"]), sums=gate_up_sums)
 
-    line_step(live, cross="q", out="out")
+    line_step(live, cross="out", out="q")
     gate_up_sums = live.pop("sums")
     for k in evens[3:]:
         gate_up_sums = placed_in(gate_up_sums, k)
@@ -1028,7 +1029,7 @@
     out = (live["middle"] + out).astype(bf16)
     fence(sums=gate_up_sums, grad_gains=grad_gains, out_final=out)
 
-    line_step(live, out="q")
+    line_step(live, out="out")
     out_sums = summed("out")
     grad_gains = small_sum(live.pop("grad_gains"), "seq")
     qkv_sums = summed("q")

time: 751 us -> 755 us (level)
    ppermute x5, waiting for transfers between devices: 28.1 us -> 4.28 us  [small_sum(): x = x + lax.ppermute(x, axis, [(i, i ^ k) for i in range(n)])]
    ppermute x8, waiting for transfers between devices: 45.3 us -> 61.9 us  [line_step(): live['o' + out] = lax.ppermute(total, 'seq', outward)]
    unnamed x184 -> x182, local copies, waits for them, and re-layouts: 31.2 us -> 30.3 us
  transfers between devices with their start and end apart: 75 -> 75, of which waited for: 38 -> 37; matrix products, arithmetic and copies ran while one was open for 17% -> 16% of each run, Pallas kernels for 27% -> 27%
where the time goes in v6:
time: 755 us; the launch traced here: 744 us
  waiting for transfers between devices  236 us (31%)
  Pallas kernels  209 us (28%)
  starting transfers between devices  117 us (15%)
  other arithmetic  87.8 us (12%)
  local copies, waits for them, and re-layouts  46 us (6%)
  matrix products  32.7 us (4%)
  between operations  15.8 us (2%)
    ppermute x39, waiting for transfers between devices, send(): return lax.ppermute(x, 'fsdp', [(i, i ^ k) for i in range(n)])  112 us
    pallas_call x3, Pallas kernels, ffn(): pl.pallas_call(functools.partial(ffn_kernel, n, count), out_shape=shapes,...  76.2 us
    ppermute x8, waiting for transfers between devices, line_step(): live['o' + out] = lax.ppermute(total, 'seq', outward)  61.9 us
    ppermute x8, starting transfers between devices, line_step(): live['i' + new] = lax.ppermute(x, 'seq', inward)  46.3 us
    convert_element_type x21, other arithmetic, added(): return (one.astype(f32) + two.astype(f32)).astype(bf16)  40 us
    ppermute x39, starting transfers between devices, send(): return lax.ppermute(x, 'fsdp', [(i, i ^ k) for i in range(n)])  38.5 us
    unnamed x182, local copies, waits for them, and re-layouts  30.3 us
    pallas_call x1, Pallas kernels, attend_back(): pl.pallas_call(functools.partial(attend_back_kernel, heads, per_kv), out_...  29.6 us
  transfers between devices with their start and end apart: 75, of which 37 were waited for; matrix products, arithmetic and copies ran while one was open for 16% of the time, Pallas kernels for 27%

profile of v6, /device:TPU:0, one launch (start us, length us, event | category | flops | bytes accessed | tf_op | source)
XLA Modules:
  0.0 743.6 jit_solution(9994960375545445543)
XLA Ops:
  35.5 17.5 %collective-permute-done.4 = bf16[128,2816]{1,0:T(8,128)(2,1)} collective-permute-done((bf16[128,2816]{1,0:T(8,128)(2,1)}, bf16[128,2816]{1,0:T(8,128)(2,1)}, u32[]{:S(2)}, u32[]{:S(2)}) %collective-permute-start.4) | collective-permute-done | bytes 720928 | tf_op jit(solution)/shard_map/ppermute | solution.py:26
  65.8 7.1 collective-permute-done.6
  72.9 14.2 %collective-permute-done.7 = bf16[128,2816]{1,0:T(8,128)(2,1)S(1)} collective-permute-done((bf16[128,2816]{1,0:T(8,128)(2,1)}, bf16[128,2816]{1,0:T(8,128)(2,1)S(1)}, u32[]{:S(2)}, u32[]{:S(2)}) %collective-permute-start.7) | collective-permute-done | bytes 720928 | tf_op jit(solution)/shard_map/ppermute | solution.py:51
  112.3 19.7 %collective-permute-done.8 = bf16[128,2816]{1,0:T(8,128)(2,1)} collective-permute-done((bf16[128,2816]{1,0:T(8,128)(2,1)}, bf16[128,2816]{1,0:T(8,128)(2,1)}, u32[]{:S(2)}, u32[]{:S(2)}) %collective-permute-start.8) | collective-permute-done | bytes 720928 | tf_op jit(solution)/shard_map/ppermute | solution.py:26
  139.5 23.0 %shard_map.167 = (bf16[256,2048]{1,0:T(8,128)(2,1)S(1)}, f32[8,4,256]{2,1,0:T(4,128)S(1)}) custom-call(s32[9]{0:T(128)S(1)} %get-tuple-element.1179.info_ref, f32[256,2048]{1,0:T(8,128)S(1)} %fusion.q_ref, bf16[1024,512]{1,0:T(8,128)(2,1)S(1)} %copy-done.20, bf16[1024,512]{1,0:T(8,128)(2,1)S(1)} %copy-done.20, f32[32,256]{1,0:T(8,128)S(1)} %get-tuple-element.1171.cos_ref, ...), custom_call_target="tpu_custom_call" | custom-call | flops 8589934592 | bytes 3145728 | tf_op jit(solution)/shard_map/pallas_call | solution.py:286
  179.8 11.5 %collective-permute-done.16.refs_3_.refs_6_ = bf16[256,2048]{1,0:T(8,128)(2,1)S(1)} collective-permute-done((bf16[256,2048]{1,0:T(8,128)(2,1)S(1)}, bf16[256,2048]{1,0:T(8,128)(2,1)S(1)}, u32[]{:S(2)}, u32[]{:S(2)}) %collective-permute-start.16) | collective-permute-done | bytes 1048608 | tf_op jit(solution)/shard_map/ppermute | solution.py:26
  196.2 21.5 %shard_map.168 = (bf16[1408,256]{1,0:T(8,128)(2,1)}, bf16[256,2816]{1,0:T(8,128)(2,1)}, bf16[256,2048]{1,0:T(8,128)(2,1)}, bf16[256,2048]{1,0:T(8,128)(2,1)}) custom-call(s32[4]{0:T(128)} %pad_add_fusion.4.info_ref, bf16[256,2048]{1,0:T(8,128)(2,1)} %get-tuple-element.812.refs_0_, bf16[256,2048]{1,0:T(8,128)(2,1)} %bitcast.47, ...), custom_call_target="tpu_custom_call" | custom-call | flops 8858370048 | bytes 17301504 | tf_op jit(solution)/shard_map/pallas_call | solution.py:493
  224.1 33.0 %shard_map.169 = (bf16[1408,256]{1,0:T(8,128)(2,1)}, bf16[1408,256]{1,0:T(8,128)(2,1)}, bf16[256,2816]{1,0:T(8,128)(2,1)}, bf16[256,2816]{1,0:T(8,128)(2,1)}, bf...) custom-call(s32[4]{0:T(128)} %pad_add_fusion.4.info_ref, ...), custom_call_target="tpu_custom_call" | custom-call | flops 17716740096 | bytes 17301504 | tf_op jit(solution)/shard_map/pallas_call | solution.py:493
  260.8 21.7 %shard_map.170 = (bf16[1408,256]{1,0:T(8,128)(2,1)}, bf16[256,2816]{1,0:T(8,128)(2,1)}, bf16[256,2048]{1,0:T(8,128)(2,1)}, bf16[256,2048]{1,0:T(8,128)(2,1)}) custom-call(s32[4]{0:T(128)} %pad_add_fusion.4.info_ref, bf16[256,2048]{1,0:T(8,128)(2,1)} %get-tuple-element.1185.refs_0_, bf16[256,2048]{1,0:T(8,128)(2,1)} %get-tuple-element.1186.refs_1_, ...), custom_call_target="tpu_custom_call" | custom-call | flops 8858370048 | bytes 17301504 | tf_op jit(solution)/shard_map/pallas_call | solution.py:493
  293.8 12.8 %shard_map.172 = bf16[1024,2816]{1,0:T(8,128)(2,1)} custom-call(s32[4]{0:T(128)S(1)} %get-tuple-element.768.info_ref, bf16[256,2048]{1,0:T(8,128)(2,1)} %get-tuple-element.812.refs_0_, bf16[256,2048]{1,0:T(8,128)(2,1)} %collective-permute-done.19.refs_0_.refs_1_, bf16[256,2048]{1,0:T(8,128)(2,1)S(1)} %copy-done.14, ...), custom_call_target="tpu_custom_call" | custom-call | flops 5905580032 | bytes 11534336 | tf_op jit(solution)/shard_map/pallas_call | solution.py:627
  336.0 15.1 %shard_map.174 = (bf16[256,2816]{1,0:T(8,128)(2,1)S(1)}, bf16[256,2816]{1,0:T(8,128)(2,1)}, bf16[256,2816]{1,0:T(8,128)(2,1)}, bf16[256,2816]{1,0:T(8,128)(2,1)}) custom-call(s32[4]{0:T(128)S(1)} %get-tuple-element.1180.info_ref, bf16[256,2048]{1,0:T(8,128)(2,1)} %get-tuple-element.812.refs_0_, bf16[256,2048]{1,0:T(8,128)(2,1)} %collective-permute-done.19.refs_0_.refs_1_, ...), custom_call_target="tpu_custom_call" | custom-call | flops 5905580032 | bytes 11534336 | tf_op jit(solution)/shard_map/pallas_call | solution.py:627
  354.4 8.3 %collective-permute-start.31 = (bf16[352,2048]{1,0:T(8,128)(2,1)S(1)}, bf16[352,2048]{1,0:T(8,128)(2,1)S(1)}, u32[]{:S(2)}, u32[]{:S(2)}) collective-permute-start(bf16[352,2048]{1,0:T(8,128)(2,1)S(1)} %get-tuple-element.890), channel_id=1, source_target_pairs={{0,1},{3,2},{4,5},{7,6},{8,9},{11,10},{12,13},{15,14},{16,17},{19,... | collective-permute-start | bytes 4325384 | tf_op jit(solution)/shard_map/ppermute | solution.py:95
  364.8 29.6 %shard_map.175 = (bf16[256,2048]{1,0:T(8,128)(2,1)S(1)}, bf16[1024,512]{1,0:T(8,128)(2,1)}) custom-call(s32[9]{0:T(128)S(1)} %get-tuple-element.1179.info_ref, f32[256,2048]{1,0:T(8,128)} %copy-done.22, bf16[1024,512]{1,0:T(8,128)(2,1)S(1)} %copy-done.21, bf16[1024,512]{1,0:T(8,128)(2,1)S(1)} %copy-done.21, bf16[256,2048]{1,0:T(8,128)(2,1)S(1)} %pad_maximum_fusion.6.g_ref, ...), custom_call_target="tpu_custom_call" | custom-call | flops 21474836480 | bytes 4194304 | tf_op jit(solution)/shard_map/pallas_call | solution.py:365
  426.7 17.0 %reduce-scatter.3.cloned.1.call-done = bf16[256,512]{1,0:T(8,128)(2,1)} async-done(((bf16[1024,512]{1,0:T(8,128)(2,1)}), bf16[256,512]{1,0:T(8,128)(2,1)}) %reduce-scatter.3.cloned.1.call-update) | async-done | bytes 262160 | tf_op jit(solution)/shard_map/reduce_scatter | solution.py:949
  465.5 7.5 %collective-permute-start.40 = (bf16[256,2816]{1,0:T(8,128)(2,1)}, bf16[256,2816]{1,0:T(8,128)(2,1)}, u32[]{:S(2)}, u32[]{:S(2)}) collective-permute-start(bf16[256,2816]{1,0:T(8,128)(2,1)} %collective-permute-done.32), channel_id=1, source_target_pairs={{0,1},{3,2},{4,5},{7,6},{8,9},{11,10},{12,13},{15,14},{16,17},{19,... | collective-permute-start | bytes 4325384 | tf_op jit(solution)/shard_map/ppermute | solution.py:95
  476.6 21.7 %collective-permute-done.41 = bf16[352,2048]{1,0:T(8,128)(2,1)} collective-permute-done((bf16[352,2048]{1,0:T(8,128)(2,1)S(1)}, bf16[352,2048]{1,0:T(8,128)(2,1)}, u32[]{:S(2)}, u32[]{:S(2)}) %collective-permute-start.41) | collective-permute-done | bytes 1441824 | tf_op jit(solution)/shard_map/ppermute | solution.py:98
  506.0 7.2 collective-permute-start.45
  529.5 11.8 %collective-permute-done.44 = bf16[128,2560]{1,0:T(8,128)(2,1)S(1)} collective-permute-done((bf16[128,2560]{1,0:T(8,128)(2,1)S(1)}, bf16[128,2560]{1,0:T(8,128)(2,1)S(1)}, u32[]{:S(2)}, u32[]{:S(2)}) %collective-permute-start.44) | collective-permute-done | bytes 655392 | tf_op jit(solution)/shard_map/ppermute | solution.py:26
  576.3 9.4 %collective-permute-done.50 = bf16[256,2560]{1,0:T(8,128)(2,1)} collective-permute-done((bf16[256,2560]{1,0:T(8,128)(2,1)}, bf16[256,2560]{1,0:T(8,128)(2,1)}, u32[]{:S(2)}, u32[]{:S(2)}) %collective-permute-start.50) | collective-permute-done | bytes 1310752 | tf_op jit(solution)/shard_map/ppermute | solution.py:26
  605.9 8.6 %collective-permute-start.55 = (bf16[256,2560]{1,0:T(8,128)(2,1)}, bf16[256,2560]{1,0:T(8,128)(2,1)}, u32[]{:S(2)}, u32[]{:S(2)}) collective-permute-start(bf16[256,2560]{1,0:T(8,128)(2,1)} %add_convert_fusion.14), channel_id=1, source_target_pairs={{0,1},{3,2},{4,5},{7,6},{8,9},{11,10},{12,13},{15,14},{16,17},{19,... | collective-permute-start | bytes 3932168 | tf_op jit(solution)/shard_map/ppermute | solution.py:95
  625.6 12.3 %collective-permute-done.55 = bf16[256,2560]{1,0:T(8,128)(2,1)} collective-permute-done((bf16[256,2560]{1,0:T(8,128)(2,1)}, bf16[256,2560]{1,0:T(8,128)(2,1)}, u32[]{:S(2)}, u32[]{:S(2)}) %collective-permute-start.55) | collective-permute-done | bytes 1310752 | tf_op jit(solution)/shard_map/ppermute | solution.py:95
  660.3 11.8 %collective-permute-done.60 = bf16[256,2048]{1,0:T(8,128)(2,1)} collective-permute-done((bf16[256,2048]{1,0:T(8,128)(2,1)}, bf16[256,2048]{1,0:T(8,128)(2,1)}, u32[]{:S(2)}, u32[]{:S(2)}) %collective-permute-start.60) | collective-permute-done | bytes 1048608 | tf_op jit(solution)/shard_map/ppermute | solution.py:26
  701.8 9.0 %collective-permute-done.66 = bf16[256,2560]{1,0:T(8,128)(2,1)} collective-permute-done((bf16[256,2560]{1,0:T(8,128)(2,1)S(1)}, bf16[256,2560]{1,0:T(8,128)(2,1)}, u32[]{:S(2)}, u32[]{:S(2)}) %collective-permute-start.66) | collective-permute-done | bytes 1310752 | tf_op jit(solution)/shard_map/ppermute | solution.py:98
  722.3 12.9 %collective-permute-done.70 = bf16[256,2048]{1,0:T(8,128)(2,1)S(1)} collective-permute-done((bf16[256,2048]{1,0:T(8,128)(2,1)S(1)}, bf16[256,2048]{1,0:T(8,128)(2,1)S(1)}, u32[]{:S(2)}, u32[]{:S(2)}) %collective-permute-start.70) | collective-permute-done | bytes 1048608 | tf_op jit(solution)/shard_map/ppermute | solution.py:98
  (460 shorter events, 363.6 us)
Async XLA Ops:
  7.2 79.9 %all-gather.3.cloned.1.call-start = ((), (), s32[]{:S(2)}) async-start(), calls=%async_computation.2 | async-start | bytes 11796480 | tf_op jit(solution)/shard_map/all_gather | solution.py:740
  7.9 124.1 %all-gather.5.cloned.1.call-start = ((), (), s32[]{:S(2)}) async-start(), calls=%async_computation.3 | async-start | bytes 1310720 | tf_op jit(solution)/shard_map/all_gather | solution.py:779
  91.0 41.0 %collective-permute-start.10 = (bf16[256,2048]{1,0:T(8,128)(2,1)}, bf16[256,2048]{1,0:T(8,128)(2,1)}, u32[]{:S(2)}, u32[]{:S(2)}) collective-permute-start(bf16[256,2048]{1,0:T(8,128)(2,1)} %param.13), channel_id=1, source_target_pairs={{0,16},{4,20},{8,24},{12,28},{16,0},{20,4},{24,8},{28,12},{1,17},{... | collective-permute-start | bytes 3145736 | tf_op jit(solution)/shard_map/ppermute | solution.py:26
  92.1 40.0 %collective-permute-start.9 = (bf16[256,2048]{1,0:T(8,128)(2,1)}, bf16[256,2048]{1,0:T(8,128)(2,1)}, u32[]{:S(2)}, u32[]{:S(2)}) collective-permute-start(bf16[256,2048]{1,0:T(8,128)(2,1)} %param.13), channel_id=1, source_target_pairs={{0,8},{4,12},{8,0},{12,4},{16,24},{20,28},{24,16},{28,20},{1,9},{5... | collective-permute-start | bytes 3145736 | tf_op jit(solution)/shard_map/ppermute | solution.py:26
  96.7 346.9 %reduce-scatter.3.cloned.1.call-start = ((), (), s32[]{:S(2)}) async-start(), calls=%async_computation.4 | async-start | bytes 1310720 | tf_op jit(solution)/shard_map/reduce_scatter | solution.py:949
  96.7 35.3 %collective-permute-start.8 = (bf16[128,2816]{1,0:T(8,128)(2,1)}, bf16[128,2816]{1,0:T(8,128)(2,1)}, u32[]{:S(2)}, u32[]{:S(2)}) collective-permute-start(bf16[128,2816]{1,0:T(8,128)(2,1)} %shard_map.164), channel_id=1, source_target_pairs={{0,24},{4,28},{8,16},{12,20},{16,8},{20,12},{24,0},{28,4},{1,25},{... | collective-permute-start | bytes 2162696 | tf_op jit(solution)/shard_map/ppermute | solution.py:26
  220.0 37.1 %collective-permute-start.21 = (bf16[128,2048]{1,0:T(8,128)(2,1)S(1)}, bf16[128,2048]{1,0:T(8,128)(2,1)S(1)}, u32[]{:S(2)}, u32[]{:S(2)}) collective-permute-start(bf16[128,2048]{1,0:T(8,128)(2,1)S(1)} %slice.150), channel_id=1, source_target_pairs={{0,8},{4,12},{8,0},{12,4},{16,24},{20,28},{24,16},{28,20},{1,9},{5... | collective-permute-start | bytes 1572872 | tf_op jit(solution)/shard_map/ppermute | solution.py:26
  220.9 36.2 %collective-permute-start.22 = (bf16[128,2048]{1,0:T(8,128)(2,1)S(1)}, bf16[128,2048]{1,0:T(8,128)(2,1)S(1)}, u32[]{:S(2)}, u32[]{:S(2)}) collective-permute-start(bf16[128,2048]{1,0:T(8,128)(2,1)S(1)} %slice.151), channel_id=1, source_target_pairs={{0,16},{4,20},{8,24},{12,28},{16,0},{20,4},{24,8},{28,12},{1,17},{... | collective-permute-start | bytes 1572872 | tf_op jit(solution)/shard_map/ppermute | solution.py:26
  222.0 35.1 %collective-permute-start.23 = (bf16[128,2048]{1,0:T(8,128)(2,1)S(1)}, bf16[128,2048]{1,0:T(8,128)(2,1)S(1)}, u32[]{:S(2)}, u32[]{:S(2)}) collective-permute-start(bf16[128,2048]{1,0:T(8,128)(2,1)S(1)} %slice.152), channel_id=1, source_target_pairs={{0,8},{4,12},{8,0},{12,4},{16,24},{20,28},{24,16},{28,20},{1,9},{5... | collective-permute-start | bytes 1572872 | tf_op jit(solution)/shard_map/ppermute | solution.py:26
  353.5 43.0 %collective-permute-start.34 = (bf16[352,2048]{1,0:T(8,128)(2,1)S(1)}, bf16[352,2048]{1,0:T(8,128)(2,1)S(1)}, u32[]{:S(2)}, u32[]{:S(2)}) collective-permute-start(bf16[352,2048]{1,0:T(8,128)(2,1)S(1)} %add_convert_fusion.11), channel_id=1, source_target_pairs={{1,2},{2,1},{5,6},{6,5},{9,10},{10,9},{13,14},{14,13},{17,18},{18,... | collective-permute-start | bytes 4325384 | tf_op jit(solution)/shard_map/ppermute | solution.py:91
  354.4 42.2 %collective-permute-start.31 = (bf16[352,2048]{1,0:T(8,128)(2,1)S(1)}, bf16[352,2048]{1,0:T(8,128)(2,1)S(1)}, u32[]{:S(2)}, u32[]{:S(2)}) collective-permute-start(bf16[352,2048]{1,0:T(8,128)(2,1)S(1)} %get-tuple-element.890), channel_id=1, source_target_pairs={{0,1},{3,2},{4,5},{7,6},{8,9},{11,10},{12,13},{15,14},{16,17},{19,... | collective-permute-start | bytes 4325384 | tf_op jit(solution)/shard_map/ppermute | solution.py:95
  402.8 192.4 %reduce-scatter.5.cloned.1.call-start = ((), (), s32[]{:S(2)}) async-start(), calls=%async_computation.5 | async-start | bytes 9437184 | tf_op jit(solution)/shard_map/reduce_scatter | solution.py:974
  402.8 55.7 %collective-permute-start.38 = (bf16[352,2048]{1,0:T(8,128)(2,1)}, bf16[352,2048]{1,0:T(8,128)(2,1)}, u32[]{:S(2)}, u32[]{:S(2)}) collective-permute-start(bf16[352,2048]{1,0:T(8,128)(2,1)} %add_convert_fusion.10), channel_id=1, source_target_pairs={{1,2},{2,1},{5,6},{6,5},{9,10},{10,9},{13,14},{14,13},{17,18},{18,... | collective-permute-start | bytes 4325384 | tf_op jit(solution)/shard_map/ppermute | solution.py:91
  404.6 53.9 %collective-permute-start.35 = (bf16[256,2816]{1,0:T(8,128)(2,1)S(1)}, bf16[256,2816]{1,0:T(8,128)(2,1)}, u32[]{:S(2)}, u32[]{:S(2)}) collective-permute-start(bf16[256,2816]{1,0:T(8,128)(2,1)S(1)} %get-tuple-element.934), channel_id=1, source_target_pairs={{0,1},{3,2},{4,5},{7,6},{8,9},{11,10},{12,13},{15,14},{16,17},{19,... | collective-permute-start | bytes 4325384 | tf_op jit(solution)/shard_map/ppermute | solution.py:95
  411.3 47.1 %collective-permute-start.36 = (bf16[352,2048]{1,0:T(8,128)(2,1)}, bf16[352,2048]{1,0:T(8,128)(2,1)}, u32[]{:S(2)}, u32[]{:S(2)}) collective-permute-start(bf16[352,2048]{1,0:T(8,128)(2,1)} %add_convert_fusion.9), channel_id=1, source_target_pairs={{1,0},{2,3},{5,4},{6,7},{9,8},{10,11},{13,12},{14,15},{17,16},{18,... | collective-permute-start | bytes 4325384 | tf_op jit(solution)/shard_map/ppermute | solution.py:98
  412.6 45.9 %collective-permute-start.37 = (bf16[256,2816]{1,0:T(8,128)(2,1)}, bf16[256,2816]{1,0:T(8,128)(2,1)}, u32[]{:S(2)}, u32[]{:S(2)}) collective-permute-start(bf16[256,2816]{1,0:T(8,128)(2,1)} %get-tuple-element.909), channel_id=1, source_target_pairs={{0,24},{4,28},{8,16},{12,20},{16,8},{20,12},{24,0},{28,4},{1,25},{... | collective-permute-start | bytes 4325384 | tf_op jit(solution)/shard_map/ppermute | solution.py:26
  460.4 42.6 %collective-permute-start.39 = (bf16[1024,2560]{1,0:T(8,128)(2,1)}, bf16[1024,2560]{1,0:T(8,128)(2,1)}, u32[]{:S(2)}, u32[]{:S(2)}) collective-permute-start(bf16[1024,2560]{1,0:T(8,128)(2,1)} %convolution_convert_fusion.2), channel_id=1, source_target_pairs={{0,4},{4,0},{8,12},{12,8},{16,20},{20,16},{24,28},{28,24},{1,5},{5... | collective-permute-start | bytes 15728648 | tf_op jit(solution)/shard_map/ppermute | solution.py:26
  462.4 35.9 %collective-permute-start.41 = (bf16[352,2048]{1,0:T(8,128)(2,1)S(1)}, bf16[352,2048]{1,0:T(8,128)(2,1)}, u32[]{:S(2)}, u32[]{:S(2)}) collective-permute-start(bf16[352,2048]{1,0:T(8,128)(2,1)S(1)} %add_convert_fusion.7), channel_id=1, source_target_pairs={{1,0},{2,3},{5,4},{6,7},{9,8},{10,11},{13,12},{14,15},{17,16},{18,... | collective-permute-start | bytes 4325384 | tf_op jit(solution)/shard_map/ppermute | solution.py:98
  465.5 37.5 %collective-permute-start.40 = (bf16[256,2816]{1,0:T(8,128)(2,1)}, bf16[256,2816]{1,0:T(8,128)(2,1)}, u32[]{:S(2)}, u32[]{:S(2)}) collective-permute-start(bf16[256,2816]{1,0:T(8,128)(2,1)} %collective-permute-done.32), channel_id=1, source_target_pairs={{0,1},{3,2},{4,5},{7,6},{8,9},{11,10},{12,13},{15,14},{16,17},{19,... | collective-permute-start | bytes 4325384 | tf_op jit(solution)/shard_map/ppermute | solution.py:95
  505.2 43.8 %collective-permute-start.47 = (bf16[256,2816]{1,0:T(8,128)(2,1)S(1)}, bf16[256,2816]{1,0:T(8,128)(2,1)S(1)}, u32[]{:S(2)}, u32[]{:S(2)}) collective-permute-start(bf16[256,2816]{1,0:T(8,128)(2,1)S(1)} %add_convert_fusion.6), channel_id=1, source_target_pairs={{1,2},{2,1},{5,6},{6,5},{9,10},{10,9},{13,14},{14,13},{17,18},{18,... | collective-permute-start | bytes 4325384 | tf_op jit(solution)/shard_map/ppermute | solution.py:91
  506.0 43.0 %collective-permute-start.45 = (bf16[256,2816]{1,0:T(8,128)(2,1)S(1)}, bf16[256,2816]{1,0:T(8,128)(2,1)S(1)}, u32[]{:S(2)}, u32[]{:S(2)}) collective-permute-start(bf16[256,2816]{1,0:T(8,128)(2,1)S(1)} %copy-done.56), channel_id=1, source_target_pairs={{0,1},{3,2},{4,5},{7,6},{8,9},{11,10},{12,13},{15,14},{16,17},{19,... | collective-permute-start | bytes 4325384 | tf_op jit(solution)/shard_map/ppermute | solution.py:95
  550.5 44.6 %collective-permute-start.52 = (bf16[256,2816]{1,0:T(8,128)(2,1)}, bf16[256,2816]{1,0:T(8,128)(2,1)}, u32[]{:S(2)}, u32[]{:S(2)}) collective-permute-start(bf16[256,2816]{1,0:T(8,128)(2,1)} %add_convert_fusion.4), channel_id=1, source_target_pairs={{1,2},{2,1},{5,6},{6,5},{9,10},{10,9},{13,14},{14,13},{17,18},{18,... | collective-permute-start | bytes 4325384 | tf_op jit(solution)/shard_map/ppermute | solution.py:91
  552.4 42.7 %collective-permute-start.48 = (bf16[256,2816]{1,0:T(8,128)(2,1)}, bf16[256,2816]{1,0:T(8,128)(2,1)}, u32[]{:S(2)}, u32[]{:S(2)}) collective-permute-start(bf16[256,2816]{1,0:T(8,128)(2,1)} %collective-permute-done.37), channel_id=1, source_target_pairs={{0,1},{3,2},{4,5},{7,6},{8,9},{11,10},{12,13},{15,14},{16,17},{19,... | collective-permute-start | bytes 4325384 | tf_op jit(solution)/shard_map/ppermute | solution.py:95
  602.8 35.1 %collective-permute-start.56 = (bf16[256,2816]{1,0:T(8,128)(2,1)S(1)}, bf16[256,2816]{1,0:T(8,128)(2,1)}, u32[]{:S(2)}, u32[]{:S(2)}) collective-permute-start(bf16[256,2816]{1,0:T(8,128)(2,1)S(1)} %add_convert_fusion.1.total_ref), channel_id=1, source_target_pairs={{1,0},{2,3},{5,4},{6,7},{9,8},{10,11},{13,12},{14,15},{17,16},{18,... | collective-permute-start | bytes 4325384 | tf_op jit(solution)/shard_map/ppermute | solution.py:98
  (136 other events, 2171.3 us)
Sparse Core Ops, SparseCore 0:
  9.9 74.4 all-gather.2
  96.8 27.9 all-gather.4
  402.9 40.6 reduce-scatter.2
  473.1 76.4 reduce-scatter.4

commit v7 on v6

--- a/solution.py
+++ b/solution.py
@@ -852,16 +852,16 @@
     new = {k: send(live["back"][k], k) for k in near}
     if rest:
         ffn_of(rest)
-    fence(returned=new)
-
-    live["returned"] |= {k: send(live["back"][k], k) for k in rest}
-
     def each(name):
         return [whole_piece(live[name][k]) for k in evens]
 
     theirs = down_grad(ffn_info, 3, each("mixed"), each("grads"))
-    gots = up_grad(after(odd_table, theirs), each("tokens"), each("both"))
-    got = send(theirs, 1)
+    fence(returned=new, theirs=theirs)
+
+    live["returned"] |= {k: send(live["back"][k], k) for k in rest}
+
+    gots = up_grad(odd_table, each("tokens"), each("both"))
+    got = send(live.pop("theirs"), 1)
     grad_down = down_grad(after(ffn_info, gots), 2, each("mixed"), each("grads"), got)
     fence(gots=gots, zd=grad_down[: share // 2], ze=grad_down[share // 2 :])
 

time: 755 us -> 755 us (level)
  Pallas kernels: 209 us -> 217 us
    pallas_call x1, Pallas kernels: 23 us -> 30.8 us  [attend(): pl.pallas_call(functools.partial(attend_kernel, heads, HEADS // KVH), out...]
    unnamed x182 -> x180, local copies, waits for them, and re-layouts: 30.3 us -> 31 us
  transfers between devices with their start and end apart: 75 -> 75, of which waited for: 37 -> 37; matrix products, arithmetic and copies ran while one was open for 16% -> 16% of each run, Pallas kernels for 27% -> 29%
where the time goes in v7:
time: 755 us; the launch traced here: 751 us
  waiting for transfers between devices  235 us (31%)
  Pallas kernels  217 us (29%)
  starting transfers between devices  117 us (15%)
  other arithmetic  88.5 us (12%)
  local copies, waits for them, and re-layouts  45.7 us (6%)
  matrix products  32.7 us (4%)
  between operations  15.7 us (2%)
    ppermute x39, waiting for transfers between devices, send(): return lax.ppermute(x, 'fsdp', [(i, i ^ k) for i in range(n)])  112 us
    pallas_call x3, Pallas kernels, ffn(): pl.pallas_call(functools.partial(ffn_kernel, n, count), out_shape=shapes,...  76.7 us
    ppermute x8, waiting for transfers between devices, line_step(): live['o' + out] = lax.ppermute(total, 'seq', outward)  62.3 us
    ppermute x8, starting transfers between devices, line_step(): live['i' + new] = lax.ppermute(x, 'seq', inward)  46.2 us
    convert_element_type x21, other arithmetic, added(): return (one.astype(f32) + two.astype(f32)).astype(bf16)  39.9 us
    ppermute x39, starting transfers between devices, send(): return lax.ppermute(x, 'fsdp', [(i, i ^ k) for i in range(n)])  38.5 us
    unnamed x180, local copies, waits for them, and re-layouts  31 us
    pallas_call x1, Pallas kernels, attend(): pl.pallas_call(functools.partial(attend_kernel, heads, HEADS // KVH), out...  30.8 us
  transfers between devices with their start and end apart: 75, of which 37 were waited for; matrix products, arithmetic and copies ran while one was open for 16% of the time, Pallas kernels for 29%

profile of v7, /device:TPU:0, one launch (start us, length us, event | category | flops | bytes accessed | tf_op | source)
XLA Modules:
  0.0 750.9 jit_solution(3646951851627622111)
XLA Ops:
  35.5 17.5 %collective-permute-done.4 = bf16[128,2816]{1,0:T(8,128)(2,1)} collective-permute-done((bf16[128,2816]{1,0:T(8,128)(2,1)}, bf16[128,2816]{1,0:T(8,128)(2,1)}, u32[]{:S(2)}, u32[]{:S(2)}) %collective-permute-start.4) | collective-permute-done | bytes 720928 | tf_op jit(solution)/shard_map/ppermute | solution.py:26
  65.7 7.2 collective-permute-done.6
  72.9 14.2 %collective-permute-done.7 = bf16[128,2816]{1,0:T(8,128)(2,1)S(1)} collective-permute-done((bf16[128,2816]{1,0:T(8,128)(2,1)}, bf16[128,2816]{1,0:T(8,128)(2,1)S(1)}, u32[]{:S(2)}, u32[]{:S(2)}) %collective-permute-start.7) | collective-permute-done | bytes 720928 | tf_op jit(solution)/shard_map/ppermute | solution.py:51
  112.3 19.7 %collective-permute-done.8 = bf16[128,2816]{1,0:T(8,128)(2,1)} collective-permute-done((bf16[128,2816]{1,0:T(8,128)(2,1)}, bf16[128,2816]{1,0:T(8,128)(2,1)}, u32[]{:S(2)}, u32[]{:S(2)}) %collective-permute-start.8) | collective-permute-done | bytes 720928 | tf_op jit(solution)/shard_map/ppermute | solution.py:26
  139.5 30.8 %shard_map.167 = (bf16[256,2048]{1,0:T(8,128)(2,1)S(1)}, f32[8,4,256]{2,1,0:T(4,128)S(1)}) custom-call(s32[9]{0:T(128)S(1)} %get-tuple-element.1179.info_ref, f32[256,2048]{1,0:T(8,128)S(1)} %fusion.q_ref, bf16[1024,512]{1,0:T(8,128)(2,1)S(1)} %copy-done.23, bf16[1024,512]{1,0:T(8,128)(2,1)S(1)} %copy-done.23, f32[32,256]{1,0:T(8,128)S(1)} %get-tuple-element.1171.cos_ref, ...), custom_call_target="tpu_custom_call" | custom-call | flops 8589934592 | bytes 3145728 | tf_op jit(solution)/shard_map/pallas_call | solution.py:286
  187.6 11.5 %collective-permute-done.16.refs_3_.refs_6_ = bf16[256,2048]{1,0:T(8,128)(2,1)S(1)} collective-permute-done((bf16[256,2048]{1,0:T(8,128)(2,1)S(1)}, bf16[256,2048]{1,0:T(8,128)(2,1)S(1)}, u32[]{:S(2)}, u32[]{:S(2)}) %collective-permute-start.16) | collective-permute-done | bytes 1048608 | tf_op jit(solution)/shard_map/ppermute | solution.py:26
  203.8 21.5 %shard_map.168 = (bf16[1408,256]{1,0:T(8,128)(2,1)}, bf16[256,2816]{1,0:T(8,128)(2,1)}, bf16[256,2048]{1,0:T(8,128)(2,1)}, bf16[256,2048]{1,0:T(8,128)(2,1)}) custom-call(s32[4]{0:T(128)} %pad_add_fusion.4.info_ref, bf16[256,2048]{1,0:T(8,128)(2,1)} %get-tuple-element.812.refs_0_, bf16[256,2048]{1,0:T(8,128)(2,1)} %bitcast.47, ...), custom_call_target="tpu_custom_call" | custom-call | flops 8858370048 | bytes 17301504 | tf_op jit(solution)/shard_map/pallas_call | solution.py:493
  231.9 33.0 %shard_map.169 = (bf16[1408,256]{1,0:T(8,128)(2,1)}, bf16[1408,256]{1,0:T(8,128)(2,1)}, bf16[256,2816]{1,0:T(8,128)(2,1)}, bf16[256,2816]{1,0:T(8,128)(2,1)}, bf...) custom-call(s32[4]{0:T(128)} %pad_add_fusion.4.info_ref, ...), custom_call_target="tpu_custom_call" | custom-call | flops 17716740096 | bytes 17301504 | tf_op jit(solution)/shard_map/pallas_call | solution.py:493
  269.3 22.2 %shard_map.170 = (bf16[1408,256]{1,0:T(8,128)(2,1)}, bf16[256,2816]{1,0:T(8,128)(2,1)}, bf16[256,2048]{1,0:T(8,128)(2,1)}, bf16[256,2048]{1,0:T(8,128)(2,1)}) custom-call(s32[4]{0:T(128)} %pad_add_fusion.4.info_ref, bf16[256,2048]{1,0:T(8,128)(2,1)} %pad_maximum_fusion.3.refs_0_, bf16[256,2048]{1,0:T(8,128)(2,1)} %copy-done.16, ...), custom_call_target="tpu_custom_call" | custom-call | flops 8858370048 | bytes 17301504 | tf_op jit(solution)/shard_map/pallas_call | solution.py:493
  301.1 12.8 %shard_map.172 = bf16[1024,2816]{1,0:T(8,128)(2,1)} custom-call(s32[4]{0:T(128)S(1)} %get-tuple-element.1181.info_ref, bf16[256,2048]{1,0:T(8,128)(2,1)} %get-tuple-element.812.refs_0_, bf16[256,2048]{1,0:T(8,128)(2,1)} %collective-permute-done.19.refs_0_.refs_1_, bf16[256,2048]{1,0:T(8,128)(2,1)S(1)} %copy-done.14, ...), custom_call_target="tpu_custom_call" | custom-call | flops 5905580032 | bytes 11534336 | tf_op jit(solution)/shard_map/pallas_call | solution.py:627
  344.7 15.1 %shard_map.174 = (bf16[256,2816]{1,0:T(8,128)(2,1)S(1)}, bf16[256,2816]{1,0:T(8,128)(2,1)}, bf16[256,2816]{1,0:T(8,128)(2,1)}, bf16[256,2816]{1,0:T(8,128)(2,1)}) custom-call(s32[4]{0:T(128)S(1)} %get-tuple-element.1180.info_ref, bf16[256,2048]{1,0:T(8,128)(2,1)} %get-tuple-element.812.refs_0_, bf16[256,2048]{1,0:T(8,128)(2,1)} %collective-permute-done.19.refs_0_.refs_1_, ...), custom_call_target="tpu_custom_call" | custom-call | flops 5905580032 | bytes 11534336 | tf_op jit(solution)/shard_map/pallas_call | solution.py:627
  361.5 8.2 %collective-permute-start.31 = (bf16[352,2048]{1,0:T(8,128)(2,1)S(1)}, bf16[352,2048]{1,0:T(8,128)(2,1)S(1)}, u32[]{:S(2)}, u32[]{:S(2)}) collective-permute-start(bf16[352,2048]{1,0:T(8,128)(2,1)S(1)} %get-tuple-element.890), channel_id=1, source_target_pairs={{0,1},{3,2},{4,5},{7,6},{8,9},{11,10},{12,13},{15,14},{16,17},{19,... | collective-permute-start | bytes 4325384 | tf_op jit(solution)/shard_map/ppermute | solution.py:95
  371.9 29.7 %shard_map.175 = (bf16[256,2048]{1,0:T(8,128)(2,1)S(1)}, bf16[1024,512]{1,0:T(8,128)(2,1)}) custom-call(s32[9]{0:T(128)S(1)} %get-tuple-element.1179.info_ref, f32[256,2048]{1,0:T(8,128)} %copy-done.25, bf16[1024,512]{1,0:T(8,128)(2,1)S(1)} %copy-done.24, bf16[1024,512]{1,0:T(8,128)(2,1)S(1)} %copy-done.24, bf16[256,2048]{1,0:T(8,128)(2,1)S(1)} %pad_maximum_fusion.6.g_ref, ...), custom_call_target="tpu_custom_call" | custom-call | flops 21474836480 | bytes 4194304 | tf_op jit(solution)/shard_map/pallas_call | solution.py:365
  434.1 16.8 %reduce-scatter.3.cloned.1.call-done = bf16[256,512]{1,0:T(8,128)(2,1)} async-done(((bf16[1024,512]{1,0:T(8,128)(2,1)}), bf16[256,512]{1,0:T(8,128)(2,1)}) %reduce-scatter.3.cloned.1.call-update) | async-done | bytes 262160 | tf_op jit(solution)/shard_map/reduce_scatter | solution.py:949
  472.7 7.4 collective-permute-start.40
  483.9 21.7 %collective-permute-done.41 = bf16[352,2048]{1,0:T(8,128)(2,1)} collective-permute-done((bf16[352,2048]{1,0:T(8,128)(2,1)S(1)}, bf16[352,2048]{1,0:T(8,128)(2,1)}, u32[]{:S(2)}, u32[]{:S(2)}) %collective-permute-start.41) | collective-permute-done | bytes 1441824 | tf_op jit(solution)/shard_map/ppermute | solution.py:98
  513.2 7.3 collective-permute-start.45
  536.8 11.8 %collective-permute-done.44 = bf16[128,2560]{1,0:T(8,128)(2,1)S(1)} collective-permute-done((bf16[128,2560]{1,0:T(8,128)(2,1)S(1)}, bf16[128,2560]{1,0:T(8,128)(2,1)S(1)}, u32[]{:S(2)}, u32[]{:S(2)}) %collective-permute-start.44) | collective-permute-done | bytes 655392 | tf_op jit(solution)/shard_map/ppermute | solution.py:26
  583.6 9.4 %collective-permute-done.50 = bf16[256,2560]{1,0:T(8,128)(2,1)} collective-permute-done((bf16[256,2560]{1,0:T(8,128)(2,1)}, bf16[256,2560]{1,0:T(8,128)(2,1)}, u32[]{:S(2)}, u32[]{:S(2)}) %collective-permute-start.50) | collective-permute-done | bytes 1310752 | tf_op jit(solution)/shard_map/ppermute | solution.py:26
  613.2 8.5 %collective-permute-start.55 = (bf16[256,2560]{1,0:T(8,128)(2,1)}, bf16[256,2560]{1,0:T(8,128)(2,1)}, u32[]{:S(2)}, u32[]{:S(2)}) collective-permute-start(bf16[256,2560]{1,0:T(8,128)(2,1)} %add_convert_fusion.14), channel_id=1, source_target_pairs={{0,1},{3,2},{4,5},{7,6},{8,9},{11,10},{12,13},{15,14},{16,17},{19,... | collective-permute-start | bytes 3932168 | tf_op jit(solution)/shard_map/ppermute | solution.py:95
  633.1 12.1 %collective-permute-done.55 = bf16[256,2560]{1,0:T(8,128)(2,1)} collective-permute-done((bf16[256,2560]{1,0:T(8,128)(2,1)}, bf16[256,2560]{1,0:T(8,128)(2,1)}, u32[]{:S(2)}, u32[]{:S(2)}) %collective-permute-start.55) | collective-permute-done | bytes 1310752 | tf_op jit(solution)/shard_map/ppermute | solution.py:95
  667.7 11.7 %collective-permute-done.60 = bf16[256,2048]{1,0:T(8,128)(2,1)} collective-permute-done((bf16[256,2048]{1,0:T(8,128)(2,1)}, bf16[256,2048]{1,0:T(8,128)(2,1)}, u32[]{:S(2)}, u32[]{:S(2)}) %collective-permute-start.60) | collective-permute-done | bytes 1048608 | tf_op jit(solution)/shard_map/ppermute | solution.py:26
  709.0 9.0 %collective-permute-done.66 = bf16[256,2560]{1,0:T(8,128)(2,1)} collective-permute-done((bf16[256,2560]{1,0:T(8,128)(2,1)S(1)}, bf16[256,2560]{1,0:T(8,128)(2,1)}, u32[]{:S(2)}, u32[]{:S(2)}) %collective-permute-start.66) | collective-permute-done | bytes 1310752 | tf_op jit(solution)/shard_map/ppermute | solution.py:98
  729.5 13.0 %collective-permute-done.70 = bf16[256,2048]{1,0:T(8,128)(2,1)S(1)} collective-permute-done((bf16[256,2048]{1,0:T(8,128)(2,1)S(1)}, bf16[256,2048]{1,0:T(8,128)(2,1)S(1)}, u32[]{:S(2)}, u32[]{:S(2)}) %collective-permute-start.70) | collective-permute-done | bytes 1048608 | tf_op jit(solution)/shard_map/ppermute | solution.py:98
  (458 shorter events, 363.2 us)
Async XLA Ops:
  7.2 79.9 %all-gather.3.cloned.1.call-start = ((), (), s32[]{:S(2)}) async-start(), calls=%async_computation.2 | async-start | bytes 11796480 | tf_op jit(solution)/shard_map/all_gather | solution.py:740
  7.9 124.1 %all-gather.5.cloned.1.call-start = ((), (), s32[]{:S(2)}) async-start(), calls=%async_computation.3 | async-start | bytes 1310720 | tf_op jit(solution)/shard_map/all_gather | solution.py:779
  91.0 41.0 %collective-permute-start.10 = (bf16[256,2048]{1,0:T(8,128)(2,1)}, bf16[256,2048]{1,0:T(8,128)(2,1)}, u32[]{:S(2)}, u32[]{:S(2)}) collective-permute-start(bf16[256,2048]{1,0:T(8,128)(2,1)} %param.13), channel_id=1, source_target_pairs={{0,16},{4,20},{8,24},{12,28},{16,0},{20,4},{24,8},{28,12},{1,17},{... | collective-permute-start | bytes 3145736 | tf_op jit(solution)/shard_map/ppermute | solution.py:26
  92.1 40.0 %collective-permute-start.9 = (bf16[256,2048]{1,0:T(8,128)(2,1)}, bf16[256,2048]{1,0:T(8,128)(2,1)}, u32[]{:S(2)}, u32[]{:S(2)}) collective-permute-start(bf16[256,2048]{1,0:T(8,128)(2,1)} %param.13), channel_id=1, source_target_pairs={{0,8},{4,12},{8,0},{12,4},{16,24},{20,28},{24,16},{28,20},{1,9},{5... | collective-permute-start | bytes 3145736 | tf_op jit(solution)/shard_map/ppermute | solution.py:26
  96.7 354.2 %reduce-scatter.3.cloned.1.call-start = ((), (), s32[]{:S(2)}) async-start(), calls=%async_computation.4 | async-start | bytes 1310720 | tf_op jit(solution)/shard_map/reduce_scatter | solution.py:949
  96.7 35.3 %collective-permute-start.8 = (bf16[128,2816]{1,0:T(8,128)(2,1)}, bf16[128,2816]{1,0:T(8,128)(2,1)}, u32[]{:S(2)}, u32[]{:S(2)}) collective-permute-start(bf16[128,2816]{1,0:T(8,128)(2,1)} %shard_map.164), channel_id=1, source_target_pairs={{0,24},{4,28},{8,16},{12,20},{16,8},{20,12},{24,0},{28,4},{1,25},{... | collective-permute-start | bytes 2162696 | tf_op jit(solution)/shard_map/ppermute | solution.py:26
  132.1 38.3 %collective-permute-start.14 = (bf16[768,2816]{1,0:T(8,128)(2,1)}, bf16[768,2816]{1,0:T(8,128)(2,1)}, u32[]{:S(2)}, u32[]{:S(2)}) collective-permute-start(bf16[768,2816]{1,0:T(8,128)(2,1)} %constant_dynamic-update-slice_fusion.refs_2_.refs_4_), channel_id=1, source_target_pairs={{0,4},{4,0},{8,12},{12,8},{16,20},{20,16},{24,28},{28,24},{1,5},{5... | collective-permute-start | bytes 12976136 | tf_op jit(solution)/shard_map/ppermute | solution.py:26
  227.8 37.1 %collective-permute-start.21 = (bf16[128,2048]{1,0:T(8,128)(2,1)S(1)}, bf16[128,2048]{1,0:T(8,128)(2,1)S(1)}, u32[]{:S(2)}, u32[]{:S(2)}) collective-permute-start(bf16[128,2048]{1,0:T(8,128)(2,1)S(1)} %slice.150), channel_id=1, source_target_pairs={{0,8},{4,12},{8,0},{12,4},{16,24},{20,28},{24,16},{28,20},{1,9},{5... | collective-permute-start | bytes 1572872 | tf_op jit(solution)/shard_map/ppermute | solution.py:26
  229.0 36.0 %collective-permute-start.22 = (bf16[128,2048]{1,0:T(8,128)(2,1)S(1)}, bf16[128,2048]{1,0:T(8,128)(2,1)S(1)}, u32[]{:S(2)}, u32[]{:S(2)}) collective-permute-start(bf16[128,2048]{1,0:T(8,128)(2,1)S(1)} %slice.151), channel_id=1, source_target_pairs={{0,16},{4,20},{8,24},{12,28},{16,0},{20,4},{24,8},{28,12},{1,17},{... | collective-permute-start | bytes 1572872 | tf_op jit(solution)/shard_map/ppermute | solution.py:26
  229.9 35.1 %collective-permute-start.23 = (bf16[128,2048]{1,0:T(8,128)(2,1)S(1)}, bf16[128,2048]{1,0:T(8,128)(2,1)S(1)}, u32[]{:S(2)}, u32[]{:S(2)}) collective-permute-start(bf16[128,2048]{1,0:T(8,128)(2,1)S(1)} %slice.152), channel_id=1, source_target_pairs={{0,8},{4,12},{8,0},{12,4},{16,24},{20,28},{24,16},{28,20},{1,9},{5... | collective-permute-start | bytes 1572872 | tf_op jit(solution)/shard_map/ppermute | solution.py:26
  360.6 43.2 %collective-permute-start.34 = (bf16[352,2048]{1,0:T(8,128)(2,1)S(1)}, bf16[352,2048]{1,0:T(8,128)(2,1)S(1)}, u32[]{:S(2)}, u32[]{:S(2)}) collective-permute-start(bf16[352,2048]{1,0:T(8,128)(2,1)S(1)} %add_convert_fusion.11), channel_id=1, source_target_pairs={{1,2},{2,1},{5,6},{6,5},{9,10},{10,9},{13,14},{14,13},{17,18},{18,... | collective-permute-start | bytes 4325384 | tf_op jit(solution)/shard_map/ppermute | solution.py:91
  361.5 42.3 %collective-permute-start.31 = (bf16[352,2048]{1,0:T(8,128)(2,1)S(1)}, bf16[352,2048]{1,0:T(8,128)(2,1)S(1)}, u32[]{:S(2)}, u32[]{:S(2)}) collective-permute-start(bf16[352,2048]{1,0:T(8,128)(2,1)S(1)} %get-tuple-element.890), channel_id=1, source_target_pairs={{0,1},{3,2},{4,5},{7,6},{8,9},{11,10},{12,13},{15,14},{16,17},{19,... | collective-permute-start | bytes 4325384 | tf_op jit(solution)/shard_map/ppermute | solution.py:95
  410.0 192.5 %reduce-scatter.5.cloned.1.call-start = ((), (), s32[]{:S(2)}) async-start(), calls=%async_computation.5 | async-start | bytes 9437184 | tf_op jit(solution)/shard_map/reduce_scatter | solution.py:974
  410.1 55.7 %collective-permute-start.38 = (bf16[352,2048]{1,0:T(8,128)(2,1)}, bf16[352,2048]{1,0:T(8,128)(2,1)}, u32[]{:S(2)}, u32[]{:S(2)}) collective-permute-start(bf16[352,2048]{1,0:T(8,128)(2,1)} %add_convert_fusion.10), channel_id=1, source_target_pairs={{1,2},{2,1},{5,6},{6,5},{9,10},{10,9},{13,14},{14,13},{17,18},{18,... | collective-permute-start | bytes 4325384 | tf_op jit(solution)/shard_map/ppermute | solution.py:91
  411.9 53.8 %collective-permute-start.35 = (bf16[256,2816]{1,0:T(8,128)(2,1)S(1)}, bf16[256,2816]{1,0:T(8,128)(2,1)}, u32[]{:S(2)}, u32[]{:S(2)}) collective-permute-start(bf16[256,2816]{1,0:T(8,128)(2,1)S(1)} %get-tuple-element.934), channel_id=1, source_target_pairs={{0,1},{3,2},{4,5},{7,6},{8,9},{11,10},{12,13},{15,14},{16,17},{19,... | collective-permute-start | bytes 4325384 | tf_op jit(solution)/shard_map/ppermute | solution.py:95
  418.6 47.1 %collective-permute-start.36 = (bf16[352,2048]{1,0:T(8,128)(2,1)}, bf16[352,2048]{1,0:T(8,128)(2,1)}, u32[]{:S(2)}, u32[]{:S(2)}) collective-permute-start(bf16[352,2048]{1,0:T(8,128)(2,1)} %add_convert_fusion.9), channel_id=1, source_target_pairs={{1,0},{2,3},{5,4},{6,7},{9,8},{10,11},{13,12},{14,15},{17,16},{18,... | collective-permute-start | bytes 4325384 | tf_op jit(solution)/shard_map/ppermute | solution.py:98
  420.0 45.7 %collective-permute-start.37 = (bf16[256,2816]{1,0:T(8,128)(2,1)}, bf16[256,2816]{1,0:T(8,128)(2,1)}, u32[]{:S(2)}, u32[]{:S(2)}) collective-permute-start(bf16[256,2816]{1,0:T(8,128)(2,1)} %get-tuple-element.909), channel_id=1, source_target_pairs={{0,24},{4,28},{8,16},{12,20},{16,8},{20,12},{24,0},{28,4},{1,25},{... | collective-permute-start | bytes 4325384 | tf_op jit(solution)/shard_map/ppermute | solution.py:26
  467.7 42.6 %collective-permute-start.39 = (bf16[1024,2560]{1,0:T(8,128)(2,1)}, bf16[1024,2560]{1,0:T(8,128)(2,1)}, u32[]{:S(2)}, u32[]{:S(2)}) collective-permute-start(bf16[1024,2560]{1,0:T(8,128)(2,1)} %convolution_convert_fusion.2), channel_id=1, source_target_pairs={{0,4},{4,0},{8,12},{12,8},{16,20},{20,16},{24,28},{28,24},{1,5},{5... | collective-permute-start | bytes 15728648 | tf_op jit(solution)/shard_map/ppermute | solution.py:26
  469.7 35.9 %collective-permute-start.41 = (bf16[352,2048]{1,0:T(8,128)(2,1)S(1)}, bf16[352,2048]{1,0:T(8,128)(2,1)}, u32[]{:S(2)}, u32[]{:S(2)}) collective-permute-start(bf16[352,2048]{1,0:T(8,128)(2,1)S(1)} %add_convert_fusion.7), channel_id=1, source_target_pairs={{1,0},{2,3},{5,4},{6,7},{9,8},{10,11},{13,12},{14,15},{17,16},{18,... | collective-permute-start | bytes 4325384 | tf_op jit(solution)/shard_map/ppermute | solution.py:98
  472.7 37.5 %collective-permute-start.40 = (bf16[256,2816]{1,0:T(8,128)(2,1)}, bf16[256,2816]{1,0:T(8,128)(2,1)}, u32[]{:S(2)}, u32[]{:S(2)}) collective-permute-start(bf16[256,2816]{1,0:T(8,128)(2,1)} %collective-permute-done.32), channel_id=1, source_target_pairs={{0,1},{3,2},{4,5},{7,6},{8,9},{11,10},{12,13},{15,14},{16,17},{19,... | collective-permute-start | bytes 4325384 | tf_op jit(solution)/shard_map/ppermute | solution.py:95
  512.5 43.8 %collective-permute-start.47 = (bf16[256,2816]{1,0:T(8,128)(2,1)S(1)}, bf16[256,2816]{1,0:T(8,128)(2,1)S(1)}, u32[]{:S(2)}, u32[]{:S(2)}) collective-permute-start(bf16[256,2816]{1,0:T(8,128)(2,1)S(1)} %add_convert_fusion.6), channel_id=1, source_target_pairs={{1,2},{2,1},{5,6},{6,5},{9,10},{10,9},{13,14},{14,13},{17,18},{18,... | collective-permute-start | bytes 4325384 | tf_op jit(solution)/shard_map/ppermute | solution.py:91
  513.2 43.1 %collective-permute-start.45 = (bf16[256,2816]{1,0:T(8,128)(2,1)S(1)}, bf16[256,2816]{1,0:T(8,128)(2,1)S(1)}, u32[]{:S(2)}, u32[]{:S(2)}) collective-permute-start(bf16[256,2816]{1,0:T(8,128)(2,1)S(1)} %copy-done.57), channel_id=1, source_target_pairs={{0,1},{3,2},{4,5},{7,6},{8,9},{11,10},{12,13},{15,14},{16,17},{19,... | collective-permute-start | bytes 4325384 | tf_op jit(solution)/shard_map/ppermute | solution.py:95
  557.8 44.7 %collective-permute-start.52 = (bf16[256,2816]{1,0:T(8,128)(2,1)}, bf16[256,2816]{1,0:T(8,128)(2,1)}, u32[]{:S(2)}, u32[]{:S(2)}) collective-permute-start(bf16[256,2816]{1,0:T(8,128)(2,1)} %add_convert_fusion.4), channel_id=1, source_target_pairs={{1,2},{2,1},{5,6},{6,5},{9,10},{10,9},{13,14},{14,13},{17,18},{18,... | collective-permute-start | bytes 4325384 | tf_op jit(solution)/shard_map/ppermute | solution.py:91
  559.7 42.8 %collective-permute-start.48 = (bf16[256,2816]{1,0:T(8,128)(2,1)}, bf16[256,2816]{1,0:T(8,128)(2,1)}, u32[]{:S(2)}, u32[]{:S(2)}) collective-permute-start(bf16[256,2816]{1,0:T(8,128)(2,1)} %collective-permute-done.37), channel_id=1, source_target_pairs={{0,1},{3,2},{4,5},{7,6},{8,9},{11,10},{12,13},{15,14},{16,17},{19,... | collective-permute-start | bytes 4325384 | tf_op jit(solution)/shard_map/ppermute | solution.py:95
  (135 other events, 2217.3 us)
Sparse Core Ops, SparseCore 0:
  9.9 74.4 all-gather.2
  96.8 27.9 all-gather.4
  410.2 40.6 reduce-scatter.2
  480.3 76.5 reduce-scatter.4
